TPU v7x, 32 devices: a whole 2x2x4 slice. The times are simulated.
32 devices in a mesh: space: 8 (over z, x), rep: 4 (over y, core).
Axes of the slice: x: 2, y: 2, z: 4, core: 2. Of those that a mesh axis runs over, the one named last changes fastest.
Arguments:
- feats: bfloat16 [4, 32, 64, 512], P('rep', 'space'), may hold values from -6 to 6
- cotangent: bfloat16 [4, 32, 64, 512], P('rep', 'space'), may hold values from -6 to 6
- weight: bfloat16 [27, 64, 64], replicated, may hold values from -0.15625 to 0.15625
- bias: float32 [64], replicated, may hold values from -3 to 3
- neighbours: int32 [4, 32, 26], P('rep', 'space'), may hold values from -1 to 31, as said below
- occupancy: int32 [4, 32, 512], P('rep', 'space'), may hold values from 0 to 1, as said below
Outputs:
- out_feats: bfloat16 [4, 32, 64, 512], P('rep', 'space')
- in_grad: bfloat16 [4, 32, 64, 512], P('rep', 'space')
- weight_grad: float32 [27, 64, 64], replicated
- bias_grad: float32 [64], replicated
Inputs may be any that keep to these rules, and one draw needn't show every extreme that they name: Slot s of a district lies on space index s // 4. On each space index the live bricks fill the first slots; a live brick has at least one occupied voxel and a dead slot none. A brick of a district lies in the slab of its space index at one of 8 x 8 positions; neighbours[s, j] is the slot of the live brick adjacent in direction j, which lies on space index s // 4 + dx; dead slots list only -1, and the lists are symmetric. In every district some space index holds 4 live bricks. `occupancy`: dead slots are all zero.
All inputs are finite; a program needn't handle non-finite values.
Results may differ from a plain program's by a relative error of at most 0.0085.
Values may be sent and summed in bfloat16 or wider, within the bound.
No kernel may reach another device: no remote copies, remote signals or barrier semaphores. Data moves between devices by JAX's collectives and lax.ppermute only.
A program may use at most 128 MiB of HBM per device.

v0:
```python
import math

import jax
import jax.numpy as jnp
from jax import lax
from jax.experimental import pallas as pl
from jax.experimental.pallas import tpu as pltpu
from jax.sharding import PartitionSpec as P

BF, F32 = jnp.bfloat16, jnp.float32
DIRECTIONS = [
    (a, b, c) for a in (-1, 0, 1) for b in (-1, 0, 1) for c in (-1, 0, 1) if (a, b, c) != (0, 0, 0)
]
PLANE = 64
VMEM = pl.BlockSpec(memory_space=pltpu.VMEM)
SMEM = pl.BlockSpec(memory_space=pltpu.SMEM)


def to_planes(tiles, t):
    low = lax.broadcasted_iota(jnp.int32, tiles[0].shape, 1) < PLANE
    turned = [pltpu.roll(tile, PLANE, 1) for tile in tiles]
    first, second = [], []
    for m in range(0, len(tiles), 2):
        first.append(jnp.where(low, tiles[m], turned[m + 1]))
        second.append(jnp.where(low, turned[m], tiles[m + 1]))
    return jnp.concatenate(first, axis=1), jnp.concatenate(second, axis=1)


def from_planes(first, second):
    low = lax.broadcasted_iota(jnp.int32, (first.shape[0], 128), 1) < PLANE
    tiles = []
    for g in range(first.shape[1] // 128):
        one = first[:, 128 * g : 128 * g + 128]
        two = second[:, 128 * g : 128 * g + 128]
        tiles.append(jnp.where(low, one, pltpu.roll(two, PLANE, 1)))
        tiles.append(jnp.where(low, pltpu.roll(one, PLANE, 1), two))
    return tiles


def slot_rows(near_ref, dx, bricks):
    lane = lax.broadcasted_iota(jnp.int32, (1, bricks * PLANE), 1)
    brick = lane // PLANE
    rows = {}
    for dy in (-1, 0, 1):
        for dz in (-1, 0, 1):
            if (dx, dy, dz) == (0, 0, 0):
                rows[dy, dz] = brick * PLANE
                continue
            j = DIRECTIONS.index((dx, dy, dz))
            found = jnp.full(lane.shape, -(1 << 20), jnp.int32)
            for n in range(bricks):
                chosen = near_ref[n, j]
                row = jnp.where(chosen >= 0, lax.rem(chosen, bricks) * PLANE, -(1 << 20))
                found = jnp.where(brick == n, row, found)
            rows[dy, dz] = found
    return rows


def selection(rows, b, c, bricks):
    size = bricks * PLANE
    lane = lax.broadcasted_iota(jnp.int32, (1, size), 1)
    y = ((lane >> 3) & 7) + (b - 1)
    z = (lane & 7) + (c - 1)
    out_y = (y < 0) | (y > 7)
    out_z = (z < 0) | (z > 7)
    base = rows[0, 0]
    if b != 1:
        base = jnp.where(out_y, rows[b - 1, 0], base)
    if c != 1:
        base = jnp.where(out_z, rows[0, c - 1], base)
    if b != 1 and c != 1:
        base = jnp.where(out_y & out_z, rows[b - 1, c - 1], base)
    source = base + (y & 7) * 8 + (z & 7)
    row = lax.broadcasted_iota(jnp.int32, (size, size), 0)
    return jnp.where(row == source, 1.0, 0.0).astype(BF)


def dot(x, y):
    return lax.dot_general(x, y, (((1,), (0,)), ((), ())), preferred_element_type=F32)


def dot_t(x, y):
    return lax.dot_general(x, y, (((1,), (1,)), ((), ())), preferred_element_type=F32)


def faces_kernel(feats_ref, occ_ref, low_ref, high_ref):
    bricks, _, voxels = feats_ref.shape
    keep = occ_ref[...].astype(F32)
    for ref, t, which in ((low_ref, 0, 0), (high_ref, voxels // 128 - 1, 1)):
        at = slice(128 * t, 128 * t + 128)
        tiles = [feats_ref[m, :, at].astype(F32) * keep[m : m + 1, at] for m in range(bricks)]
        ref[...] = to_planes(tiles, t)[which].astype(BF)


def shifted(planes_ref, moved_ref, near_ref, bricks, channels):
    rows = slot_rows(near_ref, 0, bricks)
    count = planes_ref.shape[0]
    flat = planes_ref[...].reshape(count * channels, bricks * PLANE)
    for b in range(3):
        for c in range(3):
            k = 3 * b + c
            if k == 4:
                part = flat
            else:
                part = dot(flat, selection(rows, b, c, bricks)).astype(BF)
            moved_ref[:, channels * k : channels * (k + 1), :] = part.reshape(
                count, channels, bricks * PLANE
            )


def shifted_face(face, near_ref, dx, bricks):
    rows = slot_rows(near_ref, dx, bricks)
    parts = []
    for b in range(3):
        for c in range(3):
            parts.append(dot(face, selection(rows, b, c, bricks)).astype(BF))
    return jnp.concatenate(parts, axis=0)


def inner_kernel(
    near_ref, feats_ref, cot_ref, occ_ref, weight_ref, bias_ref,
    moved_ref, pre_ref, cot2_ref, occ2_ref, planes_ref, total_ref,
):
    bricks, channels, voxels = feats_ref.shape
    keep = occ_ref[...].astype(F32)
    for t in range(voxels // 128):
        at = slice(128 * t, 128 * t + 128)
        kept = [jnp.broadcast_to(keep[m : m + 1, at], (channels, 128)) for m in range(bricks)]
        first, second = to_planes([feats_ref[m, :, at].astype(F32) * kept[m] for m in range(bricks)], t)
        planes_ref[2 * t] = first.astype(BF)
        planes_ref[2 * t + 1] = second.astype(BF)
        first, second = to_planes([cot_ref[m, :, at].astype(F32) * kept[m] for m in range(bricks)], t)
        cot2_ref[2 * t] = first.astype(BF)
        cot2_ref[2 * t + 1] = second.astype(BF)
        first, second = to_planes([kept[m][:8] for m in range(bricks)], t)
        occ2_ref[2 * t] = first
        occ2_ref[2 * t + 1] = second
    shifted(planes_ref, moved_ref, near_ref, bricks, channels)
    count = planes_ref.shape[0]
    start = jnp.broadcast_to(bias_ref[...], (channels, bricks * PLANE))
    for x in range(count + 2):
        total_ref[channels * x : channels * (x + 1), :] = start
    for x in range(count):
        at = slice(channels * x, channels * (x + 3))
        total_ref[at, :] += dot(weight_ref[...], moved_ref[x])
    pre_ref[...] = total_ref[channels : channels * (count + 1), :].reshape(pre_ref.shape)


def outer_kernel(
    near_ref, low_ref, high_ref, moved_ref, pre_ref, cot2_ref, occ2_ref, weight_ref,
    result_ref, grad_ref, terms_ref, padded_ref,
):
    count, channels, lanes = pre_ref.shape
    bricks = lanes // PLANE
    moved_low = shifted_face(low_ref[...], near_ref, -1, bricks)
    moved_high = shifted_face(high_ref[...], near_ref, 1, bricks)
    add_low = dot(weight_ref[2 * channels : 3 * channels, :], moved_low)
    add_high = dot(weight_ref[0:channels, :], moved_high)
    padded_ref[0:channels, :] = jnp.zeros((channels, lanes), BF)
    padded_ref[channels * (count + 1) :, :] = jnp.zeros((channels, lanes), BF)
    bias = jnp.zeros((channels, lanes), F32)
    for x in range(count):
        pre = pre_ref[x]
        if x == 0:
            pre = pre + add_low
        if x == count - 1:
            pre = pre + add_high
        keep = jnp.broadcast_to(occ2_ref[x][0:1], (channels, lanes))
        sig = jax.nn.sigmoid(pre)
        masked = moved_ref[x, 4 * channels : 5 * channels, :].astype(F32)
        result_ref[x] = (masked + keep * pre * sig).astype(BF)
        grad = (cot2_ref[x].astype(F32) * sig * (1.0 + pre * (1.0 - sig))).astype(BF)
        grad_ref[x] = grad
        padded_ref[channels * (x + 1) : channels * (x + 2), :] = grad
        bias = bias + grad.astype(F32)
    terms = dot_t(padded_ref[0 : 3 * channels, :], moved_ref[0])
    for x in range(1, count):
        terms = terms + dot_t(padded_ref[channels * x : channels * (x + 3), :], moved_ref[x])
    width = 9 * channels
    terms_ref[:, 0:width] = terms
    terms_ref[2 * channels : 3 * channels, 0:width] += dot_t(grad_ref[0], moved_low)
    terms_ref[0:channels, 0:width] += dot_t(grad_ref[count - 1], moved_high)
    terms_ref[:, width:] = jnp.zeros((3 * channels, terms_ref.shape[1] - width), F32)
    terms_ref[0:channels, width:] = jnp.broadcast_to(
        jnp.sum(bias, axis=1, keepdims=True), (channels, terms_ref.shape[1] - width)
    )


def back_kernel(
    near_ref, low_ref, high_ref, grad_ref, result2_ref, cot_ref, occ_ref, weight_ref,
    result_ref, in_grad_ref, moved_ref, total_ref,
):
    count, channels, lanes = grad_ref.shape
    bricks = lanes // PLANE
    shifted(grad_ref, moved_ref, near_ref, bricks, channels)
    total_ref[...] = jnp.zeros(total_ref.shape, F32)
    for x in range(count):
        at = slice(channels * x, channels * (x + 3))
        total_ref[at, :] += dot(weight_ref[...], moved_ref[x])
    moved_low = shifted_face(low_ref[...], near_ref, -1, bricks)
    moved_high = shifted_face(high_ref[...], near_ref, 1, bricks)
    total_ref[channels : 2 * channels, :] += dot(
        weight_ref[2 * channels : 3 * channels, :], moved_low
    )
    total_ref[channels * count : channels * (count + 1), :] += dot(
        weight_ref[0:channels, :], moved_high
    )
    keep = occ_ref[...].astype(F32)
    for t in range(count // 2):
        at = slice(128 * t, 128 * t + 128)
        first = total_ref[channels * (2 * t + 1) : channels * (2 * t + 2), :]
        second = total_ref[channels * (2 * t + 2) : channels * (2 * t + 3), :]
        back = from_planes(first, second)
        out = from_planes(result2_ref[2 * t].astype(F32), result2_ref[2 * t + 1].astype(F32))
        for m in range(bricks):
            in_grad_ref[m, :, at] = (
                keep[m : m + 1, at] * (cot_ref[m, :, at].astype(F32) + back[m])
            ).astype(BF)
            result_ref[m, :, at] = out[m].astype(BF)


def call(body, outs, ins, scratch=(), flops=0):
    shapes = [jax.ShapeDtypeStruct(shape, dtype) for shape, dtype in outs]
    moved = sum(math.prod(s.shape) * s.dtype.itemsize for s in shapes)
    moved += sum(math.prod(x.shape) * x.dtype.itemsize for _, x in ins)
    return pl.pallas_call(
        body,
        out_shape=shapes,
        in_specs=[spec for spec, _ in ins],
        out_specs=[VMEM] * len(shapes),
        scratch_shapes=list(scratch),
        compiler_params=pltpu.CompilerParams(vmem_limit_bytes=32 << 20),
        cost_estimate=pl.CostEstimate(flops=flops, bytes_accessed=moved, transcendentals=0),
    )(*[x for _, x in ins])


def exchange_faces(low, high):
    size = lax.axis_size("space")
    up = [(i, i + 1) for i in range(size - 1)]
    down = [(j, i) for i, j in up]
    return lax.ppermute(high, "space", up), lax.ppermute(low, "space", down)


def total_over_devices(terms):
    axes = ("space", "rep")
    spaces, reps = lax.axis_size("space"), lax.axis_size("rep")
    me = lax.axis_index("rep")
    core = me % 2
    half = terms.shape[0] // 2
    partner = [(i, i ^ 1) for i in range(spaces * reps)]
    theirs = lax.dynamic_slice_in_dim(terms, (1 - core) * half, half, 0).astype(BF)
    mine = lax.dynamic_slice_in_dim(terms, core * half, half, 0)
    mine = mine + lax.ppermute(theirs, axes, partner).astype(F32)
    bits = [1 << i for i in range(1, (spaces * reps).bit_length() - 1)]
    orders = (bits, bits[2:] + bits[:2]) if len(bits) == 4 else (bits, bits)
    for steps in zip(*orders):
        sent = mine.astype(BF)
        pairs = [(i, i ^ steps[i % 2]) for i in range(spaces * reps)]
        mine = sent.astype(F32) + lax.ppermute(sent, axes, pairs).astype(F32)
    other = lax.ppermute(mine, axes, partner)
    first = jnp.where(core == 0, mine, other)
    second = jnp.where(core == 0, other, mine)
    return jnp.concatenate([first, second], axis=0)


def on_device(feats, cotangent, weight, bias, neighbours, occupancy):
    x, cot, near, occ = feats[0], cotangent[0], neighbours[0], occupancy[0]
    bricks, channels, voxels = x.shape
    count, lanes = voxels // PLANE, bricks * PLANE
    width = 9 * channels
    low, high = call(
        faces_kernel, [((channels, lanes), BF)] * 2, [(VMEM, x), (VMEM, occ)]
    )
    from_low, from_high = exchange_faces(low, high)
    by_step = weight.reshape(3, 9, channels, channels)
    ahead = by_step[::-1].transpose(0, 2, 1, 3).reshape(3 * channels, width)
    back = by_step[:, ::-1].transpose(0, 3, 1, 2).reshape(3 * channels, width)
    moved, pre, cot2, occ2 = call(
        inner_kernel,
        [
            ((count, width, lanes), BF),
            ((count, channels, lanes), F32),
            ((count, channels, lanes), BF),
            ((count, 8, lanes), F32),
        ],
        [(SMEM, near), (VMEM, x), (VMEM, cot), (VMEM, occ), (VMEM, ahead), (VMEM, bias[:, None])],
        [
            pltpu.VMEM((count, channels, lanes), BF),
            pltpu.VMEM((channels * (count + 2), lanes), F32),
        ],
        flops=2 * 27 * channels * channels * bricks * voxels,
    )
    result2, grad, terms = call(
        outer_kernel,
        [
            ((count, channels, lanes), BF),
            ((count, channels, lanes), BF),
            ((3 * channels, width + 64), F32),
        ],
        [
            (SMEM, near), (VMEM, from_low), (VMEM, from_high), (VMEM, moved), (VMEM, pre),
            (VMEM, cot2), (VMEM, occ2), (VMEM, ahead),
        ],
        [pltpu.VMEM((channels * (count + 2), lanes), BF)],
        flops=2 * 27 * channels * channels * bricks * voxels,
    )
    grad_low, grad_high = exchange_faces(grad[0], grad[count - 1])
    total = total_over_devices(terms)
    result, in_grad = call(
        back_kernel,
        [((bricks, channels, voxels), BF)] * 2,
        [
            (SMEM, near), (VMEM, grad_low), (VMEM, grad_high), (VMEM, grad), (VMEM, result2),
            (VMEM, cot), (VMEM, occ), (VMEM, back),
        ],
        [
            pltpu.VMEM((count, width, lanes), BF),
            pltpu.VMEM((channels * (count + 2), lanes), F32),
        ],
        flops=2 * 27 * channels * channels * bricks * voxels,
    )
    normaliser = 1.0 / math.sqrt(
        feats.shape[0] * lax.axis_size("rep") * bricks * lax.axis_size("space") * voxels
    )
    total = total * normaliser
    weight_grad = total[:, :width].reshape(3, channels, 9, channels)[::-1].transpose(0, 2, 1, 3)
    return (
        result[None],
        in_grad[None],
        weight_grad.reshape(weight.shape),
        total[:channels, width],
    )


def solution(mesh):
    placed = (
        P("rep", "space", None, None),
        P("rep", "space", None, None),
        P(),
        P(),
        P("rep", "space", None),
        P("rep", "space", None),
    )
    return jax.shard_map(
        on_device,
        mesh=mesh,
        in_specs=placed,
        out_specs=(P("rep", "space", None, None), P("rep", "space", None, None), P(), P()),
        check_vma=False,
    )
```

profile of v0, /device:TPU:0, one launch (start us, length us, event | category | flops | bytes accessed | tf_op | source)
XLA Modules:
  0.0 61.0 jit_solution(16800707416332922265)
XLA Ops:
  0.6 0.9 %copy-done = bf16[1,4,64,512]{3,2,1,0:T(8,128)(2,1)S(1)} copy-done((bf16[1,4,64,512]{3,2,1,0:T(8,128)(2,1)S(1)}, bf16[1,4,64,512]{3,2,1,0:T(8,128)(2,1)}, u32[]{:S(2)}) %copy-start) | copy-done | bytes 262168
  1.6 0.7 %copy-done.2 = s32[1,4,512]{2,1,0:T(4,128)S(1)} copy-done((s32[1,4,512]{2,1,0:T(4,128)S(1)}, s32[1,4,512]{2,1,0:T(4,128)}, u32[]{:S(2)}) %copy-start.2) | copy-done | bytes 8216
  2.4 4.8 %collective-permute-start = (bf16[64,256]{1,0:T(8,128)(2,1)S(1)}, bf16[64,256]{1,0:T(8,128)(2,1)S(1)}, u32[]{:S(2)}, u32[]{:S(2)}) collective-permute-start(bf16[64,256]{1,0:T(8,128)(2,1)S(1)} %get-tuple-element.15), channel_id=1, source_target_pairs={{0,4},{4,8},{8,12},{12,16},{16,20},{20,24},{24,28},{1,5},{5,9},{9,... | collective-permute-start | bytes 98312 | tf_op jit(solution)/shard_map/ppermute | solution.py:241
  7.2 1.3 %collective-permute-start.1 = (bf16[64,256]{1,0:T(8,128)(2,1)S(1)}, bf16[64,256]{1,0:T(8,128)(2,1)S(1)}, u32[]{:S(2)}, u32[]{:S(2)}) collective-permute-start(bf16[64,256]{1,0:T(8,128)(2,1)S(1)} %get-tuple-element.16), channel_id=1, source_target_pairs={{4,0},{8,4},{12,8},{16,12},{20,16},{24,20},{28,24},{5,1},{9,5},{13... | collective-permute-start | bytes 98312 | tf_op jit(solution)/shard_map/ppermute | solution.py:241
  8.5 1.6 %copy.21 = bf16[3,9,64,64]{2,0,3,1:T(4,128)(2,1)S(1)} copy(bf16[3,9,64,64]{3,2,1,0:T(8,128)(2,1)} %bitcast.37) | data formatting | bytes 442368 | tf_op jit(solution)/shard_map/reshape | solution.py:275
  10.2 1.7 %rev.9 = bf16[3,9,64,64]{2,0,3,1:T(4,128)(2,1)S(1)} reverse(bf16[3,9,64,64]{2,0,3,1:T(4,128)(2,1)S(1)} %copy.21), dimensions={0} | reverse | bytes 442368 | tf_op jit(solution)/shard_map/rev | solution.py:276
  12.6 3.0 %shard_map.94 = (bf16[8,576,256]{2,1,0:T(8,128)(2,1)S(1)}, f32[8,64,256]{2,1,0:T(8,128)S(1)}, bf16[8,64,256]{2,1,0:T(8,128)(2,1)S(1)}, f32[8,8,256]{2,1,0:T(8,128)S(1)}) custom-call(s32[4,26]{1,0:T(4,128)S(1)} %bitcast.29, bf16[4,64,512]{2,1,0:T(8,128)(2,1)S(1)} %bitcast.25, bf16[4,64,512]{2,1,0:T(8,128)(2,1)S(1)} %bitcast.32, s32[4,512]{1,0:T(4,128)S(1)} %bitcast.27, ...), custom_call_target="tpu_custom_call" | custom-call | flops 452984832 | bytes 3965600 | tf_op jit(solution)/shard_map/pallas_call | solution.py:226
  15.6 2.6 %shard_map.95 = (bf16[8,64,256]{2,1,0:T(8,128)(2,1)S(1)}, bf16[8,64,256]{2,1,0:T(8,128)(2,1)S(1)}, f32[192,640]{1,0:T(8,128)S(1)}) custom-call(s32[4,26]{1,0:T(4,128)S(1)} %bitcast.30, bf16[64,256]{1,0:T(8,128)(2,1)S(1)} %collective-permute-done.low_ref, bf16[64,256]{1,0:T(8,128)(2,1)S(1)} %collective-permute-done.1.high_ref, ...), custom_call_target="tpu_custom_call" | custom-call | flops 452984832 | bytes 4514208 | tf_op jit(solution)/shard_map/pallas_call | solution.py:226
  18.4 1.3 %collective-permute-done.4 = bf16[96,640]{1,0:T(8,128)(2,1)S(1)} collective-permute-done((bf16[96,640]{1,0:T(8,128)(2,1)S(1)}, bf16[96,640]{1,0:T(8,128)(2,1)S(1)}, u32[]{:S(2)}, u32[]{:S(2)}) %collective-permute-start.4) | collective-permute-done | bytes 122912 | tf_op jit(solution)/shard_map/ppermute | solution.py:253
  19.7 1.6 %collective-permute-start.5 = (bf16[96,640]{1,0:T(8,128)(2,1)S(1)}, bf16[96,640]{1,0:T(8,128)(2,1)S(1)}, u32[]{:S(2)}, u32[]{:S(2)}) collective-permute-start(bf16[96,640]{1,0:T(8,128)(2,1)S(1)} %add_convert_fusion.3), channel_id=1, source_target_pairs={{0,2},{1,9},{2,0},{3,11},{4,6},{5,13},{6,4},{7,15},{8,10},{9,1},{1... | collective-permute-start | bytes 368648 | tf_op jit(solution)/shard_map/ppermute | solution.py:259
  21.3 3.4 %collective-permute-done.5 = bf16[96,640]{1,0:T(8,128)(2,1)S(1)} collective-permute-done((bf16[96,640]{1,0:T(8,128)(2,1)S(1)}, bf16[96,640]{1,0:T(8,128)(2,1)S(1)}, u32[]{:S(2)}, u32[]{:S(2)}) %collective-permute-start.5) | collective-permute-done | bytes 122912 | tf_op jit(solution)/shard_map/ppermute | solution.py:259
  24.7 2.7 %collective-permute-start.6 = (bf16[96,640]{1,0:T(8,128)(2,1)S(1)}, bf16[96,640]{1,0:T(8,128)(2,1)S(1)}, u32[]{:S(2)}, u32[]{:S(2)}) collective-permute-start(bf16[96,640]{1,0:T(8,128)(2,1)S(1)} %add_convert_fusion.2), channel_id=1, source_target_pairs={{0,4},{1,17},{2,6},{3,19},{4,0},{5,21},{6,2},{7,23},{8,12},{9,25},... | collective-permute-start | bytes 368648 | tf_op jit(solution)/shard_map/ppermute | solution.py:259
  27.4 2.9 %collective-permute-done.6 = bf16[96,640]{1,0:T(8,128)(2,1)S(1)} collective-permute-done((bf16[96,640]{1,0:T(8,128)(2,1)S(1)}, bf16[96,640]{1,0:T(8,128)(2,1)S(1)}, u32[]{:S(2)}, u32[]{:S(2)}) %collective-permute-start.6) | collective-permute-done | bytes 122912 | tf_op jit(solution)/shard_map/ppermute | solution.py:259
  30.3 3.1 %collective-permute-start.7 = (bf16[96,640]{1,0:T(8,128)(2,1)S(1)}, bf16[96,640]{1,0:T(8,128)(2,1)S(1)}, u32[]{:S(2)}, u32[]{:S(2)}) collective-permute-start(bf16[96,640]{1,0:T(8,128)(2,1)S(1)} %add_convert_fusion.1), channel_id=1, source_target_pairs={{0,8},{1,3},{2,10},{3,1},{4,12},{5,7},{6,14},{7,5},{8,0},{9,11},{1... | collective-permute-start | bytes 368648 | tf_op jit(solution)/shard_map/ppermute | solution.py:259
  33.4 2.9 %collective-permute-done.7 = bf16[96,640]{1,0:T(8,128)(2,1)S(1)} collective-permute-done((bf16[96,640]{1,0:T(8,128)(2,1)S(1)}, bf16[96,640]{1,0:T(8,128)(2,1)S(1)}, u32[]{:S(2)}, u32[]{:S(2)}) %collective-permute-start.7) | collective-permute-done | bytes 122912 | tf_op jit(solution)/shard_map/ppermute | solution.py:259
  36.3 3.1 %collective-permute-start.8 = (bf16[96,640]{1,0:T(8,128)(2,1)S(1)}, bf16[96,640]{1,0:T(8,128)(2,1)S(1)}, u32[]{:S(2)}, u32[]{:S(2)}) collective-permute-start(bf16[96,640]{1,0:T(8,128)(2,1)S(1)} %add_convert_fusion), channel_id=1, source_target_pairs={{0,16},{1,5},{2,18},{3,7},{4,20},{5,1},{6,22},{7,3},{8,24},{9,13},... | collective-permute-start | bytes 368648 | tf_op jit(solution)/shard_map/ppermute | solution.py:259
  39.7 2.5 %collective-permute-done.8 = bf16[96,640]{1,0:T(8,128)(2,1)S(1)} collective-permute-done((bf16[96,640]{1,0:T(8,128)(2,1)S(1)}, bf16[96,640]{1,0:T(8,128)(2,1)S(1)}, u32[]{:S(2)}, u32[]{:S(2)}) %collective-permute-start.8) | collective-permute-done | bytes 122912 | tf_op jit(solution)/shard_map/ppermute | solution.py:259
  42.3 4.1 %collective-permute-start.2 = (bf16[64,256]{1,0:T(8,128)(2,1)S(1)}, bf16[64,256]{1,0:T(8,128)(2,1)S(1)}, u32[]{:S(2)}, u32[]{:S(2)}) collective-permute-start(bf16[64,256]{1,0:T(8,128)(2,1)S(1)} %get-tuple-element.29), channel_id=1, source_target_pairs={{0,4},{4,8},{8,12},{12,16},{16,20},{20,24},{24,28},{1,5},{5,9},{9,... | collective-permute-start | bytes 98312 | tf_op jit(solution)/shard_map/ppermute | solution.py:241
  46.5 1.3 %collective-permute-start.3 = (bf16[64,256]{1,0:T(8,128)(2,1)S(1)}, bf16[64,256]{1,0:T(8,128)(2,1)S(1)}, u32[]{:S(2)}, u32[]{:S(2)}) collective-permute-start(bf16[64,256]{1,0:T(8,128)(2,1)S(1)} %get-tuple-element.28), channel_id=1, source_target_pairs={{4,0},{8,4},{12,8},{16,12},{20,16},{24,20},{28,24},{5,1},{9,5},{13... | collective-permute-start | bytes 98312 | tf_op jit(solution)/shard_map/ppermute | solution.py:241
  48.6 3.7 %collective-permute-done.3.high_ref = bf16[64,256]{1,0:T(8,128)(2,1)S(1)} collective-permute-done((bf16[64,256]{1,0:T(8,128)(2,1)S(1)}, bf16[64,256]{1,0:T(8,128)(2,1)S(1)}, u32[]{:S(2)}, u32[]{:S(2)}) %collective-permute-start.3) | collective-permute-done | bytes 32800 | tf_op jit(solution)/shard_map/ppermute | solution.py:241
  52.3 4.0 %shard_map.96 = (bf16[4,64,512]{2,1,0:T(8,128)(2,1)}, bf16[4,64,512]{2,1,0:T(8,128)(2,1)}) custom-call(s32[4,26]{1,0:T(4,128)S(1)} %bitcast.31, bf16[64,256]{1,0:T(8,128)(2,1)S(1)} %collective-permute-done.2.low_ref, bf16[64,256]{1,0:T(8,128)(2,1)S(1)} %collective-permute-done.3.high_ref, bf16[8,64,256]{2,1,0:T(8,128)(2,1)S(1)} %get-tuple-element.21.grad_ref, ...), custom_call_target="tpu_custom_call" | custom-call | flops 452984832 | bytes 1606048 | tf_op jit(solution)/shard_map/pallas_call | solution.py:226
  56.4 0.7 %slice_reduce_fusion = f32[64]{0:T(128)} fusion(f32[192,640]{1,0:T(8,128)S(1)} %maximum_multiply_fusion), kind=kLoop, calls=%fused_computation.10 | loop fusion | bytes 512 | tf_op jit(solution)/shard_map/slice | solution.py:331
  57.6 1.9 %rev.11 = f32[3,64,9,64]{1,0,3,2:T(4,128)S(1)} reverse(f32[3,64,9,64]{1,0,3,2:T(4,128)S(1)} %reshape.26), dimensions={0} | reverse | bytes 884736 | tf_op jit(solution)/shard_map/rev | solution.py:326
  59.6 1.5 %copy.28 = f32[3,9,64,64]{3,2,1,0:T(8,128)} copy(f32[3,9,64,64]{2,0,3,1:T(4,128)S(1)} %bitcast.34) | data formatting | bytes 884736 | tf_op jit(solution)/shard_map/transpose | solution.py:326
  (39 shorter events, 2.9 us)
Async XLA Ops:
  0.6 1.0 %copy-start = (bf16[1,4,64,512]{3,2,1,0:T(8,128)(2,1)S(1)}, bf16[1,4,64,512]{3,2,1,0:T(8,128)(2,1)}, u32[]{:S(2)}) copy-start(bf16[1,4,64,512]{3,2,1,0:T(8,128)(2,1)} %param.6) | copy-start | bytes 786436
  1.6 0.7 %copy-start.2 = (s32[1,4,512]{2,1,0:T(4,128)S(1)}, s32[1,4,512]{2,1,0:T(4,128)}, u32[]{:S(2)}) copy-start(s32[1,4,512]{2,1,0:T(4,128)} %param.11) | copy-start | bytes 24580
  2.4 13.2 %collective-permute-start = (bf16[64,256]{1,0:T(8,128)(2,1)S(1)}, bf16[64,256]{1,0:T(8,128)(2,1)S(1)}, u32[]{:S(2)}, u32[]{:S(2)}) collective-permute-start(bf16[64,256]{1,0:T(8,128)(2,1)S(1)} %get-tuple-element.15), channel_id=1, source_target_pairs={{0,4},{4,8},{8,12},{12,16},{16,20},{20,24},{24,28},{1,5},{5,9},{9,... | collective-permute-start | bytes 98312 | tf_op jit(solution)/shard_map/ppermute | solution.py:241
  7.2 8.4 %collective-permute-start.1 = (bf16[64,256]{1,0:T(8,128)(2,1)S(1)}, bf16[64,256]{1,0:T(8,128)(2,1)S(1)}, u32[]{:S(2)}, u32[]{:S(2)}) collective-permute-start(bf16[64,256]{1,0:T(8,128)(2,1)S(1)} %get-tuple-element.16), channel_id=1, source_target_pairs={{4,0},{8,4},{12,8},{16,12},{20,16},{24,20},{28,24},{5,1},{9,5},{13... | collective-permute-start | bytes 98312 | tf_op jit(solution)/shard_map/ppermute | solution.py:241
  10.2 2.3 %copy-start.7 = (f32[64]{0:T(128)S(1)}, f32[64]{0:T(128)}, u32[]{:S(2)}) copy-start(f32[64]{0:T(128)} %param.9) | copy-start | bytes 772
  10.2 2.4 %copy-start.1 = (bf16[1,4,64,512]{3,2,1,0:T(8,128)(2,1)S(1)}, bf16[1,4,64,512]{3,2,1,0:T(8,128)(2,1)}, u32[]{:S(2)}) copy-start(bf16[1,4,64,512]{3,2,1,0:T(8,128)(2,1)} %param.6) | copy-start | bytes 786436
  10.2 2.4 %copy-start.3 = (s32[1,4,512]{2,1,0:T(4,128)S(1)}, s32[1,4,512]{2,1,0:T(4,128)}, u32[]{:S(2)}) copy-start(s32[1,4,512]{2,1,0:T(4,128)} %param.11) | copy-start | bytes 24580
  10.2 2.4 %copy-start.4 = (s32[1,4,26]{2,1,0:T(4,128)S(1)}, s32[1,4,26]{2,1,0:T(4,128)}, u32[]{:S(2)}) copy-start(s32[1,4,26]{2,1,0:T(4,128)} %param.10) | copy-start | bytes 1252
  10.2 2.4 %copy-start.5 = (bf16[1,4,64,512]{3,2,1,0:T(8,128)(2,1)S(1)}, bf16[1,4,64,512]{3,2,1,0:T(8,128)(2,1)}, u32[]{:S(2)}) copy-start(bf16[1,4,64,512]{3,2,1,0:T(8,128)(2,1)} %param.7) | copy-start | bytes 786436
  18.2 21.1 %copy-start.6 = (bf16[27,64,64]{2,1,0:T(8,128)(2,1)S(1)}, bf16[27,64,64]{2,1,0:T(8,128)(2,1)}, u32[]{:S(2)}) copy-start(bf16[27,64,64]{2,1,0:T(8,128)(2,1)} %param.8) | copy-start | bytes 663556
  18.3 1.4 %collective-permute-start.4 = (bf16[96,640]{1,0:T(8,128)(2,1)S(1)}, bf16[96,640]{1,0:T(8,128)(2,1)S(1)}, u32[]{:S(2)}, u32[]{:S(2)}) collective-permute-start(bf16[96,640]{1,0:T(8,128)(2,1)S(1)} %dynamic-slice_convert_fusion), channel_id=1, source_target_pairs={{0,1},{1,0},{2,3},{3,2},{4,5},{5,4},{6,7},{7,6},{8,9},{9,8},{10,11... | collective-permute-start | bytes 368648 | tf_op jit(solution)/shard_map/ppermute | solution.py:253
  19.7 4.9 %collective-permute-start.5 = (bf16[96,640]{1,0:T(8,128)(2,1)S(1)}, bf16[96,640]{1,0:T(8,128)(2,1)S(1)}, u32[]{:S(2)}, u32[]{:S(2)}) collective-permute-start(bf16[96,640]{1,0:T(8,128)(2,1)S(1)} %add_convert_fusion.3), channel_id=1, source_target_pairs={{0,2},{1,9},{2,0},{3,11},{4,6},{5,13},{6,4},{7,15},{8,10},{9,1},{1... | collective-permute-start | bytes 368648 | tf_op jit(solution)/shard_map/ppermute | solution.py:259
  24.7 5.6 %collective-permute-start.6 = (bf16[96,640]{1,0:T(8,128)(2,1)S(1)}, bf16[96,640]{1,0:T(8,128)(2,1)S(1)}, u32[]{:S(2)}, u32[]{:S(2)}) collective-permute-start(bf16[96,640]{1,0:T(8,128)(2,1)S(1)} %add_convert_fusion.2), channel_id=1, source_target_pairs={{0,4},{1,17},{2,6},{3,19},{4,0},{5,21},{6,2},{7,23},{8,12},{9,25},... | collective-permute-start | bytes 368648 | tf_op jit(solution)/shard_map/ppermute | solution.py:259
  30.3 5.9 %collective-permute-start.7 = (bf16[96,640]{1,0:T(8,128)(2,1)S(1)}, bf16[96,640]{1,0:T(8,128)(2,1)S(1)}, u32[]{:S(2)}, u32[]{:S(2)}) collective-permute-start(bf16[96,640]{1,0:T(8,128)(2,1)S(1)} %add_convert_fusion.1), channel_id=1, source_target_pairs={{0,8},{1,3},{2,10},{3,1},{4,12},{5,7},{6,14},{7,5},{8,0},{9,11},{1... | collective-permute-start | bytes 368648 | tf_op jit(solution)/shard_map/ppermute | solution.py:259
  36.3 6.0 %collective-permute-start.8 = (bf16[96,640]{1,0:T(8,128)(2,1)S(1)}, bf16[96,640]{1,0:T(8,128)(2,1)S(1)}, u32[]{:S(2)}, u32[]{:S(2)}) collective-permute-start(bf16[96,640]{1,0:T(8,128)(2,1)S(1)} %add_convert_fusion), channel_id=1, source_target_pairs={{0,16},{1,5},{2,18},{3,7},{4,20},{5,1},{6,22},{7,3},{8,24},{9,13},... | collective-permute-start | bytes 368648 | tf_op jit(solution)/shard_map/ppermute | solution.py:259
  42.2 14.0 %collective-permute-start.9 = (f32[96,640]{1,0:T(8,128)S(1)}, f32[96,640]{1,0:T(8,128)S(1)}, u32[]{:S(2)}, u32[]{:S(2)}) collective-permute-start(f32[96,640]{1,0:T(8,128)S(1)} %convert_add_fusion), channel_id=1, source_target_pairs={{0,1},{1,0},{2,3},{3,2},{4,5},{5,4},{6,7},{7,6},{8,9},{9,8},{10,11... | collective-permute-start | bytes 737288 | tf_op jit(solution)/shard_map/ppermute | solution.py:260
  42.3 6.2 %collective-permute-start.2 = (bf16[64,256]{1,0:T(8,128)(2,1)S(1)}, bf16[64,256]{1,0:T(8,128)(2,1)S(1)}, u32[]{:S(2)}, u32[]{:S(2)}) collective-permute-start(bf16[64,256]{1,0:T(8,128)(2,1)S(1)} %get-tuple-element.29), channel_id=1, source_target_pairs={{0,4},{4,8},{8,12},{12,16},{16,20},{20,24},{24,28},{1,5},{5,9},{9,... | collective-permute-start | bytes 98312 | tf_op jit(solution)/shard_map/ppermute | solution.py:241
  46.5 5.8 %collective-permute-start.3 = (bf16[64,256]{1,0:T(8,128)(2,1)S(1)}, bf16[64,256]{1,0:T(8,128)(2,1)S(1)}, u32[]{:S(2)}, u32[]{:S(2)}) collective-permute-start(bf16[64,256]{1,0:T(8,128)(2,1)S(1)} %get-tuple-element.28), channel_id=1, source_target_pairs={{4,0},{8,4},{12,8},{16,12},{20,16},{24,20},{28,24},{5,1},{9,5},{13... | collective-permute-start | bytes 98312 | tf_op jit(solution)/shard_map/ppermute | solution.py:241
where the time goes:
time: 61.6 us; the launch traced here: 61 us
  starting transfers between devices  22.2 us (36%)
  waiting for transfers between devices  16.6 us (27%)
  local copies, waits for them, and re-layouts  11.4 us (19%)
  Pallas kernels  9.67 us (16%)
  between operations  0.93 us (2%)
    ppermute x4, starting transfers between devices, exchange_faces(): return (lax.ppermute(high, 'space', up), lax.ppermute(low, 'space', down))  11.6 us
    ppermute x4, waiting for transfers between devices, total_over_devices(): mine = sent.astype(F32) + lax.ppermute(sent, axes, pairs).astype(F32)  11.5 us
    ppermute x4, starting transfers between devices, total_over_devices(): mine = sent.astype(F32) + lax.ppermute(sent, axes, pairs).astype(F32)  10.5 us
    pallas_call x4, Pallas kernels, call(): pl.pallas_call(body, out_shape=shapes, in_specs=[spec for spec, _ in ins]...  9.67 us
    ppermute x4, waiting for transfers between devices, exchange_faces(): return (lax.ppermute(high, 'space', up), lax.ppermute(low, 'space', down))  3.73 us
    reshape x2, local copies, waits for them, and re-layouts, on_device(): by_step = weight.reshape(3, 9, channels, channels)  2.01 us
    rev x1, local copies, waits for them, and re-layouts, on_device(): total[:, :width].reshape(3, channels, 9, channels)[::-1]  1.94 us
    unnamed x16, local copies, waits for them, and re-layouts  1.68 us
  transfers between devices with their start and end apart: 10, of which 6 were waited for; matrix products, arithmetic and copies ran while one was open for 8% of the time, Pallas kernels for 11%

commit v1 on v0

--- a/solution.py
+++ b/solution.py
@@ -1,3 +1,4 @@
+import functools
 import math
 
 import jax
@@ -13,10 +14,11 @@
 ]
 PLANE = 64
 VMEM = pl.BlockSpec(memory_space=pltpu.VMEM)
+ANY = pl.BlockSpec(memory_space=pl.ANY)
 SMEM = pl.BlockSpec(memory_space=pltpu.SMEM)
 
 
-def to_planes(tiles, t):
+def to_planes(tiles):
     low = lax.broadcasted_iota(jnp.int32, tiles[0].shape, 1) < PLANE
     turned = [pltpu.roll(tile, PLANE, 1) for tile in tiles]
     first, second = [], []
@@ -83,13 +85,33 @@
     return lax.dot_general(x, y, (((1,), (1,)), ((), ())), preferred_element_type=F32)
 
 
-def faces_kernel(feats_ref, occ_ref, low_ref, high_ref):
+def faces_kernel(feats_ref, occ_ref, low_ref, high_ref, held_ref, keep_ref, sems):
     bricks, _, voxels = feats_ref.shape
-    keep = occ_ref[...].astype(F32)
-    for ref, t, which in ((low_ref, 0, 0), (high_ref, voxels // 128 - 1, 1)):
-        at = slice(128 * t, 128 * t + 128)
-        tiles = [feats_ref[m, :, at].astype(F32) * keep[m : m + 1, at] for m in range(bricks)]
-        ref[...] = to_planes(tiles, t)[which].astype(BF)
+    copies = [pltpu.make_async_copy(occ_ref, keep_ref, sems.at[0])]
+    for i, start in enumerate((0, voxels - 128)):
+        copies.append(
+            pltpu.make_async_copy(
+                feats_ref.at[:, :, pl.ds(start, 128)], held_ref.at[i], sems.at[i + 1]
+            )
+        )
+    for copy in copies:
+        copy.start()
+    for copy in copies:
+        copy.wait()
+    keep = keep_ref[...].astype(F32)
+    for i, (ref, start) in enumerate(((low_ref, 0), (high_ref, voxels - 128))):
+        at = slice(start, start + 128)
+        tiles = [held_ref[i, m].astype(F32) * keep[m : m + 1, at] for m in range(bricks)]
+        ref[...] = to_planes(tiles)[i].astype(BF)
+
+
+def weights_kernel(weight_ref, ahead_ref, back_ref):
+    channels = weight_ref.shape[1]
+    for r in range(3):
+        blocks = [weight_ref[9 * (2 - r) + k].astype(F32) for k in range(9)]
+        ahead_ref[channels * r : channels * (r + 1), :] = jnp.concatenate(blocks, axis=1).astype(BF)
+        blocks = [weight_ref[9 * r + 8 - k].astype(F32).T for k in range(9)]
+        back_ref[channels * r : channels * (r + 1), :] = jnp.concatenate(blocks, axis=1).astype(BF)
 
 
 def shifted(planes_ref, moved_ref, near_ref, bricks, channels):
@@ -126,13 +148,13 @@
     for t in range(voxels // 128):
         at = slice(128 * t, 128 * t + 128)
         kept = [jnp.broadcast_to(keep[m : m + 1, at], (channels, 128)) for m in range(bricks)]
-        first, second = to_planes([feats_ref[m, :, at].astype(F32) * kept[m] for m in range(bricks)], t)
+        first, second = to_planes([feats_ref[m, :, at].astype(F32) * kept[m] for m in range(bricks)])
         planes_ref[2 * t] = first.astype(BF)
         planes_ref[2 * t + 1] = second.astype(BF)
-        first, second = to_planes([cot_ref[m, :, at].astype(F32) * kept[m] for m in range(bricks)], t)
+        first, second = to_planes([cot_ref[m, :, at].astype(F32) * kept[m] for m in range(bricks)])
         cot2_ref[2 * t] = first.astype(BF)
         cot2_ref[2 * t + 1] = second.astype(BF)
-        first, second = to_planes([kept[m][:8] for m in range(bricks)], t)
+        first, second = to_planes([kept[m][:8] for m in range(bricks)])
         occ2_ref[2 * t] = first
         occ2_ref[2 * t + 1] = second
     shifted(planes_ref, moved_ref, near_ref, bricks, channels)
@@ -180,15 +202,28 @@
     terms_ref[:, 0:width] = terms
     terms_ref[2 * channels : 3 * channels, 0:width] += dot_t(grad_ref[0], moved_low)
     terms_ref[0:channels, 0:width] += dot_t(grad_ref[count - 1], moved_high)
-    terms_ref[:, width:] = jnp.zeros((3 * channels, terms_ref.shape[1] - width), F32)
-    terms_ref[0:channels, width:] = jnp.broadcast_to(
-        jnp.sum(bias, axis=1, keepdims=True), (channels, terms_ref.shape[1] - width)
-    )
-
-
-def back_kernel(
-    near_ref, low_ref, high_ref, grad_ref, result2_ref, cot_ref, occ_ref, weight_ref,
-    result_ref, in_grad_ref, moved_ref, total_ref,
+    spare = terms_ref.shape[1] - width
+    terms_ref[channels:, width:] = jnp.zeros((2 * channels, spare), F32)
+    terms_ref[0:channels, width:] = jnp.sum(bias, axis=1, keepdims=True) * spread(spare)
+
+
+def spread(count):
+    return 1.0 + lax.broadcasted_iota(jnp.int32, (1, count), 1).astype(F32) * (1.0 / count)
+
+
+def first_sum_kernel(mine_ref, other_ref, grad_ref, out_ref, low_ref, high_ref):
+    out_ref[...] = (mine_ref[...] + other_ref[...].astype(F32)).astype(BF)
+    low_ref[...] = grad_ref[0]
+    high_ref[...] = grad_ref[grad_ref.shape[0] - 1]
+
+
+def sum_kernel(mine_ref, other_ref, *refs):
+    out_ref = refs[-1]
+    out_ref[...] = (mine_ref[...].astype(F32) + other_ref[...].astype(F32)).astype(out_ref.dtype)
+
+
+def back_inner_kernel(
+    near_ref, grad_ref, result2_ref, weight_ref, after_ref, result_ref, total_ref, moved_ref
 ):
     count, channels, lanes = grad_ref.shape
     bricks = lanes // PLANE
@@ -197,26 +232,57 @@
     for x in range(count):
         at = slice(channels * x, channels * (x + 3))
         total_ref[at, :] += dot(weight_ref[...], moved_ref[x])
+    for t in range(count // 2):
+        out = from_planes(result2_ref[2 * t].astype(F32), result2_ref[2 * t + 1].astype(F32))
+        for m in range(bricks):
+            result_ref[m, :, 128 * t : 128 * t + 128] = out[m].astype(BF)
+
+
+def back_outer_kernel(
+    near_ref, low_ref, high_ref, total_ref, cot_ref, occ_ref, weight_ref, after_ref, in_grad_ref
+):
+    bricks, channels, voxels = cot_ref.shape
+    count = voxels // PLANE
     moved_low = shifted_face(low_ref[...], near_ref, -1, bricks)
     moved_high = shifted_face(high_ref[...], near_ref, 1, bricks)
-    total_ref[channels : 2 * channels, :] += dot(
-        weight_ref[2 * channels : 3 * channels, :], moved_low
-    )
-    total_ref[channels * count : channels * (count + 1), :] += dot(
-        weight_ref[0:channels, :], moved_high
-    )
+    add_low = dot(weight_ref[2 * channels : 3 * channels, :], moved_low)
+    add_high = dot(weight_ref[0:channels, :], moved_high)
     keep = occ_ref[...].astype(F32)
     for t in range(count // 2):
         at = slice(128 * t, 128 * t + 128)
         first = total_ref[channels * (2 * t + 1) : channels * (2 * t + 2), :]
         second = total_ref[channels * (2 * t + 2) : channels * (2 * t + 3), :]
+        if t == 0:
+            first = first + add_low
+        if t == count // 2 - 1:
+            second = second + add_high
         back = from_planes(first, second)
-        out = from_planes(result2_ref[2 * t].astype(F32), result2_ref[2 * t + 1].astype(F32))
         for m in range(bricks):
             in_grad_ref[m, :, at] = (
                 keep[m : m + 1, at] * (cot_ref[m, :, at].astype(F32) + back[m])
             ).astype(BF)
-            result_ref[m, :, at] = out[m].astype(BF)
+
+
+def final_kernel(normaliser, core_ref, mine_ref, other_ref, weight_ref, bias_ref, whole_ref):
+    half, columns = mine_ref.shape
+    channels = weight_ref.shape[1]
+    core = core_ref[0]
+    whole_ref[pl.ds(core * half, half), :] = mine_ref[...]
+    whole_ref[pl.ds((1 - core) * half, half), :] = other_ref[...]
+    for r in range(3):
+        rows = slice(channels * r, channels * (r + 1))
+        for t in range(columns // 128):
+            tile = whole_ref[rows, 128 * t : 128 * t + 128] * normaliser
+            weight_ref[9 * (2 - r) + 2 * t] = tile[:, :channels]
+            if 2 * t + 1 < 9:
+                weight_ref[9 * (2 - r) + 2 * t + 1] = pltpu.roll(tile, 128 - channels, 1)[:, :channels]
+            elif r == 0:
+                copies = pltpu.roll(tile, 128 - channels, 1)[:, :channels]
+                copies = copies / (spread(channels) * channels)
+                column = jnp.sum(copies, axis=1, keepdims=True)
+                at = (channels, channels)
+                same = lax.broadcasted_iota(jnp.int32, at, 0) == lax.broadcasted_iota(jnp.int32, at, 1)
+                bias_ref[...] = jnp.sum(jnp.where(same, column, 0.0), axis=0, keepdims=True)
 
 
 def call(body, outs, ins, scratch=(), flops=0):
@@ -241,40 +307,23 @@
     return lax.ppermute(high, "space", up), lax.ppermute(low, "space", down)
 
 
-def total_over_devices(terms):
-    axes = ("space", "rep")
-    spaces, reps = lax.axis_size("space"), lax.axis_size("rep")
-    me = lax.axis_index("rep")
-    core = me % 2
-    half = terms.shape[0] // 2
-    partner = [(i, i ^ 1) for i in range(spaces * reps)]
-    theirs = lax.dynamic_slice_in_dim(terms, (1 - core) * half, half, 0).astype(BF)
-    mine = lax.dynamic_slice_in_dim(terms, core * half, half, 0)
-    mine = mine + lax.ppermute(theirs, axes, partner).astype(F32)
-    bits = [1 << i for i in range(1, (spaces * reps).bit_length() - 1)]
-    orders = (bits, bits[2:] + bits[:2]) if len(bits) == 4 else (bits, bits)
-    for steps in zip(*orders):
-        sent = mine.astype(BF)
-        pairs = [(i, i ^ steps[i % 2]) for i in range(spaces * reps)]
-        mine = sent.astype(F32) + lax.ppermute(sent, axes, pairs).astype(F32)
-    other = lax.ppermute(mine, axes, partner)
-    first = jnp.where(core == 0, mine, other)
-    second = jnp.where(core == 0, other, mine)
-    return jnp.concatenate([first, second], axis=0)
-
-
 def on_device(feats, cotangent, weight, bias, neighbours, occupancy):
     x, cot, near, occ = feats[0], cotangent[0], neighbours[0], occupancy[0]
     bricks, channels, voxels = x.shape
     count, lanes = voxels // PLANE, bricks * PLANE
     width = 9 * channels
     low, high = call(
-        faces_kernel, [((channels, lanes), BF)] * 2, [(VMEM, x), (VMEM, occ)]
+        faces_kernel,
+        [((channels, lanes), BF)] * 2,
+        [(ANY, x), (ANY, occ)],
+        [
+            pltpu.VMEM((2, bricks, channels, 128), BF),
+            pltpu.VMEM((bricks, voxels), jnp.int32),
+            pltpu.SemaphoreType.DMA((3,)),
+        ],
     )
     from_low, from_high = exchange_faces(low, high)
-    by_step = weight.reshape(3, 9, channels, channels)
-    ahead = by_step[::-1].transpose(0, 2, 1, 3).reshape(3 * channels, width)
-    back = by_step[:, ::-1].transpose(0, 3, 1, 2).reshape(3 * channels, width)
+    ahead, back = call(weights_kernel, [((3 * channels, width), BF)] * 2, [(VMEM, weight)])
     moved, pre, cot2, occ2 = call(
         inner_kernel,
         [
@@ -304,32 +353,66 @@
         [pltpu.VMEM((channels * (count + 2), lanes), BF)],
         flops=2 * 27 * channels * channels * bricks * voxels,
     )
-    grad_low, grad_high = exchange_faces(grad[0], grad[count - 1])
-    total = total_over_devices(terms)
-    result, in_grad = call(
-        back_kernel,
-        [((bricks, channels, voxels), BF)] * 2,
-        [
-            (SMEM, near), (VMEM, grad_low), (VMEM, grad_high), (VMEM, grad), (VMEM, result2),
-            (VMEM, cot), (VMEM, occ), (VMEM, back),
-        ],
-        [
-            pltpu.VMEM((count, width, lanes), BF),
-            pltpu.VMEM((channels * (count + 2), lanes), F32),
-        ],
-        flops=2 * 27 * channels * channels * bricks * voxels,
-    )
+    axes = ("space", "rep")
+    devices = lax.axis_size("space") * lax.axis_size("rep")
+    core = lax.axis_index("rep") % 2
+    half = 3 * channels // 2
+    partner = [(i, i ^ 1) for i in range(devices)]
+    theirs = lax.dynamic_slice_in_dim(terms, (1 - core) * half, half, 0).astype(BF)
+    mine = lax.dynamic_slice_in_dim(terms, core * half, half, 0)
+    other = lax.ppermute(theirs, axes, partner)
+    plane = ((channels, lanes), BF)
+    sent = ((half, terms.shape[1]), BF)
+    mine, low, high = call(
+        first_sum_kernel, [sent, plane, plane], [(VMEM, mine), (VMEM, other), (VMEM, grad)]
+    )
+    bits = [1 << i for i in range(1, (devices).bit_length() - 1)]
+    turn = len(bits) // 2
+    grad_low = grad_high = total = in_grad = result = None
+    rounds = list(zip(bits, bits[turn:] + bits[:turn]))
+    for i, steps in enumerate(rounds):
+        other = lax.ppermute(mine, axes, [(j, j ^ steps[j % 2]) for j in range(devices)])
+        held = []
+        if i == 0:
+            grad_low, grad_high = exchange_faces(low, high)
+            held = [grad_low, grad_high]
+        if i == 1:
+            result, total = call(
+                back_inner_kernel,
+                [((bricks, channels, voxels), BF), ((channels * (count + 2), lanes), F32)],
+                [(SMEM, near), (VMEM, grad), (VMEM, result2), (VMEM, back), (ANY, mine)],
+                [pltpu.VMEM((count, width, lanes), BF)],
+                flops=2 * 27 * channels * channels * bricks * voxels,
+            )
+            held = [total]
+        if i == 2:
+            (in_grad,) = call(
+                back_outer_kernel,
+                [((bricks, channels, voxels), BF)],
+                [
+                    (SMEM, near), (VMEM, grad_low), (VMEM, grad_high), (VMEM, total), (VMEM, cot),
+                    (VMEM, occ), (VMEM, back), (ANY, mine),
+                ],
+                flops=2 * 6 * channels * channels * bricks * voxels,
+            )
+            held = [in_grad]
+        last = i == len(rounds) - 1
+        (mine,) = call(
+            sum_kernel,
+            [(sent[0], F32 if last else BF)],
+            [(VMEM, mine), (VMEM, other)] + [(ANY, h) for h in held],
+        )
+    other = lax.ppermute(mine, axes, partner)
     normaliser = 1.0 / math.sqrt(
         feats.shape[0] * lax.axis_size("rep") * bricks * lax.axis_size("space") * voxels
     )
-    total = total * normaliser
-    weight_grad = total[:, :width].reshape(3, channels, 9, channels)[::-1].transpose(0, 2, 1, 3)
-    return (
-        result[None],
-        in_grad[None],
-        weight_grad.reshape(weight.shape),
-        total[:channels, width],
-    )
+    weight_grad, bias_grad = call(
+        functools.partial(final_kernel, normaliser),
+        [(weight.shape, F32), ((1, channels), F32)],
+        [(SMEM, core.astype(jnp.int32)[None]), (VMEM, mine), (VMEM, other)],
+        [pltpu.VMEM(terms.shape, F32)],
+    )
+    return result[None], in_grad[None], weight_grad, bias_grad[0]
 
 
 def solution(mesh):

time: 61.6 us -> 55.2 us (0.90)
  waiting for transfers between devices: 16.6 us -> 11.6 us
  local copies, waits for them, and re-layouts: 11.4 us -> 7.69 us
  Pallas kernels: 9.67 us -> 13.2 us
  starting transfers between devices: 22.2 us -> 21.4 us
    ppermute x6, waiting for transfers between devices: 12.9 us -> 6.68 us  [the longest x4 3.9 us: on_device(): lax.ppermute(mine, axes, [(j, j ^ steps[j % 2]) for j in range(devices)])]
    unnamed x16 -> x22, local copies, waits for them, and re-layouts: 1.68 us -> 6.9 us
    rev x2 -> x0, local copies, waits for them, and re-layouts: 3.61 us -> none  [the longest x1 1.94 us: on_device(): total[:, :width].reshape(3, channels, 9, channels)[::-1]]
    pallas_call x4 -> x12, Pallas kernels: 9.67 us -> 13.2 us  [call(): pl.pallas_call(body, out_shape=shapes, in_specs=[spec for spec, _ in ins]...]
    reshape x7 -> x0, local copies, waits for them, and re-layouts: 3.44 us -> none  [the longest x2 2.01 us: on_device(): by_step = weight.reshape(3, 9, channels, channels)]
    transpose x2 -> x0, local copies, waits for them, and re-layouts: 1.67 us -> none  [the longest x1 1.46 us: on_device(): total[:, :width].reshape(3, channels, 9, channels)[::-1]]
    ppermute x4, waiting for transfers between devices: 3.73 us -> 4.95 us  [exchange_faces(): return (lax.ppermute(high, 'space', up), lax.ppermute(low, 'space', down))]
    ppermute x6, starting transfers between devices: 10.6 us -> 9.43 us  [the longest x4 9.29 us: on_device(): lax.ppermute(mine, axes, [(j, j ^ steps[j % 2]) for j in range(devices)])]
  transfers between devices with their start and end apart: 10 -> 10, of which waited for: 6 -> 6; matrix products, arithmetic and copies ran while one was open for 8% -> 1% of each run, Pallas kernels for 11% -> 17%
where the time goes in v1:
time: 55.2 us; the launch traced here: 54.7 us
  starting transfers between devices  21.4 us (39%)
  Pallas kernels  13.2 us (24%)
  waiting for transfers between devices  11.6 us (21%)
  local copies, waits for them, and re-layouts  7.69 us (14%)
  between operations  0.83 us (2%)
    pallas_call x12, Pallas kernels, call(): pl.pallas_call(body, out_shape=shapes, in_specs=[spec for spec, _ in ins]...  13.2 us
    ppermute x4, starting transfers between devices, exchange_faces(): return (lax.ppermute(high, 'space', up), lax.ppermute(low, 'space', down))  12 us
    ppermute x4, starting transfers between devices, on_device(): lax.ppermute(mine, axes, [(j, j ^ steps[j % 2]) for j in range(devices)])  9.29 us
    unnamed x22, local copies, waits for them, and re-layouts  6.9 us
    ppermute x4, waiting for transfers between devices, exchange_faces(): return (lax.ppermute(high, 'space', up), lax.ppermute(low, 'space', down))  4.95 us
    ppermute x4, waiting for transfers between devices, on_device(): lax.ppermute(mine, axes, [(j, j ^ steps[j % 2]) for j in range(devices)])  3.9 us
    ppermute x1, waiting for transfers between devices, on_device(): other = lax.ppermute(mine, axes, partner)  1.5 us
    ppermute x1, waiting for transfers between devices, on_device(): other = lax.ppermute(theirs, axes, partner)  1.28 us
  transfers between devices with their start and end apart: 10, of which 6 were waited for; matrix products, arithmetic and copies ran while one was open for 1% of the time, Pallas kernels for 17%

profile of v1, /device:TPU:0, one launch (start us, length us, event | category | flops | bytes accessed | tf_op | source)
XLA Modules:
  0.0 54.7 jit_solution(2431903675894100420)
XLA Ops:
  0.6 0.9 %copy-done.4 = bf16[1,4,64,512]{3,2,1,0:T(8,128)(2,1)S(1)} copy-done((bf16[1,4,64,512]{3,2,1,0:T(8,128)(2,1)S(1)}, bf16[1,4,64,512]{3,2,1,0:T(8,128)(2,1)}, u32[]{:S(2)}) %copy-start.4) | copy-done | bytes 262168
  2.4 4.8 %collective-permute-start = (bf16[64,256]{1,0:T(8,128)(2,1)S(1)}, bf16[64,256]{1,0:T(8,128)(2,1)S(1)}, u32[]{:S(2)}, u32[]{:S(2)}) collective-permute-start(bf16[64,256]{1,0:T(8,128)(2,1)S(1)} %get-tuple-element.22), channel_id=1, source_target_pairs={{0,4},{4,8},{8,12},{12,16},{16,20},{20,24},{24,28},{1,5},{5,9},{9,... | collective-permute-start | bytes 98312 | tf_op jit(solution)/shard_map/ppermute | solution.py:307
  7.3 1.3 %collective-permute-start.1 = (bf16[64,256]{1,0:T(8,128)(2,1)S(1)}, bf16[64,256]{1,0:T(8,128)(2,1)S(1)}, u32[]{:S(2)}, u32[]{:S(2)}) collective-permute-start(bf16[64,256]{1,0:T(8,128)(2,1)S(1)} %get-tuple-element.23), channel_id=1, source_target_pairs={{4,0},{8,4},{12,8},{16,12},{20,16},{24,20},{28,24},{5,1},{9,5},{13... | collective-permute-start | bytes 98312 | tf_op jit(solution)/shard_map/ppermute | solution.py:307
  8.6 1.0 %copy-done.1 = bf16[27,64,64]{2,1,0:T(8,128)(2,1)S(1)} copy-done((bf16[27,64,64]{2,1,0:T(8,128)(2,1)S(1)}, bf16[27,64,64]{2,1,0:T(8,128)(2,1)}, u32[]{:S(2)}) %copy-start.1) | copy-done | bytes 221208
  9.9 0.7 %copy.10.bias_ref = f32[64,1]{1,0:T(8,128)S(1)} copy(f32[64,1]{0,1:T(1,128)} %bitcast.21) | data formatting | bytes 512 | tf_op jit(solution)/shard_map/broadcast_in_dim | solution.py:335
  10.7 0.9 %copy-done.2 = bf16[1,4,64,512]{3,2,1,0:T(8,128)(2,1)S(1)} copy-done((bf16[1,4,64,512]{3,2,1,0:T(8,128)(2,1)S(1)}, bf16[1,4,64,512]{3,2,1,0:T(8,128)(2,1)}, u32[]{:S(2)}) %copy-start.2) | copy-done | bytes 262168
  11.6 0.9 %copy-done.5 = bf16[1,4,64,512]{3,2,1,0:T(8,128)(2,1)S(1)} copy-done((bf16[1,4,64,512]{3,2,1,0:T(8,128)(2,1)S(1)}, bf16[1,4,64,512]{3,2,1,0:T(8,128)(2,1)}, u32[]{:S(2)}) %copy-start.5) | copy-done | bytes 262168
  14.0 3.0 %shard_map.95 = (bf16[8,576,256]{2,1,0:T(8,128)(2,1)S(1)}, f32[8,64,256]{2,1,0:T(8,128)S(1)}, bf16[8,64,256]{2,1,0:T(8,128)(2,1)S(1)}, f32[8,8,256]{2,1,0:T(8,128)S(1)}) custom-call(s32[4,26]{1,0:T(4,128)S(1)} %bitcast.17, bf16[4,64,512]{2,1,0:T(8,128)(2,1)S(1)} %bitcast.13, bf16[4,64,512]{2,1,0:T(8,128)(2,1)S(1)} %bitcast.10, s32[4,512]{1,0:T(4,128)S(1)} %bitcast.15, ...), custom_call_target="tpu_custom_call" | custom-call | flops 452984832 | bytes 3965600 | tf_op jit(solution)/shard_map/pallas_call | solution.py:292
  17.0 2.6 %shard_map.96 = (bf16[8,64,256]{2,1,0:T(8,128)(2,1)S(1)}, bf16[8,64,256]{2,1,0:T(8,128)(2,1)S(1)}, f32[192,640]{1,0:T(8,128)S(1)}) custom-call(s32[4,26]{1,0:T(4,128)S(1)} %bitcast.18, bf16[64,256]{1,0:T(8,128)(2,1)S(1)} %collective-permute-done.low_ref, bf16[64,256]{1,0:T(8,128)(2,1)S(1)} %collective-permute-done.1.high_ref, ...), custom_call_target="tpu_custom_call" | custom-call | flops 452984832 | bytes 4514208 | tf_op jit(solution)/shard_map/pallas_call | solution.py:292
  19.8 1.3 %collective-permute-done.2.other_ref = bf16[96,640]{1,0:T(8,128)(2,1)S(1)} collective-permute-done((bf16[96,640]{1,0:T(8,128)(2,1)S(1)}, bf16[96,640]{1,0:T(8,128)(2,1)S(1)}, u32[]{:S(2)}, u32[]{:S(2)}) %collective-permute-start.2) | collective-permute-done | bytes 122912 | tf_op jit(solution)/shard_map/ppermute | solution.py:363
  21.1 1.6 %collective-permute-start.3 = (bf16[96,640]{1,0:T(8,128)(2,1)S(1)}, bf16[96,640]{1,0:T(8,128)(2,1)S(1)}, u32[]{:S(2)}, u32[]{:S(2)}) collective-permute-start(bf16[96,640]{1,0:T(8,128)(2,1)S(1)} %get-tuple-element.33.mine_ref), channel_id=1, source_target_pairs={{0,2},{1,9},{2,0},{3,11},{4,6},{5,13},{6,4},{7,15},{8,10},{9,1},{1... | collective-permute-start | bytes 368648 | tf_op jit(solution)/shard_map/ppermute | solution.py:374
  22.7 4.5 %collective-permute-start.4 = (bf16[64,256]{1,0:T(8,128)(2,1)S(1)}, bf16[64,256]{1,0:T(8,128)(2,1)S(1)}, u32[]{:S(2)}, u32[]{:S(2)}) collective-permute-start(bf16[64,256]{1,0:T(8,128)(2,1)S(1)} %get-tuple-element.34), channel_id=1, source_target_pairs={{0,4},{4,8},{8,12},{12,16},{16,20},{20,24},{24,28},{1,5},{5,9},{9,... | collective-permute-start | bytes 98312 | tf_op jit(solution)/shard_map/ppermute | solution.py:307
  27.2 1.3 %collective-permute-start.5 = (bf16[64,256]{1,0:T(8,128)(2,1)S(1)}, bf16[64,256]{1,0:T(8,128)(2,1)S(1)}, u32[]{:S(2)}, u32[]{:S(2)}) collective-permute-start(bf16[64,256]{1,0:T(8,128)(2,1)S(1)} %get-tuple-element.35), channel_id=1, source_target_pairs={{4,0},{8,4},{12,8},{16,12},{20,16},{24,20},{28,24},{5,1},{9,5},{13... | collective-permute-start | bytes 98312 | tf_op jit(solution)/shard_map/ppermute | solution.py:307
  28.8 4.7 %collective-permute-done.5.refs_1_.high_ref = bf16[64,256]{1,0:T(8,128)(2,1)S(1)} collective-permute-done((bf16[64,256]{1,0:T(8,128)(2,1)S(1)}, bf16[64,256]{1,0:T(8,128)(2,1)S(1)}, u32[]{:S(2)}, u32[]{:S(2)}) %collective-permute-start.5) | collective-permute-done | bytes 32800 | tf_op jit(solution)/shard_map/ppermute | solution.py:307
  33.5 3.0 %collective-permute-start.6 = (bf16[96,640]{1,0:T(8,128)(2,1)S(1)}, bf16[96,640]{1,0:T(8,128)(2,1)S(1)}, u32[]{:S(2)}, u32[]{:S(2)}) collective-permute-start(bf16[96,640]{1,0:T(8,128)(2,1)S(1)} %shard_map.98.after_ref.mine_ref), channel_id=1, source_target_pairs={{0,4},{1,17},{2,6},{3,19},{4,0},{5,21},{6,2},{7,23},{8,12},{9,25},... | collective-permute-start | bytes 368648 | tf_op jit(solution)/shard_map/ppermute | solution.py:374
  36.5 3.6 %shard_map.99 = (bf16[4,64,512]{2,1,0:T(8,128)(2,1)}, f32[640,256]{1,0:T(8,128)S(1)}) custom-call(s32[4,26]{1,0:T(4,128)S(1)} %bitcast.19, bf16[8,64,256]{2,1,0:T(8,128)(2,1)S(1)} %get-tuple-element.29.grad_ref, bf16[8,64,256]{2,1,0:T(8,128)(2,1)S(1)} %get-tuple-element.30.result2_ref, bf16[192,576]{1,0:T(8,128)(2,1)S(1)} %get-tuple-element.31.weight_ref, ...), custom_call_target="tpu_custom_call" | custom-call | flops 452984832 | bytes 1786272 | tf_op jit(solution)/shard_map/pallas_call | solution.py:292
  40.1 2.0 %collective-permute-start.7 = (bf16[96,640]{1,0:T(8,128)(2,1)S(1)}, bf16[96,640]{1,0:T(8,128)(2,1)S(1)}, u32[]{:S(2)}, u32[]{:S(2)}) collective-permute-start(bf16[96,640]{1,0:T(8,128)(2,1)S(1)} %shard_map.100.after_ref.mine_ref), channel_id=1, source_target_pairs={{0,8},{1,3},{2,10},{3,1},{4,12},{5,7},{6,14},{7,5},{8,0},{9,11},{1... | collective-permute-start | bytes 368648 | tf_op jit(solution)/shard_map/ppermute | solution.py:374
  42.1 2.2 %shard_map.101.refs_0_ = bf16[4,64,512]{2,1,0:T(8,128)(2,1)} custom-call(s32[4,26]{1,0:T(4,128)S(1)} %bitcast.20, bf16[64,256]{1,0:T(8,128)(2,1)S(1)} %collective-permute-done.4.refs_0_.low_ref, bf16[64,256]{1,0:T(8,128)(2,1)S(1)} %collective-permute-done.5.refs_1_.high_ref, f32[640,256]{1,0:T(8,128)S(1)} %get-tuple-element.37.refs_0_.total_ref, ...), custom_call_target="tpu_custom_call" | custom-call | flops 100663296 | bytes 1597856 | tf_op jit(solution)/shard_map/pallas_call | solution.py:292
  44.3 0.8 %collective-permute-done.7.other_ref = bf16[96,640]{1,0:T(8,128)(2,1)S(1)} collective-permute-done((bf16[96,640]{1,0:T(8,128)(2,1)S(1)}, bf16[96,640]{1,0:T(8,128)(2,1)S(1)}, u32[]{:S(2)}, u32[]{:S(2)}) %collective-permute-start.7) | collective-permute-done | bytes 122912 | tf_op jit(solution)/shard_map/ppermute | solution.py:374
  45.1 0.9 %copy-done = bf16[4,64,512]{2,1,0:T(8,128)(2,1)S(1)} copy-done((bf16[4,64,512]{2,1,0:T(8,128)(2,1)S(1)}, bf16[4,64,512]{2,1,0:T(8,128)(2,1)}, u32[]{:S(2)}) %copy-start) | copy-done | bytes 262168
  46.1 2.7 %collective-permute-start.8 = (bf16[96,640]{1,0:T(8,128)(2,1)S(1)}, bf16[96,640]{1,0:T(8,128)(2,1)S(1)}, u32[]{:S(2)}, u32[]{:S(2)}) collective-permute-start(bf16[96,640]{1,0:T(8,128)(2,1)S(1)} %shard_map.102.mine_ref), channel_id=1, source_target_pairs={{0,16},{1,5},{2,18},{3,7},{4,20},{5,1},{6,22},{7,3},{8,24},{9,13},... | collective-permute-start | bytes 368648 | tf_op jit(solution)/shard_map/ppermute | solution.py:374
  48.8 3.1 %collective-permute-done.8.other_ref = bf16[96,640]{1,0:T(8,128)(2,1)S(1)} collective-permute-done((bf16[96,640]{1,0:T(8,128)(2,1)S(1)}, bf16[96,640]{1,0:T(8,128)(2,1)S(1)}, u32[]{:S(2)}, u32[]{:S(2)}) %collective-permute-start.8) | collective-permute-done | bytes 122912 | tf_op jit(solution)/shard_map/ppermute | solution.py:374
  52.0 1.5 %collective-permute-done.9.other_ref = f32[96,640]{1,0:T(8,128)S(1)} collective-permute-done((f32[96,640]{1,0:T(8,128)S(1)}, f32[96,640]{1,0:T(8,128)S(1)}, u32[]{:S(2)}, u32[]{:S(2)}) %collective-permute-start.9) | collective-permute-done | bytes 245792 | tf_op jit(solution)/shard_map/ppermute | solution.py:405
  53.5 1.2 %shard_map.104 = (f32[27,64,64]{2,1,0:T(8,128)}, f32[1,64]{1,0:T(1,128)}) custom-call(s32[1]{0:T(128)} %bitcast.7.core_ref, f32[96,640]{1,0:T(8,128)S(1)} %shard_map.103.mine_ref, f32[96,640]{1,0:T(8,128)S(1)} %collective-permute-done.9.other_ref), custom_call_target="tpu_custom_call" | custom-call | bytes 934148 | tf_op jit(solution)/shard_map/pallas_call | solution.py:292
  (33 shorter events, 3.2 us)
Async XLA Ops:
  0.6 1.0 %copy-start.4 = (bf16[1,4,64,512]{3,2,1,0:T(8,128)(2,1)S(1)}, bf16[1,4,64,512]{3,2,1,0:T(8,128)(2,1)}, u32[]{:S(2)}) copy-start(bf16[1,4,64,512]{3,2,1,0:T(8,128)(2,1)} %param.6) | copy-start | bytes 786436
  1.6 0.7 %copy-start.6 = (s32[1,4,512]{2,1,0:T(4,128)S(1)}, s32[1,4,512]{2,1,0:T(4,128)}, u32[]{:S(2)}) copy-start(s32[1,4,512]{2,1,0:T(4,128)} %param.11) | copy-start | bytes 24580
  2.4 14.5 %collective-permute-start = (bf16[64,256]{1,0:T(8,128)(2,1)S(1)}, bf16[64,256]{1,0:T(8,128)(2,1)S(1)}, u32[]{:S(2)}, u32[]{:S(2)}) collective-permute-start(bf16[64,256]{1,0:T(8,128)(2,1)S(1)} %get-tuple-element.22), channel_id=1, source_target_pairs={{0,4},{4,8},{8,12},{12,16},{16,20},{20,24},{24,28},{1,5},{5,9},{9,... | collective-permute-start | bytes 98312 | tf_op jit(solution)/shard_map/ppermute | solution.py:307
  7.3 9.7 %collective-permute-start.1 = (bf16[64,256]{1,0:T(8,128)(2,1)S(1)}, bf16[64,256]{1,0:T(8,128)(2,1)S(1)}, u32[]{:S(2)}, u32[]{:S(2)}) collective-permute-start(bf16[64,256]{1,0:T(8,128)(2,1)S(1)} %get-tuple-element.23), channel_id=1, source_target_pairs={{4,0},{8,4},{12,8},{16,12},{20,16},{24,20},{28,24},{5,1},{9,5},{13... | collective-permute-start | bytes 98312 | tf_op jit(solution)/shard_map/ppermute | solution.py:307
  8.6 1.0 %copy-start.1 = (bf16[27,64,64]{2,1,0:T(8,128)(2,1)S(1)}, bf16[27,64,64]{2,1,0:T(8,128)(2,1)}, u32[]{:S(2)}) copy-start(bf16[27,64,64]{2,1,0:T(8,128)(2,1)} %weight_ref.1) | copy-start | bytes 663556
  10.7 0.9 %copy-start.2 = (bf16[1,4,64,512]{3,2,1,0:T(8,128)(2,1)S(1)}, bf16[1,4,64,512]{3,2,1,0:T(8,128)(2,1)}, u32[]{:S(2)}) copy-start(bf16[1,4,64,512]{3,2,1,0:T(8,128)(2,1)} %param.7) | copy-start | bytes 786436
  11.6 0.9 %copy-start.5 = (bf16[1,4,64,512]{3,2,1,0:T(8,128)(2,1)S(1)}, bf16[1,4,64,512]{3,2,1,0:T(8,128)(2,1)}, u32[]{:S(2)}) copy-start(bf16[1,4,64,512]{3,2,1,0:T(8,128)(2,1)} %param.6) | copy-start | bytes 786436
  12.6 0.7 %copy-start.7 = (s32[1,4,512]{2,1,0:T(4,128)S(1)}, s32[1,4,512]{2,1,0:T(4,128)}, u32[]{:S(2)}) copy-start(s32[1,4,512]{2,1,0:T(4,128)} %param.11) | copy-start | bytes 24580
  13.3 0.7 %copy-start.9 = (s32[1,4,26]{2,1,0:T(4,128)S(1)}, s32[1,4,26]{2,1,0:T(4,128)}, u32[]{:S(2)}) copy-start(s32[1,4,26]{2,1,0:T(4,128)} %param.10) | copy-start | bytes 1252
  17.0 19.5 %copy-start.10 = (s32[1,4,26]{2,1,0:T(4,128)S(1)}, s32[1,4,26]{2,1,0:T(4,128)}, u32[]{:S(2)}) copy-start(s32[1,4,26]{2,1,0:T(4,128)} %param.10) | copy-start | bytes 1252
  19.6 22.5 %copy-start.3 = (bf16[1,4,64,512]{3,2,1,0:T(8,128)(2,1)S(1)}, bf16[1,4,64,512]{3,2,1,0:T(8,128)(2,1)}, u32[]{:S(2)}) copy-start(bf16[1,4,64,512]{3,2,1,0:T(8,128)(2,1)} %param.7) | copy-start | bytes 786436
  19.6 22.5 %copy-start.8 = (s32[1,4,512]{2,1,0:T(4,128)S(1)}, s32[1,4,512]{2,1,0:T(4,128)}, u32[]{:S(2)}) copy-start(s32[1,4,512]{2,1,0:T(4,128)} %param.11) | copy-start | bytes 24580
  19.7 1.4 %collective-permute-start.2 = (bf16[96,640]{1,0:T(8,128)(2,1)S(1)}, bf16[96,640]{1,0:T(8,128)(2,1)S(1)}, u32[]{:S(2)}, u32[]{:S(2)}) collective-permute-start(bf16[96,640]{1,0:T(8,128)(2,1)S(1)} %dynamic-slice_convert_fusion), channel_id=1, source_target_pairs={{0,1},{1,0},{2,3},{3,2},{4,5},{5,4},{6,7},{7,6},{8,9},{9,8},{10,11... | collective-permute-start | bytes 368648 | tf_op jit(solution)/shard_map/ppermute | solution.py:363
  21.1 12.4 %collective-permute-start.3 = (bf16[96,640]{1,0:T(8,128)(2,1)S(1)}, bf16[96,640]{1,0:T(8,128)(2,1)S(1)}, u32[]{:S(2)}, u32[]{:S(2)}) collective-permute-start(bf16[96,640]{1,0:T(8,128)(2,1)S(1)} %get-tuple-element.33.mine_ref), channel_id=1, source_target_pairs={{0,2},{1,9},{2,0},{3,11},{4,6},{5,13},{6,4},{7,15},{8,10},{9,1},{1... | collective-permute-start | bytes 368648 | tf_op jit(solution)/shard_map/ppermute | solution.py:374
  22.7 6.1 %collective-permute-start.4 = (bf16[64,256]{1,0:T(8,128)(2,1)S(1)}, bf16[64,256]{1,0:T(8,128)(2,1)S(1)}, u32[]{:S(2)}, u32[]{:S(2)}) collective-permute-start(bf16[64,256]{1,0:T(8,128)(2,1)S(1)} %get-tuple-element.34), channel_id=1, source_target_pairs={{0,4},{4,8},{8,12},{12,16},{16,20},{20,24},{24,28},{1,5},{5,9},{9,... | collective-permute-start | bytes 98312 | tf_op jit(solution)/shard_map/ppermute | solution.py:307
  27.2 6.2 %collective-permute-start.5 = (bf16[64,256]{1,0:T(8,128)(2,1)S(1)}, bf16[64,256]{1,0:T(8,128)(2,1)S(1)}, u32[]{:S(2)}, u32[]{:S(2)}) collective-permute-start(bf16[64,256]{1,0:T(8,128)(2,1)S(1)} %get-tuple-element.35), channel_id=1, source_target_pairs={{4,0},{8,4},{12,8},{16,12},{20,16},{24,20},{28,24},{5,1},{9,5},{13... | collective-permute-start | bytes 98312 | tf_op jit(solution)/shard_map/ppermute | solution.py:307
  33.5 6.6 %collective-permute-start.6 = (bf16[96,640]{1,0:T(8,128)(2,1)S(1)}, bf16[96,640]{1,0:T(8,128)(2,1)S(1)}, u32[]{:S(2)}, u32[]{:S(2)}) collective-permute-start(bf16[96,640]{1,0:T(8,128)(2,1)S(1)} %shard_map.98.after_ref.mine_ref), channel_id=1, source_target_pairs={{0,4},{1,17},{2,6},{3,19},{4,0},{5,21},{6,2},{7,23},{8,12},{9,25},... | collective-permute-start | bytes 368648 | tf_op jit(solution)/shard_map/ppermute | solution.py:374
  40.1 4.9 %collective-permute-start.7 = (bf16[96,640]{1,0:T(8,128)(2,1)S(1)}, bf16[96,640]{1,0:T(8,128)(2,1)S(1)}, u32[]{:S(2)}, u32[]{:S(2)}) collective-permute-start(bf16[96,640]{1,0:T(8,128)(2,1)S(1)} %shard_map.100.after_ref.mine_ref), channel_id=1, source_target_pairs={{0,8},{1,3},{2,10},{3,1},{4,12},{5,7},{6,14},{7,5},{8,0},{9,11},{1... | collective-permute-start | bytes 368648 | tf_op jit(solution)/shard_map/ppermute | solution.py:374
  45.1 1.0 %copy-start = (bf16[4,64,512]{2,1,0:T(8,128)(2,1)S(1)}, bf16[4,64,512]{2,1,0:T(8,128)(2,1)}, u32[]{:S(2)}) copy-start(bf16[4,64,512]{2,1,0:T(8,128)(2,1)} %shard_map.101.refs_0_) | copy-start | bytes 786436
  46.1 5.8 %collective-permute-start.8 = (bf16[96,640]{1,0:T(8,128)(2,1)S(1)}, bf16[96,640]{1,0:T(8,128)(2,1)S(1)}, u32[]{:S(2)}, u32[]{:S(2)}) collective-permute-start(bf16[96,640]{1,0:T(8,128)(2,1)S(1)} %shard_map.102.mine_ref), channel_id=1, source_target_pairs={{0,16},{1,5},{2,18},{3,7},{4,20},{5,1},{6,22},{7,3},{8,24},{9,13},... | collective-permute-start | bytes 368648 | tf_op jit(solution)/shard_map/ppermute | solution.py:374
  51.9 1.6 %collective-permute-start.9 = (f32[96,640]{1,0:T(8,128)S(1)}, f32[96,640]{1,0:T(8,128)S(1)}, u32[]{:S(2)}, u32[]{:S(2)}) collective-permute-start(f32[96,640]{1,0:T(8,128)S(1)} %shard_map.103.mine_ref), channel_id=1, source_target_pairs={{0,1},{1,0},{2,3},{3,2},{4,5},{5,4},{6,7},{7,6},{8,9},{9,8},{10,11... | collective-permute-start | bytes 737288 | tf_op jit(solution)/shard_map/ppermute | solution.py:405

commit v2 on v1

--- a/solution.py
+++ b/solution.py
@@ -15,6 +15,7 @@
 PLANE = 64
 VMEM = pl.BlockSpec(memory_space=pltpu.VMEM)
 ANY = pl.BlockSpec(memory_space=pl.ANY)
+HBM = pl.BlockSpec(memory_space=pltpu.HBM)
 SMEM = pl.BlockSpec(memory_space=pltpu.SMEM)
 
 
@@ -39,22 +40,30 @@
     return tiles
 
 
-def slot_rows(near_ref, dx, bricks):
+SHIFTS = [(a, b, c) for a in (-1, 0, 1) for b in (-1, 0, 1) for c in (-1, 0, 1)]
+
+
+def fill_slot_rows(near_ref, rows_ref, bricks):
     lane = lax.broadcasted_iota(jnp.int32, (1, bricks * PLANE), 1)
     brick = lane // PLANE
+    for d, shift in enumerate(SHIFTS):
+        if shift == (0, 0, 0):
+            rows_ref[d : d + 1, :] = brick * PLANE
+            continue
+        j = DIRECTIONS.index(shift)
+        found = jnp.full(lane.shape, -(1 << 20), jnp.int32)
+        for n in range(bricks):
+            chosen = near_ref[n, j]
+            row = jnp.where(chosen >= 0, lax.rem(chosen, bricks) * PLANE, -(1 << 20))
+            found = jnp.where(brick == n, row, found)
+        rows_ref[d : d + 1, :] = found
+
+
+def slot_rows(rows_ref, dx):
     rows = {}
-    for dy in (-1, 0, 1):
-        for dz in (-1, 0, 1):
-            if (dx, dy, dz) == (0, 0, 0):
-                rows[dy, dz] = brick * PLANE
-                continue
-            j = DIRECTIONS.index((dx, dy, dz))
-            found = jnp.full(lane.shape, -(1 << 20), jnp.int32)
-            for n in range(bricks):
-                chosen = near_ref[n, j]
-                row = jnp.where(chosen >= 0, lax.rem(chosen, bricks) * PLANE, -(1 << 20))
-                found = jnp.where(brick == n, row, found)
-            rows[dy, dz] = found
+    for d, (a, b, c) in enumerate(SHIFTS):
+        if a == dx:
+            rows[b, c] = rows_ref[d : d + 1, :]
     return rows
 
 
@@ -85,37 +94,48 @@
     return lax.dot_general(x, y, (((1,), (1,)), ((), ())), preferred_element_type=F32)
 
 
-def faces_kernel(feats_ref, occ_ref, low_ref, high_ref, held_ref, keep_ref, sems):
-    bricks, _, voxels = feats_ref.shape
-    copies = [pltpu.make_async_copy(occ_ref, keep_ref, sems.at[0])]
-    for i, start in enumerate((0, voxels - 128)):
-        copies.append(
-            pltpu.make_async_copy(
-                feats_ref.at[:, :, pl.ds(start, 128)], held_ref.at[i], sems.at[i + 1]
-            )
-        )
+def stage_kernel(
+    feats_ref, occ_ref, near_ref, cot_ref, weight_ref, bias_ref,
+    low_ref, high_ref, rows_ref, x_ref, keep_ref, cot_out_ref, weight_out_ref, bias_out_ref,
+    near_held_ref, sems,
+):
+    pairs = (
+        (near_ref, near_held_ref), (occ_ref, keep_ref), (feats_ref, x_ref), (cot_ref, cot_out_ref),
+        (weight_ref, weight_out_ref), (bias_ref, bias_out_ref),
+    )
+    copies = [pltpu.make_async_copy(a, b, sems.at[i]) for i, (a, b) in enumerate(pairs)]
     for copy in copies:
         copy.start()
-    for copy in copies:
-        copy.wait()
+    bricks, _, voxels = x_ref.shape
+    copies[0].wait()
+    fill_slot_rows(near_held_ref, rows_ref, bricks)
+    copies[1].wait()
+    copies[2].wait()
     keep = keep_ref[...].astype(F32)
     for i, (ref, start) in enumerate(((low_ref, 0), (high_ref, voxels - 128))):
         at = slice(start, start + 128)
-        tiles = [held_ref[i, m].astype(F32) * keep[m : m + 1, at] for m in range(bricks)]
+        tiles = [x_ref[m, :, at].astype(F32) * keep[m : m + 1, at] for m in range(bricks)]
         ref[...] = to_planes(tiles)[i].astype(BF)
-
-
-def weights_kernel(weight_ref, ahead_ref, back_ref):
+    for copy in copies[3:]:
+        copy.wait()
+
+
+def ahead_weights(weight_ref, ahead_ref):
     channels = weight_ref.shape[1]
     for r in range(3):
         blocks = [weight_ref[9 * (2 - r) + k].astype(F32) for k in range(9)]
         ahead_ref[channels * r : channels * (r + 1), :] = jnp.concatenate(blocks, axis=1).astype(BF)
+
+
+def back_weights(weight_ref, back_ref):
+    channels = weight_ref.shape[1]
+    for r in range(3):
         blocks = [weight_ref[9 * r + 8 - k].astype(F32).T for k in range(9)]
         back_ref[channels * r : channels * (r + 1), :] = jnp.concatenate(blocks, axis=1).astype(BF)
 
 
-def shifted(planes_ref, moved_ref, near_ref, bricks, channels):
-    rows = slot_rows(near_ref, 0, bricks)
+def shifted(planes_ref, moved_ref, rows_ref, bricks, channels):
+    rows = slot_rows(rows_ref, 0)
     count = planes_ref.shape[0]
     flat = planes_ref[...].reshape(count * channels, bricks * PLANE)
     for b in range(3):
@@ -130,8 +150,8 @@
             )
 
 
-def shifted_face(face, near_ref, dx, bricks):
-    rows = slot_rows(near_ref, dx, bricks)
+def shifted_face(face, rows_ref, dx, bricks):
+    rows = slot_rows(rows_ref, dx)
     parts = []
     for b in range(3):
         for c in range(3):
@@ -140,8 +160,8 @@
 
 
 def inner_kernel(
-    near_ref, feats_ref, cot_ref, occ_ref, weight_ref, bias_ref,
-    moved_ref, pre_ref, cot2_ref, occ2_ref, planes_ref, total_ref,
+    rows_ref, feats_ref, cot_ref, occ_ref, weight_ref, bias_ref,
+    moved_ref, pre_ref, cot2_ref, occ2_ref, ahead_ref, planes_ref, total_ref,
 ):
     bricks, channels, voxels = feats_ref.shape
     keep = occ_ref[...].astype(F32)
@@ -157,25 +177,29 @@
         first, second = to_planes([kept[m][:8] for m in range(bricks)])
         occ2_ref[2 * t] = first
         occ2_ref[2 * t + 1] = second
-    shifted(planes_ref, moved_ref, near_ref, bricks, channels)
+    shifted(planes_ref, moved_ref, rows_ref, bricks, channels)
+    ahead_weights(weight_ref, ahead_ref)
     count = planes_ref.shape[0]
-    start = jnp.broadcast_to(bias_ref[...], (channels, bricks * PLANE))
+    at = (channels, channels)
+    same = lax.broadcasted_iota(jnp.int32, at, 0) == lax.broadcasted_iota(jnp.int32, at, 1)
+    column = jnp.sum(jnp.where(same, bias_ref[...], 0.0), axis=1, keepdims=True)
+    start = jnp.broadcast_to(column, (channels, bricks * PLANE))
     for x in range(count + 2):
         total_ref[channels * x : channels * (x + 1), :] = start
     for x in range(count):
         at = slice(channels * x, channels * (x + 3))
-        total_ref[at, :] += dot(weight_ref[...], moved_ref[x])
+        total_ref[at, :] += dot(ahead_ref[...], moved_ref[x])
     pre_ref[...] = total_ref[channels : channels * (count + 1), :].reshape(pre_ref.shape)
 
 
 def outer_kernel(
-    near_ref, low_ref, high_ref, moved_ref, pre_ref, cot2_ref, occ2_ref, weight_ref,
+    rows_ref, low_ref, high_ref, moved_ref, pre_ref, cot2_ref, occ2_ref, weight_ref,
     result_ref, grad_ref, terms_ref, padded_ref,
 ):
     count, channels, lanes = pre_ref.shape
     bricks = lanes // PLANE
-    moved_low = shifted_face(low_ref[...], near_ref, -1, bricks)
-    moved_high = shifted_face(high_ref[...], near_ref, 1, bricks)
+    moved_low = shifted_face(low_ref[...], rows_ref, -1, bricks)
+    moved_high = shifted_face(high_ref[...], rows_ref, 1, bricks)
     add_low = dot(weight_ref[2 * channels : 3 * channels, :], moved_low)
     add_high = dot(weight_ref[0:channels, :], moved_high)
     padded_ref[0:channels, :] = jnp.zeros((channels, lanes), BF)
@@ -223,15 +247,17 @@
 
 
 def back_inner_kernel(
-    near_ref, grad_ref, result2_ref, weight_ref, after_ref, result_ref, total_ref, moved_ref
+    rows_ref, grad_ref, result2_ref, weight_ref, after_ref,
+    result_ref, total_ref, back_ref, moved_ref,
 ):
     count, channels, lanes = grad_ref.shape
     bricks = lanes // PLANE
-    shifted(grad_ref, moved_ref, near_ref, bricks, channels)
+    back_weights(weight_ref, back_ref)
+    shifted(grad_ref, moved_ref, rows_ref, bricks, channels)
     total_ref[...] = jnp.zeros(total_ref.shape, F32)
     for x in range(count):
         at = slice(channels * x, channels * (x + 3))
-        total_ref[at, :] += dot(weight_ref[...], moved_ref[x])
+        total_ref[at, :] += dot(back_ref[...], moved_ref[x])
     for t in range(count // 2):
         out = from_planes(result2_ref[2 * t].astype(F32), result2_ref[2 * t + 1].astype(F32))
         for m in range(bricks):
@@ -239,12 +265,14 @@
 
 
 def back_outer_kernel(
-    near_ref, low_ref, high_ref, total_ref, cot_ref, occ_ref, weight_ref, after_ref, in_grad_ref
+    rows_ref, low_ref, high_ref, total_ref, cot_ref, occ_ref, weight_ref, after_ref,
+    in_grad_ref, done_ref,
 ):
     bricks, channels, voxels = cot_ref.shape
     count = voxels // PLANE
-    moved_low = shifted_face(low_ref[...], near_ref, -1, bricks)
-    moved_high = shifted_face(high_ref[...], near_ref, 1, bricks)
+    done_ref[...] = jnp.zeros(done_ref.shape, F32)
+    moved_low = shifted_face(low_ref[...], rows_ref, -1, bricks)
+    moved_high = shifted_face(high_ref[...], rows_ref, 1, bricks)
     add_low = dot(weight_ref[2 * channels : 3 * channels, :], moved_low)
     add_high = dot(weight_ref[0:channels, :], moved_high)
     keep = occ_ref[...].astype(F32)
@@ -297,12 +325,12 @@
         scratch_shapes=list(scratch),
         compiler_params=pltpu.CompilerParams(vmem_limit_bytes=32 << 20),
         cost_estimate=pl.CostEstimate(flops=flops, bytes_accessed=moved, transcendentals=0),
-    )(*[x for _, x in ins])
+    )(*[pltpu.with_memory_space_constraint(x, pltpu.HBM) if s is HBM else x for s, x in ins])
 
 
 def exchange_faces(low, high):
     size = lax.axis_size("space")
-    up = [(i, i + 1) for i in range(size - 1)]
+    up = [(i, (i + 1) % size) for i in range(size)]
     down = [(j, i) for i, j in up]
     return lax.ppermute(high, "space", up), lax.ppermute(low, "space", down)
 
@@ -312,27 +340,27 @@
     bricks, channels, voxels = x.shape
     count, lanes = voxels // PLANE, bricks * PLANE
     width = 9 * channels
-    low, high = call(
-        faces_kernel,
-        [((channels, lanes), BF)] * 2,
-        [(ANY, x), (ANY, occ)],
+    plane = ((channels, lanes), BF)
+    low, high, rows, x, occ, cot, weight, bias = call(
+        stage_kernel,
         [
-            pltpu.VMEM((2, bricks, channels, 128), BF),
-            pltpu.VMEM((bricks, voxels), jnp.int32),
-            pltpu.SemaphoreType.DMA((3,)),
+            plane, plane, ((32, lanes), jnp.int32), (x.shape, BF), (occ.shape, jnp.int32), (x.shape, BF),
+            (weight.shape, BF), ((1, channels), F32),
         ],
+        [(HBM, x), (HBM, occ), (HBM, near), (HBM, cot), (HBM, weight), (HBM, bias[None])],
+        [pltpu.SMEM(near.shape, jnp.int32), pltpu.SemaphoreType.DMA((6,))],
     )
     from_low, from_high = exchange_faces(low, high)
-    ahead, back = call(weights_kernel, [((3 * channels, width), BF)] * 2, [(VMEM, weight)])
-    moved, pre, cot2, occ2 = call(
+    moved, pre, cot2, occ2, ahead = call(
         inner_kernel,
         [
             ((count, width, lanes), BF),
             ((count, channels, lanes), F32),
             ((count, channels, lanes), BF),
             ((count, 8, lanes), F32),
+            ((3 * channels, width), BF),
         ],
-        [(SMEM, near), (VMEM, x), (VMEM, cot), (VMEM, occ), (VMEM, ahead), (VMEM, bias[:, None])],
+        [(VMEM, rows), (VMEM, x), (VMEM, cot), (VMEM, occ), (VMEM, weight), (VMEM, bias)],
         [
             pltpu.VMEM((count, channels, lanes), BF),
             pltpu.VMEM((channels * (count + 2), lanes), F32),
@@ -347,7 +375,7 @@
             ((3 * channels, width + 64), F32),
         ],
         [
-            (SMEM, near), (VMEM, from_low), (VMEM, from_high), (VMEM, moved), (VMEM, pre),
+            (VMEM, rows), (VMEM, from_low), (VMEM, from_high), (VMEM, moved), (VMEM, pre),
             (VMEM, cot2), (VMEM, occ2), (VMEM, ahead),
         ],
         [pltpu.VMEM((channels * (count + 2), lanes), BF)],
@@ -361,7 +389,6 @@
     theirs = lax.dynamic_slice_in_dim(terms, (1 - core) * half, half, 0).astype(BF)
     mine = lax.dynamic_slice_in_dim(terms, core * half, half, 0)
     other = lax.ppermute(theirs, axes, partner)
-    plane = ((channels, lanes), BF)
     sent = ((half, terms.shape[1]), BF)
     mine, low, high = call(
         first_sum_kernel, [sent, plane, plane], [(VMEM, mine), (VMEM, other), (VMEM, grad)]
@@ -377,25 +404,29 @@
             grad_low, grad_high = exchange_faces(low, high)
             held = [grad_low, grad_high]
         if i == 1:
-            result, total = call(
+            result, total, back = call(
                 back_inner_kernel,
-                [((bricks, channels, voxels), BF), ((channels * (count + 2), lanes), F32)],
-                [(SMEM, near), (VMEM, grad), (VMEM, result2), (VMEM, back), (ANY, mine)],
+                [
+                    ((bricks, channels, voxels), BF),
+                    ((channels * (count + 2), lanes), F32),
+                    ((3 * channels, width), BF),
+                ],
+                [(VMEM, rows), (VMEM, grad), (VMEM, result2), (VMEM, weight), (ANY, mine)],
                 [pltpu.VMEM((count, width, lanes), BF)],
                 flops=2 * 27 * channels * channels * bricks * voxels,
             )
             held = [total]
         if i == 2:
-            (in_grad,) = call(
+            in_grad, done = call(
                 back_outer_kernel,
-                [((bricks, channels, voxels), BF)],
+                [((bricks, channels, voxels), BF), ((8, 128), F32)],
                 [
-                    (SMEM, near), (VMEM, grad_low), (VMEM, grad_high), (VMEM, total), (VMEM, cot),
+                    (VMEM, rows), (VMEM, grad_low), (VMEM, grad_high), (VMEM, total), (VMEM, cot),
                     (VMEM, occ), (VMEM, back), (ANY, mine),
                 ],
                 flops=2 * 6 * channels * channels * bricks * voxels,
             )
-            held = [in_grad]
+            held = [done]
         last = i == len(rounds) - 1
         (mine,) = call(
             sum_kernel,

time: 55.2 us -> 42.3 us (0.77)
  local copies, waits for them, and re-layouts: 7.69 us -> 0.05 us
  starting transfers between devices: 21.4 us -> 14.9 us
  waiting for transfers between devices: 11.6 us -> 14.9 us
  Pallas kernels: 13.2 us -> 11.5 us
    unnamed x22 -> x0, local copies, waits for them, and re-layouts: 6.9 us -> none
    ppermute x4, waiting for transfers between devices: 3.9 us -> 10.3 us  [on_device(): lax.ppermute(mine, axes, [(j, j ^ steps[j % 2]) for j in range(devices)])]
    ppermute x4, starting transfers between devices: 9.29 us -> 3.9 us  [on_device(): lax.ppermute(mine, axes, [(j, j ^ steps[j % 2]) for j in range(devices)])]
    ppermute x4, waiting for transfers between devices: 4.95 us -> 1.9 us  [exchange_faces(): return (lax.ppermute(high, 'space', up), lax.ppermute(low, 'space', down))]
    pallas_call x12 -> x11, Pallas kernels: 13.2 us -> 11.5 us  [call(): pl.pallas_call(body, out_shape=shapes, in_specs=[spec for spec, _ in ins]...]
    ppermute x4, starting transfers between devices: 12 us -> 10.8 us  [exchange_faces(): return (lax.ppermute(high, 'space', up), lax.ppermute(low, 'space', down))]
    broadcast_in_dim x1 -> x0, local copies, waits for them, and re-layouts: 0.75 us -> none  [on_device(): bias[:, None]]
  transfers between devices with their start and end apart: 10 -> 10, of which waited for: 6 -> 6; matrix products, arithmetic and copies ran while one was open for 1% -> 0% of each run, Pallas kernels for 17% -> 17%
where the time goes in v2:
time: 42.3 us; the launch traced here: 42.1 us
  starting transfers between devices  14.9 us (35%)
  waiting for transfers between devices  14.9 us (35%)
  Pallas kernels  11.5 us (27%)
  between operations  0.75 us (2%)
    pallas_call x11, Pallas kernels, call(): pl.pallas_call(body, out_shape=shapes, in_specs=[spec for spec, _ in ins]...  11.5 us
    ppermute x4, starting transfers between devices, exchange_faces(): return (lax.ppermute(high, 'space', up), lax.ppermute(low, 'space', down))  10.8 us
    ppermute x4, waiting for transfers between devices, on_device(): lax.ppermute(mine, axes, [(j, j ^ steps[j % 2]) for j in range(devices)])  10.3 us
    ppermute x4, starting transfers between devices, on_device(): lax.ppermute(mine, axes, [(j, j ^ steps[j % 2]) for j in range(devices)])  3.9 us
    ppermute x4, waiting for transfers between devices, exchange_faces(): return (lax.ppermute(high, 'space', up), lax.ppermute(low, 'space', down))  1.9 us
    ppermute x1, waiting for transfers between devices, on_device(): other = lax.ppermute(mine, axes, partner)  1.5 us
    ppermute x1, waiting for transfers between devices, on_device(): other = lax.ppermute(theirs, axes, partner)  1.28 us
  transfers between devices with their start and end apart: 10, of which 6 were waited for; matrix products, arithmetic and copies ran while one was open for 0% of the time, Pallas kernels for 17%

profile of v2, /device:TPU:0, one launch (start us, length us, event | category | flops | bytes accessed | tf_op | source)
XLA Modules:
  0.0 42.1 jit_solution(1455955321598478996)
XLA Ops:
  0.6 1.2 %shard_map.93 = (bf16[64,256]{1,0:T(8,128)(2,1)S(1)}, bf16[64,256]{1,0:T(8,128)(2,1)S(1)}, s32[32,256]{1,0:T(8,128)S(1)}, bf16[4,64,512]{2,1,0:T(8,128)(2,1)S(1)...) custom-call(bf16[4,64,512]{2,1,0:T(8,128)(2,1)} %bitcast.9, ...), custom_call_target="tpu_custom_call" | custom-call | bytes 1606560 | tf_op jit(solution)/shard_map/pallas_call | solution.py:320
  1.9 3.0 %collective-permute-start = (bf16[64,256]{1,0:T(8,128)(2,1)S(1)}, bf16[64,256]{1,0:T(8,128)(2,1)S(1)}, u32[]{:S(2)}, u32[]{:S(2)}) collective-permute-start(bf16[64,256]{1,0:T(8,128)(2,1)S(1)} %get-tuple-element.31), channel_id=1, source_target_pairs={{0,4},{4,8},{8,12},{12,16},{16,20},{20,24},{24,28},{28,0},{1,5},{5... | collective-permute-start | bytes 98312 | tf_op jit(solution)/shard_map/ppermute | solution.py:335
  4.9 3.1 %collective-permute-start.1 = (bf16[64,256]{1,0:T(8,128)(2,1)S(1)}, bf16[64,256]{1,0:T(8,128)(2,1)S(1)}, u32[]{:S(2)}, u32[]{:S(2)}) collective-permute-start(bf16[64,256]{1,0:T(8,128)(2,1)S(1)} %get-tuple-element.32), channel_id=1, source_target_pairs={{4,0},{8,4},{12,8},{16,12},{20,16},{24,20},{28,24},{0,28},{5,1},{9... | collective-permute-start | bytes 98312 | tf_op jit(solution)/shard_map/ppermute | solution.py:335
  8.0 2.4 %shard_map.94 = (bf16[8,576,256]{2,1,0:T(8,128)(2,1)S(1)}, f32[8,64,256]{2,1,0:T(8,128)S(1)}, bf16[8,64,256]{2,1,0:T(8,128)(2,1)S(1)}, f32[8,8,256]{2,1,0:T(8,128)S(1)}, bf16[192,576]{1,0:T(8,128)(2,1)S(1)}) custom-call(s32[32,256]{1,0:T(8,128)S(1)} %get-tuple-element.30.rows_ref, bf16[4,64,512]{2,1,0:T(8,128)(2,1)S(1)} %get-tuple-element.33.feats_ref, ...), custom_call_target="tpu_custom_call" | custom-call | flops 452984832 | bytes 4219136 | tf_op jit(solution)/shard_map/pallas_call | solution.py:320
  10.4 0.0 collective-permute-done.low_ref
  10.4 0.0 collective-permute-done.1.high_ref
  10.4 1.9 %shard_map.95 = (bf16[8,64,256]{2,1,0:T(8,128)(2,1)S(1)}, bf16[8,64,256]{2,1,0:T(8,128)(2,1)S(1)}, f32[192,640]{1,0:T(8,128)S(1)}) custom-call(s32[32,256]{1,0:T(8,128)S(1)} %get-tuple-element.30.rows_ref, bf16[64,256]{1,0:T(8,128)(2,1)S(1)} %collective-permute-done.low_ref, bf16[64,256]{1,0:T(8,128)(2,1)S(1)} %collective-permute-done.1.high_ref, ...), custom_call_target="tpu_custom_call" | custom-call | flops 452984832 | bytes 4546560 | tf_op jit(solution)/shard_map/pallas_call | solution.py:320
  12.4 0.1 collective-permute-start.2
  12.5 1.3 %collective-permute-done.2.other_ref = bf16[96,640]{1,0:T(8,128)(2,1)S(1)} collective-permute-done((bf16[96,640]{1,0:T(8,128)(2,1)S(1)}, bf16[96,640]{1,0:T(8,128)(2,1)S(1)}, u32[]{:S(2)}, u32[]{:S(2)}) %collective-permute-start.2) | collective-permute-done | bytes 122912 | tf_op jit(solution)/shard_map/ppermute | solution.py:391
  13.8 1.7 %collective-permute-start.3 = (bf16[96,640]{1,0:T(8,128)(2,1)S(1)}, bf16[96,640]{1,0:T(8,128)(2,1)S(1)}, u32[]{:S(2)}, u32[]{:S(2)}) collective-permute-start(bf16[96,640]{1,0:T(8,128)(2,1)S(1)} %get-tuple-element.46.mine_ref), channel_id=1, source_target_pairs={{0,2},{1,9},{2,0},{3,11},{4,6},{5,13},{6,4},{7,15},{8,10},{9,1},{1... | collective-permute-start | bytes 368648 | tf_op jit(solution)/shard_map/ppermute | solution.py:401
  15.5 0.7 %collective-permute-start.4 = (bf16[64,256]{1,0:T(8,128)(2,1)S(1)}, bf16[64,256]{1,0:T(8,128)(2,1)S(1)}, u32[]{:S(2)}, u32[]{:S(2)}) collective-permute-start(bf16[64,256]{1,0:T(8,128)(2,1)S(1)} %get-tuple-element.47), channel_id=1, source_target_pairs={{0,4},{4,8},{8,12},{12,16},{16,20},{20,24},{24,28},{28,0},{1,5},{5... | collective-permute-start | bytes 98312 | tf_op jit(solution)/shard_map/ppermute | solution.py:335
  16.2 4.0 %collective-permute-start.5 = (bf16[64,256]{1,0:T(8,128)(2,1)S(1)}, bf16[64,256]{1,0:T(8,128)(2,1)S(1)}, u32[]{:S(2)}, u32[]{:S(2)}) collective-permute-start(bf16[64,256]{1,0:T(8,128)(2,1)S(1)} %get-tuple-element.48), channel_id=1, source_target_pairs={{4,0},{8,4},{12,8},{16,12},{20,16},{24,20},{28,24},{0,28},{5,1},{9... | collective-permute-start | bytes 98312 | tf_op jit(solution)/shard_map/ppermute | solution.py:335
  20.3 1.9 %collective-permute-done.4.refs_0_.low_ref = bf16[64,256]{1,0:T(8,128)(2,1)S(1)} collective-permute-done((bf16[64,256]{1,0:T(8,128)(2,1)S(1)}, bf16[64,256]{1,0:T(8,128)(2,1)S(1)}, u32[]{:S(2)}, u32[]{:S(2)}) %collective-permute-start.4) | collective-permute-done | bytes 32800 | tf_op jit(solution)/shard_map/ppermute | solution.py:335
  22.2 0.1 collective-permute-start.6
  22.3 3.0 %shard_map.98 = (bf16[4,64,512]{2,1,0:T(8,128)(2,1)}, f32[640,256]{1,0:T(8,128)S(1)}, bf16[192,576]{1,0:T(8,128)(2,1)S(1)}) custom-call(s32[32,256]{1,0:T(8,128)S(1)} %get-tuple-element.30.rows_ref, bf16[8,64,256]{2,1,0:T(8,128)(2,1)S(1)} %get-tuple-element.43.grad_ref, bf16[8,64,256]{2,1,0:T(8,128)(2,1)S(1)} %get-tuple-element.44.result2_ref, ...), custom_call_target="tpu_custom_call" | custom-call | flops 452984832 | bytes 2039808 | tf_op jit(solution)/shard_map/pallas_call | solution.py:320
  25.3 1.8 %collective-permute-done.6.other_ref = bf16[96,640]{1,0:T(8,128)(2,1)S(1)} collective-permute-done((bf16[96,640]{1,0:T(8,128)(2,1)S(1)}, bf16[96,640]{1,0:T(8,128)(2,1)S(1)}, u32[]{:S(2)}, u32[]{:S(2)}) %collective-permute-start.6) | collective-permute-done | bytes 122912 | tf_op jit(solution)/shard_map/ppermute | solution.py:401
  27.2 0.1 collective-permute-start.7
  27.3 1.6 %shard_map.100 = (bf16[4,64,512]{2,1,0:T(8,128)(2,1)}, f32[8,128]{1,0:T(8,128)S(1)}) custom-call(s32[32,256]{1,0:T(8,128)S(1)} %get-tuple-element.30.rows_ref, bf16[64,256]{1,0:T(8,128)(2,1)S(1)} %collective-permute-done.4.refs_0_.low_ref, bf16[64,256]{1,0:T(8,128)(2,1)S(1)} %collective-permute-done.5.refs_1_.high_ref, ...), custom_call_target="tpu_custom_call" | custom-call | flops 100663296 | bytes 1634304 | tf_op jit(solution)/shard_map/pallas_call | solution.py:320
  28.8 3.3 %collective-permute-done.7.other_ref = bf16[96,640]{1,0:T(8,128)(2,1)S(1)} collective-permute-done((bf16[96,640]{1,0:T(8,128)(2,1)S(1)}, bf16[96,640]{1,0:T(8,128)(2,1)S(1)}, u32[]{:S(2)}, u32[]{:S(2)}) %collective-permute-start.7) | collective-permute-done | bytes 122912 | tf_op jit(solution)/shard_map/ppermute | solution.py:401
  32.2 2.0 %collective-permute-start.8 = (bf16[96,640]{1,0:T(8,128)(2,1)S(1)}, bf16[96,640]{1,0:T(8,128)(2,1)S(1)}, u32[]{:S(2)}, u32[]{:S(2)}) collective-permute-start(bf16[96,640]{1,0:T(8,128)(2,1)S(1)} %shard_map.101.mine_ref), channel_id=1, source_target_pairs={{0,16},{1,5},{2,18},{3,7},{4,20},{5,1},{6,22},{7,3},{8,24},{9,13},... | collective-permute-start | bytes 368648 | tf_op jit(solution)/shard_map/ppermute | solution.py:401
  34.2 5.1 %collective-permute-done.8.other_ref = bf16[96,640]{1,0:T(8,128)(2,1)S(1)} collective-permute-done((bf16[96,640]{1,0:T(8,128)(2,1)S(1)}, bf16[96,640]{1,0:T(8,128)(2,1)S(1)}, u32[]{:S(2)}, u32[]{:S(2)}) %collective-permute-start.8) | collective-permute-done | bytes 122912 | tf_op jit(solution)/shard_map/ppermute | solution.py:401
  39.4 0.1 collective-permute-start.9
  39.4 1.5 %collective-permute-done.9.other_ref = f32[96,640]{1,0:T(8,128)S(1)} collective-permute-done((f32[96,640]{1,0:T(8,128)S(1)}, f32[96,640]{1,0:T(8,128)S(1)}, u32[]{:S(2)}, u32[]{:S(2)}) %collective-permute-start.9) | collective-permute-done | bytes 245792 | tf_op jit(solution)/shard_map/ppermute | solution.py:436
  40.9 1.2 %shard_map.103 = (f32[27,64,64]{2,1,0:T(8,128)}, f32[1,64]{1,0:T(1,128)}) custom-call(s32[1]{0:T(128)} %bitcast.7.core_ref, f32[96,640]{1,0:T(8,128)S(1)} %shard_map.102.mine_ref, f32[96,640]{1,0:T(8,128)S(1)} %collective-permute-done.9.other_ref), custom_call_target="tpu_custom_call" | custom-call | bytes 934148 | tf_op jit(solution)/shard_map/pallas_call | solution.py:320
  (9 shorter events, 0.2 us)
Async XLA Ops:
  1.9 8.5 %collective-permute-start = (bf16[64,256]{1,0:T(8,128)(2,1)S(1)}, bf16[64,256]{1,0:T(8,128)(2,1)S(1)}, u32[]{:S(2)}, u32[]{:S(2)}) collective-permute-start(bf16[64,256]{1,0:T(8,128)(2,1)S(1)} %get-tuple-element.31), channel_id=1, source_target_pairs={{0,4},{4,8},{8,12},{12,16},{16,20},{20,24},{24,28},{28,0},{1,5},{5... | collective-permute-start | bytes 98312 | tf_op jit(solution)/shard_map/ppermute | solution.py:335
  4.9 5.5 %collective-permute-start.1 = (bf16[64,256]{1,0:T(8,128)(2,1)S(1)}, bf16[64,256]{1,0:T(8,128)(2,1)S(1)}, u32[]{:S(2)}, u32[]{:S(2)}) collective-permute-start(bf16[64,256]{1,0:T(8,128)(2,1)S(1)} %get-tuple-element.32), channel_id=1, source_target_pairs={{4,0},{8,4},{12,8},{16,12},{20,16},{24,20},{28,24},{0,28},{5,1},{9... | collective-permute-start | bytes 98312 | tf_op jit(solution)/shard_map/ppermute | solution.py:335
  12.4 1.4 %collective-permute-start.2 = (bf16[96,640]{1,0:T(8,128)(2,1)S(1)}, bf16[96,640]{1,0:T(8,128)(2,1)S(1)}, u32[]{:S(2)}, u32[]{:S(2)}) collective-permute-start(bf16[96,640]{1,0:T(8,128)(2,1)S(1)} %dynamic-slice_convert_fusion), channel_id=1, source_target_pairs={{0,1},{1,0},{2,3},{3,2},{4,5},{5,4},{6,7},{7,6},{8,9},{9,8},{10,11... | collective-permute-start | bytes 368648 | tf_op jit(solution)/shard_map/ppermute | solution.py:391
  13.8 8.3 %collective-permute-start.3 = (bf16[96,640]{1,0:T(8,128)(2,1)S(1)}, bf16[96,640]{1,0:T(8,128)(2,1)S(1)}, u32[]{:S(2)}, u32[]{:S(2)}) collective-permute-start(bf16[96,640]{1,0:T(8,128)(2,1)S(1)} %get-tuple-element.46.mine_ref), channel_id=1, source_target_pairs={{0,2},{1,9},{2,0},{3,11},{4,6},{5,13},{6,4},{7,15},{8,10},{9,1},{1... | collective-permute-start | bytes 368648 | tf_op jit(solution)/shard_map/ppermute | solution.py:401
  15.5 6.6 %collective-permute-start.4 = (bf16[64,256]{1,0:T(8,128)(2,1)S(1)}, bf16[64,256]{1,0:T(8,128)(2,1)S(1)}, u32[]{:S(2)}, u32[]{:S(2)}) collective-permute-start(bf16[64,256]{1,0:T(8,128)(2,1)S(1)} %get-tuple-element.47), channel_id=1, source_target_pairs={{0,4},{4,8},{8,12},{12,16},{16,20},{20,24},{24,28},{28,0},{1,5},{5... | collective-permute-start | bytes 98312 | tf_op jit(solution)/shard_map/ppermute | solution.py:335
  16.2 5.9 %collective-permute-start.5 = (bf16[64,256]{1,0:T(8,128)(2,1)S(1)}, bf16[64,256]{1,0:T(8,128)(2,1)S(1)}, u32[]{:S(2)}, u32[]{:S(2)}) collective-permute-start(bf16[64,256]{1,0:T(8,128)(2,1)S(1)} %get-tuple-element.48), channel_id=1, source_target_pairs={{4,0},{8,4},{12,8},{16,12},{20,16},{24,20},{28,24},{0,28},{5,1},{9... | collective-permute-start | bytes 98312 | tf_op jit(solution)/shard_map/ppermute | solution.py:335
  22.2 4.9 %collective-permute-start.6 = (bf16[96,640]{1,0:T(8,128)(2,1)S(1)}, bf16[96,640]{1,0:T(8,128)(2,1)S(1)}, u32[]{:S(2)}, u32[]{:S(2)}) collective-permute-start(bf16[96,640]{1,0:T(8,128)(2,1)S(1)} %shard_map.97.after_ref.mine_ref), channel_id=1, source_target_pairs={{0,4},{1,17},{2,6},{3,19},{4,0},{5,21},{6,2},{7,23},{8,12},{9,25},... | collective-permute-start | bytes 368648 | tf_op jit(solution)/shard_map/ppermute | solution.py:401
  27.2 4.9 %collective-permute-start.7 = (bf16[96,640]{1,0:T(8,128)(2,1)S(1)}, bf16[96,640]{1,0:T(8,128)(2,1)S(1)}, u32[]{:S(2)}, u32[]{:S(2)}) collective-permute-start(bf16[96,640]{1,0:T(8,128)(2,1)S(1)} %shard_map.99.after_ref.mine_ref), channel_id=1, source_target_pairs={{0,8},{1,3},{2,10},{3,1},{4,12},{5,7},{6,14},{7,5},{8,0},{9,11},{1... | collective-permute-start | bytes 368648 | tf_op jit(solution)/shard_map/ppermute | solution.py:401
  32.2 7.2 %collective-permute-start.8 = (bf16[96,640]{1,0:T(8,128)(2,1)S(1)}, bf16[96,640]{1,0:T(8,128)(2,1)S(1)}, u32[]{:S(2)}, u32[]{:S(2)}) collective-permute-start(bf16[96,640]{1,0:T(8,128)(2,1)S(1)} %shard_map.101.mine_ref), channel_id=1, source_target_pairs={{0,16},{1,5},{2,18},{3,7},{4,20},{5,1},{6,22},{7,3},{8,24},{9,13},... | collective-permute-start | bytes 368648 | tf_op jit(solution)/shard_map/ppermute | solution.py:401
  39.4 1.6 %collective-permute-start.9 = (f32[96,640]{1,0:T(8,128)S(1)}, f32[96,640]{1,0:T(8,128)S(1)}, u32[]{:S(2)}, u32[]{:S(2)}) collective-permute-start(f32[96,640]{1,0:T(8,128)S(1)} %shard_map.102.mine_ref), channel_id=1, source_target_pairs={{0,1},{1,0},{2,3},{3,2},{4,5},{5,4},{6,7},{7,6},{8,9},{9,8},{10,11... | collective-permute-start | bytes 737288 | tf_op jit(solution)/shard_map/ppermute | solution.py:436

commit v3 on v2

--- a/solution.py
+++ b/solution.py
@@ -94,9 +94,29 @@
     return lax.dot_general(x, y, (((1,), (1,)), ((), ())), preferred_element_type=F32)
 
 
+def store_faces(core_ref, low, high, first_ref, second_ref):
+    even = core_ref[0] == 0
+
+    @pl.when(even)
+    def _():
+        first_ref[...] = high
+        second_ref[...] = low
+
+    @pl.when(jnp.logical_not(even))
+    def _():
+        first_ref[...] = low
+        second_ref[...] = high
+
+
+def load_faces(core_ref, first_ref, second_ref):
+    even = core_ref[0] == 0
+    first, second = first_ref[...].astype(F32), second_ref[...].astype(F32)
+    return jnp.where(even, first, second).astype(BF), jnp.where(even, second, first).astype(BF)
+
+
 def stage_kernel(
-    feats_ref, occ_ref, near_ref, cot_ref, weight_ref, bias_ref,
-    low_ref, high_ref, rows_ref, x_ref, keep_ref, cot_out_ref, weight_out_ref, bias_out_ref,
+    core_ref, feats_ref, occ_ref, near_ref, cot_ref, weight_ref, bias_ref,
+    first_ref, second_ref, rows_ref, x_ref, keep_ref, cot_out_ref, weight_out_ref, bias_out_ref,
     near_held_ref, sems,
 ):
     pairs = (
@@ -112,10 +132,12 @@
     copies[1].wait()
     copies[2].wait()
     keep = keep_ref[...].astype(F32)
-    for i, (ref, start) in enumerate(((low_ref, 0), (high_ref, voxels - 128))):
+    faces = []
+    for i, start in enumerate((0, voxels - 128)):
         at = slice(start, start + 128)
         tiles = [x_ref[m, :, at].astype(F32) * keep[m : m + 1, at] for m in range(bricks)]
-        ref[...] = to_planes(tiles)[i].astype(BF)
+        faces.append(to_planes(tiles)[i].astype(BF))
+    store_faces(core_ref, faces[0], faces[1], first_ref, second_ref)
     for copy in copies[3:]:
         copy.wait()
 
@@ -193,13 +215,14 @@
 
 
 def outer_kernel(
-    rows_ref, low_ref, high_ref, moved_ref, pre_ref, cot2_ref, occ2_ref, weight_ref,
+    core_ref, rows_ref, first_ref, second_ref, moved_ref, pre_ref, cot2_ref, occ2_ref, weight_ref,
     result_ref, grad_ref, terms_ref, padded_ref,
 ):
     count, channels, lanes = pre_ref.shape
     bricks = lanes // PLANE
-    moved_low = shifted_face(low_ref[...], rows_ref, -1, bricks)
-    moved_high = shifted_face(high_ref[...], rows_ref, 1, bricks)
+    low, high = load_faces(core_ref, first_ref, second_ref)
+    moved_low = shifted_face(low, rows_ref, -1, bricks)
+    moved_high = shifted_face(high, rows_ref, 1, bricks)
     add_low = dot(weight_ref[2 * channels : 3 * channels, :], moved_low)
     add_high = dot(weight_ref[0:channels, :], moved_high)
     padded_ref[0:channels, :] = jnp.zeros((channels, lanes), BF)
@@ -235,10 +258,10 @@
     return 1.0 + lax.broadcasted_iota(jnp.int32, (1, count), 1).astype(F32) * (1.0 / count)
 
 
-def first_sum_kernel(mine_ref, other_ref, grad_ref, out_ref, low_ref, high_ref):
+def first_sum_kernel(core_ref, mine_ref, other_ref, grad_ref, out_ref, first_ref, second_ref):
     out_ref[...] = (mine_ref[...] + other_ref[...].astype(F32)).astype(BF)
-    low_ref[...] = grad_ref[0]
-    high_ref[...] = grad_ref[grad_ref.shape[0] - 1]
+    last = grad_ref.shape[0] - 1
+    store_faces(core_ref, grad_ref[0], grad_ref[last], first_ref, second_ref)
 
 
 def sum_kernel(mine_ref, other_ref, *refs):
@@ -265,14 +288,15 @@
 
 
 def back_outer_kernel(
-    rows_ref, low_ref, high_ref, total_ref, cot_ref, occ_ref, weight_ref, after_ref,
+    core_ref, rows_ref, first_ref, second_ref, total_ref, cot_ref, occ_ref, weight_ref, after_ref,
     in_grad_ref, done_ref,
 ):
     bricks, channels, voxels = cot_ref.shape
     count = voxels // PLANE
     done_ref[...] = jnp.zeros(done_ref.shape, F32)
-    moved_low = shifted_face(low_ref[...], rows_ref, -1, bricks)
-    moved_high = shifted_face(high_ref[...], rows_ref, 1, bricks)
+    low, high = load_faces(core_ref, first_ref, second_ref)
+    moved_low = shifted_face(low, rows_ref, -1, bricks)
+    moved_high = shifted_face(high, rows_ref, 1, bricks)
     add_low = dot(weight_ref[2 * channels : 3 * channels, :], moved_low)
     add_high = dot(weight_ref[0:channels, :], moved_high)
     keep = occ_ref[...].astype(F32)
@@ -328,11 +352,19 @@
     )(*[pltpu.with_memory_space_constraint(x, pltpu.HBM) if s is HBM else x for s, x in ins])
 
 
-def exchange_faces(low, high):
-    size = lax.axis_size("space")
-    up = [(i, (i + 1) % size) for i in range(size)]
-    down = [(j, i) for i, j in up]
-    return lax.ppermute(high, "space", up), lax.ppermute(low, "space", down)
+def exchange_faces(first, second):
+    spaces, reps = lax.axis_size("space"), lax.axis_size("rep")
+    pairs = []
+    for space in range(spaces):
+        for rep in range(reps):
+            step = 1 if rep % 2 == 0 else -1
+            there, to = space + step, rep
+            if not 0 <= there < spaces:
+                there, to = space, rep ^ 1
+            pairs.append((space * reps + rep, there * reps + to))
+    back = [(j, i) for i, j in pairs]
+    axes = ("space", "rep")
+    return lax.ppermute(first, axes, pairs), lax.ppermute(second, axes, back)
 
 
 def on_device(feats, cotangent, weight, bias, neighbours, occupancy):
@@ -341,16 +373,18 @@
     count, lanes = voxels // PLANE, bricks * PLANE
     width = 9 * channels
     plane = ((channels, lanes), BF)
-    low, high, rows, x, occ, cot, weight, bias = call(
+    core = (lax.axis_index("rep") % 2).astype(jnp.int32)
+    cores = core[None]
+    first, second, rows, x, occ, cot, weight, bias = call(
         stage_kernel,
         [
             plane, plane, ((32, lanes), jnp.int32), (x.shape, BF), (occ.shape, jnp.int32), (x.shape, BF),
             (weight.shape, BF), ((1, channels), F32),
         ],
-        [(HBM, x), (HBM, occ), (HBM, near), (HBM, cot), (HBM, weight), (HBM, bias[None])],
+        [(SMEM, cores), (HBM, x), (HBM, occ), (HBM, near), (HBM, cot), (HBM, weight), (HBM, bias[None])],
         [pltpu.SMEM(near.shape, jnp.int32), pltpu.SemaphoreType.DMA((6,))],
     )
-    from_low, from_high = exchange_faces(low, high)
+    first, second = exchange_faces(first, second)
     moved, pre, cot2, occ2, ahead = call(
         inner_kernel,
         [
@@ -375,7 +409,7 @@
             ((3 * channels, width + 64), F32),
         ],
         [
-            (VMEM, rows), (VMEM, from_low), (VMEM, from_high), (VMEM, moved), (VMEM, pre),
+            (SMEM, cores), (VMEM, rows), (VMEM, first), (VMEM, second), (VMEM, moved), (VMEM, pre),
             (VMEM, cot2), (VMEM, occ2), (VMEM, ahead),
         ],
         [pltpu.VMEM((channels * (count + 2), lanes), BF)],
@@ -383,26 +417,27 @@
     )
     axes = ("space", "rep")
     devices = lax.axis_size("space") * lax.axis_size("rep")
-    core = lax.axis_index("rep") % 2
     half = 3 * channels // 2
     partner = [(i, i ^ 1) for i in range(devices)]
     theirs = lax.dynamic_slice_in_dim(terms, (1 - core) * half, half, 0).astype(BF)
     mine = lax.dynamic_slice_in_dim(terms, core * half, half, 0)
     other = lax.ppermute(theirs, axes, partner)
     sent = ((half, terms.shape[1]), BF)
-    mine, low, high = call(
-        first_sum_kernel, [sent, plane, plane], [(VMEM, mine), (VMEM, other), (VMEM, grad)]
+    mine, first, second = call(
+        first_sum_kernel,
+        [sent, plane, plane],
+        [(SMEM, cores), (VMEM, mine), (VMEM, other), (VMEM, grad)],
     )
     bits = [1 << i for i in range(1, (devices).bit_length() - 1)]
     turn = len(bits) // 2
-    grad_low = grad_high = total = in_grad = result = None
+    total = in_grad = result = None
     rounds = list(zip(bits, bits[turn:] + bits[:turn]))
     for i, steps in enumerate(rounds):
         other = lax.ppermute(mine, axes, [(j, j ^ steps[j % 2]) for j in range(devices)])
         held = []
         if i == 0:
-            grad_low, grad_high = exchange_faces(low, high)
-            held = [grad_low, grad_high]
+            first, second = exchange_faces(first, second)
+            held = [first, second]
         if i == 1:
             result, total, back = call(
                 back_inner_kernel,
@@ -421,7 +456,7 @@
                 back_outer_kernel,
                 [((bricks, channels, voxels), BF), ((8, 128), F32)],
                 [
-                    (VMEM, rows), (VMEM, grad_low), (VMEM, grad_high), (VMEM, total), (VMEM, cot),
+                    (SMEM, cores), (VMEM, rows), (VMEM, first), (VMEM, second), (VMEM, total), (VMEM, cot),
                     (VMEM, occ), (VMEM, back), (ANY, mine),
                 ],
                 flops=2 * 6 * channels * channels * bricks * voxels,
@@ -440,7 +475,7 @@
     weight_grad, bias_grad = call(
         functools.partial(final_kernel, normaliser),
         [(weight.shape, F32), ((1, channels), F32)],
-        [(SMEM, core.astype(jnp.int32)[None]), (VMEM, mine), (VMEM, other)],
+        [(SMEM, cores), (VMEM, mine), (VMEM, other)],
         [pltpu.VMEM(terms.shape, F32)],
     )
     return result[None], in_grad[None], weight_grad, bias_grad[0]

time: 42.3 us -> 40.4 us (0.955)
  starting transfers between devices: 14.9 us -> 13.1 us
    ppermute x4, starting transfers between devices: 10.8 us -> 5.44 us  [exchange_faces(): return (lax.ppermute(first, axes, pairs), lax.ppermute(second, axes, back))]
    ppermute x4, waiting for transfers between devices: 10.3 us -> 6.53 us  [on_device(): lax.ppermute(mine, axes, [(j, j ^ steps[j % 2]) for j in range(devices)])]
    ppermute x4, starting transfers between devices: 3.9 us -> 7.52 us  [on_device(): lax.ppermute(mine, axes, [(j, j ^ steps[j % 2]) for j in range(devices)])]
    ppermute x4, waiting for transfers between devices: 1.9 us -> 5.4 us  [exchange_faces(): return (lax.ppermute(first, axes, pairs), lax.ppermute(second, axes, back))]
  transfers between devices with their start and end apart: 10 -> 10, of which waited for: 6 -> 8; matrix products, arithmetic and copies ran while one was open for 0% -> 0% of each run, Pallas kernels for 17% -> 17%
where the time goes in v3:
time: 40.4 us; the launch traced here: 40.2 us
  waiting for transfers between devices  14.7 us (36%)
  starting transfers between devices  13.1 us (32%)
  Pallas kernels  11.6 us (29%)
  between operations  0.74 us (2%)
    pallas_call x11, Pallas kernels, call(): pl.pallas_call(body, out_shape=shapes, in_specs=[spec for spec, _ in ins]...  11.6 us
    ppermute x4, starting transfers between devices, on_device(): lax.ppermute(mine, axes, [(j, j ^ steps[j % 2]) for j in range(devices)])  7.52 us
    ppermute x4, waiting for transfers between devices, on_device(): lax.ppermute(mine, axes, [(j, j ^ steps[j % 2]) for j in range(devices)])  6.53 us
    ppermute x4, starting transfers between devices, exchange_faces(): return (lax.ppermute(first, axes, pairs), lax.ppermute(second, axes, back))  5.44 us
    ppermute x4, waiting for transfers between devices, exchange_faces(): return (lax.ppermute(first, axes, pairs), lax.ppermute(second, axes, back))  5.4 us
    ppermute x1, waiting for transfers between devices, on_device(): other = lax.ppermute(mine, axes, partner)  1.5 us
    ppermute x1, waiting for transfers between devices, on_device(): other = lax.ppermute(theirs, axes, partner)  1.28 us
  transfers between devices with their start and end apart: 10, of which 8 were waited for; matrix products, arithmetic and copies ran while one was open for 0% of the time, Pallas kernels for 17%

profile of v3, /device:TPU:0, one launch (start us, length us, event | category | flops | bytes accessed | tf_op | source)
XLA Modules:
  0.0 40.2 jit_solution(438378528421472084)
XLA Ops:
  0.6 1.2 %shard_map.93 = (bf16[64,256]{1,0:T(8,128)(2,1)S(1)}, bf16[64,256]{1,0:T(8,128)(2,1)S(1)}, s32[32,256]{1,0:T(8,128)S(1)}, bf16[4,64,512]{2,1,0:T(8,128)(2,1)S(1)...) custom-call(s32[1]{0:T(128)} %bitcast.core_ref, ...), custom_call_target="tpu_custom_call" | custom-call | bytes 1606564 | tf_op jit(solution)/shard_map/pallas_call | solution.py:344
  1.9 3.0 %collective-permute-start = (bf16[64,256]{1,0:T(8,128)(2,1)S(1)}, bf16[64,256]{1,0:T(8,128)(2,1)S(1)}, u32[]{:S(2)}, u32[]{:S(2)}) collective-permute-start(bf16[64,256]{1,0:T(8,128)(2,1)S(1)} %get-tuple-element.31), channel_id=1, source_target_pairs={{0,4},{1,0},{2,6},{3,2},{4,8},{5,1},{6,10},{7,3},{8,12},{9,5},{10,... | collective-permute-start | bytes 98312 | tf_op jit(solution)/shard_map/ppermute | solution.py:367
  4.9 0.0 collective-permute-start.1
  4.9 2.4 %shard_map.94 = (bf16[8,576,256]{2,1,0:T(8,128)(2,1)S(1)}, f32[8,64,256]{2,1,0:T(8,128)S(1)}, bf16[8,64,256]{2,1,0:T(8,128)(2,1)S(1)}, f32[8,8,256]{2,1,0:T(8,128)S(1)}, bf16[192,576]{1,0:T(8,128)(2,1)S(1)}) custom-call(s32[32,256]{1,0:T(8,128)S(1)} %get-tuple-element.30.rows_ref, bf16[4,64,512]{2,1,0:T(8,128)(2,1)S(1)} %get-tuple-element.33.feats_ref, ...), custom_call_target="tpu_custom_call" | custom-call | flops 452984832 | bytes 4219136 | tf_op jit(solution)/shard_map/pallas_call | solution.py:344
  7.3 1.5 %collective-permute-done.1.second_ref = bf16[64,256]{1,0:T(8,128)(2,1)S(1)} collective-permute-done((bf16[64,256]{1,0:T(8,128)(2,1)S(1)}, bf16[64,256]{1,0:T(8,128)(2,1)S(1)}, u32[]{:S(2)}, u32[]{:S(2)}) %collective-permute-start.1) | collective-permute-done | bytes 32800 | tf_op jit(solution)/shard_map/ppermute | solution.py:367
  8.8 2.0 %shard_map.95 = (bf16[8,64,256]{2,1,0:T(8,128)(2,1)S(1)}, bf16[8,64,256]{2,1,0:T(8,128)(2,1)S(1)}, f32[192,640]{1,0:T(8,128)S(1)}) custom-call(s32[1]{0:T(128)} %bitcast.core_ref, s32[32,256]{1,0:T(8,128)S(1)} %get-tuple-element.30.rows_ref, bf16[64,256]{1,0:T(8,128)(2,1)S(1)} %collective-permute-done.first_ref, ...), custom_call_target="tpu_custom_call" | custom-call | flops 452984832 | bytes 4546564 | tf_op jit(solution)/shard_map/pallas_call | solution.py:344
  10.8 0.1 collective-permute-start.2
  10.9 1.3 %collective-permute-done.2.other_ref = bf16[96,640]{1,0:T(8,128)(2,1)S(1)} collective-permute-done((bf16[96,640]{1,0:T(8,128)(2,1)S(1)}, bf16[96,640]{1,0:T(8,128)(2,1)S(1)}, u32[]{:S(2)}, u32[]{:S(2)}) %collective-permute-start.2) | collective-permute-done | bytes 122912 | tf_op jit(solution)/shard_map/ppermute | solution.py:424
  12.3 1.6 %collective-permute-start.3 = (bf16[96,640]{1,0:T(8,128)(2,1)S(1)}, bf16[96,640]{1,0:T(8,128)(2,1)S(1)}, u32[]{:S(2)}, u32[]{:S(2)}) collective-permute-start(bf16[96,640]{1,0:T(8,128)(2,1)S(1)} %get-tuple-element.46.mine_ref), channel_id=1, source_target_pairs={{0,2},{1,9},{2,0},{3,11},{4,6},{5,13},{6,4},{7,15},{8,10},{9,1},{1... | collective-permute-start | bytes 368648 | tf_op jit(solution)/shard_map/ppermute | solution.py:436
  13.9 2.4 %collective-permute-start.4 = (bf16[64,256]{1,0:T(8,128)(2,1)S(1)}, bf16[64,256]{1,0:T(8,128)(2,1)S(1)}, u32[]{:S(2)}, u32[]{:S(2)}) collective-permute-start(bf16[64,256]{1,0:T(8,128)(2,1)S(1)} %get-tuple-element.47), channel_id=1, source_target_pairs={{0,4},{1,0},{2,6},{3,2},{4,8},{5,1},{6,10},{7,3},{8,12},{9,5},{10,... | collective-permute-start | bytes 98312 | tf_op jit(solution)/shard_map/ppermute | solution.py:367
  16.3 0.0 collective-permute-start.5
  16.3 1.7 %collective-permute-done.4.refs_0_.first_ref = bf16[64,256]{1,0:T(8,128)(2,1)S(1)} collective-permute-done((bf16[64,256]{1,0:T(8,128)(2,1)S(1)}, bf16[64,256]{1,0:T(8,128)(2,1)S(1)}, u32[]{:S(2)}, u32[]{:S(2)}) %collective-permute-start.4) | collective-permute-done | bytes 32800 | tf_op jit(solution)/shard_map/ppermute | solution.py:367
  18.0 2.2 %collective-permute-done.5.refs_1_.second_ref = bf16[64,256]{1,0:T(8,128)(2,1)S(1)} collective-permute-done((bf16[64,256]{1,0:T(8,128)(2,1)S(1)}, bf16[64,256]{1,0:T(8,128)(2,1)S(1)}, u32[]{:S(2)}, u32[]{:S(2)}) %collective-permute-start.5) | collective-permute-done | bytes 32800 | tf_op jit(solution)/shard_map/ppermute | solution.py:367
  20.2 1.6 %collective-permute-start.6 = (bf16[96,640]{1,0:T(8,128)(2,1)S(1)}, bf16[96,640]{1,0:T(8,128)(2,1)S(1)}, u32[]{:S(2)}, u32[]{:S(2)}) collective-permute-start(bf16[96,640]{1,0:T(8,128)(2,1)S(1)} %shard_map.97.after_ref.mine_ref), channel_id=1, source_target_pairs={{0,4},{1,17},{2,6},{3,19},{4,0},{5,21},{6,2},{7,23},{8,12},{9,25},... | collective-permute-start | bytes 368648 | tf_op jit(solution)/shard_map/ppermute | solution.py:436
  21.9 3.0 %shard_map.98 = (bf16[4,64,512]{2,1,0:T(8,128)(2,1)}, f32[640,256]{1,0:T(8,128)S(1)}, bf16[192,576]{1,0:T(8,128)(2,1)S(1)}) custom-call(s32[32,256]{1,0:T(8,128)S(1)} %get-tuple-element.30.rows_ref, bf16[8,64,256]{2,1,0:T(8,128)(2,1)S(1)} %get-tuple-element.43.grad_ref, bf16[8,64,256]{2,1,0:T(8,128)(2,1)S(1)} %get-tuple-element.44.result2_ref, ...), custom_call_target="tpu_custom_call" | custom-call | flops 452984832 | bytes 2039808 | tf_op jit(solution)/shard_map/pallas_call | solution.py:344
  24.9 0.3 collective-permute-done.6.other_ref
  25.2 1.6 %collective-permute-start.7 = (bf16[96,640]{1,0:T(8,128)(2,1)S(1)}, bf16[96,640]{1,0:T(8,128)(2,1)S(1)}, u32[]{:S(2)}, u32[]{:S(2)}) collective-permute-start(bf16[96,640]{1,0:T(8,128)(2,1)S(1)} %shard_map.99.after_ref.mine_ref), channel_id=1, source_target_pairs={{0,8},{1,3},{2,10},{3,1},{4,12},{5,7},{6,14},{7,5},{8,0},{9,11},{1... | collective-permute-start | bytes 368648 | tf_op jit(solution)/shard_map/ppermute | solution.py:436
  26.9 1.6 %shard_map.100 = (bf16[4,64,512]{2,1,0:T(8,128)(2,1)}, f32[8,128]{1,0:T(8,128)S(1)}) custom-call(s32[1]{0:T(128)} %bitcast.core_ref, s32[32,256]{1,0:T(8,128)S(1)} %get-tuple-element.30.rows_ref, bf16[64,256]{1,0:T(8,128)(2,1)S(1)} %collective-permute-done.4.refs_0_.first_ref, bf16[64,256]{1,0:T(8,128)(2,1)S(1)} %collective-permute-done.5.refs_1_.second_ref, ...), custom_call_target="tpu_custom_call" | custom-call | flops 100663296 | bytes 1634308 | tf_op jit(solution)/shard_map/pallas_call | solution.py:344
  28.5 1.7 %collective-permute-done.7.other_ref = bf16[96,640]{1,0:T(8,128)(2,1)S(1)} collective-permute-done((bf16[96,640]{1,0:T(8,128)(2,1)S(1)}, bf16[96,640]{1,0:T(8,128)(2,1)S(1)}, u32[]{:S(2)}, u32[]{:S(2)}) %collective-permute-start.7) | collective-permute-done | bytes 122912 | tf_op jit(solution)/shard_map/ppermute | solution.py:436
  30.2 2.7 %collective-permute-start.8 = (bf16[96,640]{1,0:T(8,128)(2,1)S(1)}, bf16[96,640]{1,0:T(8,128)(2,1)S(1)}, u32[]{:S(2)}, u32[]{:S(2)}) collective-permute-start(bf16[96,640]{1,0:T(8,128)(2,1)S(1)} %shard_map.101.mine_ref), channel_id=1, source_target_pairs={{0,16},{1,5},{2,18},{3,7},{4,20},{5,1},{6,22},{7,3},{8,24},{9,13},... | collective-permute-start | bytes 368648 | tf_op jit(solution)/shard_map/ppermute | solution.py:436
  32.9 4.5 %collective-permute-done.8.other_ref = bf16[96,640]{1,0:T(8,128)(2,1)S(1)} collective-permute-done((bf16[96,640]{1,0:T(8,128)(2,1)S(1)}, bf16[96,640]{1,0:T(8,128)(2,1)S(1)}, u32[]{:S(2)}, u32[]{:S(2)}) %collective-permute-start.8) | collective-permute-done | bytes 122912 | tf_op jit(solution)/shard_map/ppermute | solution.py:436
  37.4 0.1 collective-permute-start.9
  37.5 1.5 %collective-permute-done.9.other_ref = f32[96,640]{1,0:T(8,128)S(1)} collective-permute-done((f32[96,640]{1,0:T(8,128)S(1)}, f32[96,640]{1,0:T(8,128)S(1)}, u32[]{:S(2)}, u32[]{:S(2)}) %collective-permute-start.9) | collective-permute-done | bytes 245792 | tf_op jit(solution)/shard_map/ppermute | solution.py:471
  39.0 1.2 %shard_map.103 = (f32[27,64,64]{2,1,0:T(8,128)}, f32[1,64]{1,0:T(1,128)}) custom-call(s32[1]{0:T(128)} %bitcast.core_ref, f32[96,640]{1,0:T(8,128)S(1)} %shard_map.102.mine_ref, f32[96,640]{1,0:T(8,128)S(1)} %collective-permute-done.9.other_ref), custom_call_target="tpu_custom_call" | custom-call | bytes 934148 | tf_op jit(solution)/shard_map/pallas_call | solution.py:344
  (9 shorter events, 0.2 us)
Async XLA Ops:
  1.9 5.4 %collective-permute-start = (bf16[64,256]{1,0:T(8,128)(2,1)S(1)}, bf16[64,256]{1,0:T(8,128)(2,1)S(1)}, u32[]{:S(2)}, u32[]{:S(2)}) collective-permute-start(bf16[64,256]{1,0:T(8,128)(2,1)S(1)} %get-tuple-element.31), channel_id=1, source_target_pairs={{0,4},{1,0},{2,6},{3,2},{4,8},{5,1},{6,10},{7,3},{8,12},{9,5},{10,... | collective-permute-start | bytes 98312 | tf_op jit(solution)/shard_map/ppermute | solution.py:367
  4.9 3.9 %collective-permute-start.1 = (bf16[64,256]{1,0:T(8,128)(2,1)S(1)}, bf16[64,256]{1,0:T(8,128)(2,1)S(1)}, u32[]{:S(2)}, u32[]{:S(2)}) collective-permute-start(bf16[64,256]{1,0:T(8,128)(2,1)S(1)} %get-tuple-element.32), channel_id=1, source_target_pairs={{4,0},{0,1},{6,2},{2,3},{8,4},{1,5},{10,6},{3,7},{12,8},{5,9},{14,... | collective-permute-start | bytes 98312 | tf_op jit(solution)/shard_map/ppermute | solution.py:367
  10.8 1.4 %collective-permute-start.2 = (bf16[96,640]{1,0:T(8,128)(2,1)S(1)}, bf16[96,640]{1,0:T(8,128)(2,1)S(1)}, u32[]{:S(2)}, u32[]{:S(2)}) collective-permute-start(bf16[96,640]{1,0:T(8,128)(2,1)S(1)} %dynamic-slice_convert_fusion), channel_id=1, source_target_pairs={{0,1},{1,0},{2,3},{3,2},{4,5},{5,4},{6,7},{7,6},{8,9},{9,8},{10,11... | collective-permute-start | bytes 368648 | tf_op jit(solution)/shard_map/ppermute | solution.py:424
  12.3 8.0 %collective-permute-start.3 = (bf16[96,640]{1,0:T(8,128)(2,1)S(1)}, bf16[96,640]{1,0:T(8,128)(2,1)S(1)}, u32[]{:S(2)}, u32[]{:S(2)}) collective-permute-start(bf16[96,640]{1,0:T(8,128)(2,1)S(1)} %get-tuple-element.46.mine_ref), channel_id=1, source_target_pairs={{0,2},{1,9},{2,0},{3,11},{4,6},{5,13},{6,4},{7,15},{8,10},{9,1},{1... | collective-permute-start | bytes 368648 | tf_op jit(solution)/shard_map/ppermute | solution.py:436
  13.9 4.1 %collective-permute-start.4 = (bf16[64,256]{1,0:T(8,128)(2,1)S(1)}, bf16[64,256]{1,0:T(8,128)(2,1)S(1)}, u32[]{:S(2)}, u32[]{:S(2)}) collective-permute-start(bf16[64,256]{1,0:T(8,128)(2,1)S(1)} %get-tuple-element.47), channel_id=1, source_target_pairs={{0,4},{1,0},{2,6},{3,2},{4,8},{5,1},{6,10},{7,3},{8,12},{9,5},{10,... | collective-permute-start | bytes 98312 | tf_op jit(solution)/shard_map/ppermute | solution.py:367
  16.3 3.9 %collective-permute-start.5 = (bf16[64,256]{1,0:T(8,128)(2,1)S(1)}, bf16[64,256]{1,0:T(8,128)(2,1)S(1)}, u32[]{:S(2)}, u32[]{:S(2)}) collective-permute-start(bf16[64,256]{1,0:T(8,128)(2,1)S(1)} %get-tuple-element.48), channel_id=1, source_target_pairs={{4,0},{0,1},{6,2},{2,3},{8,4},{1,5},{10,6},{3,7},{12,8},{5,9},{14,... | collective-permute-start | bytes 98312 | tf_op jit(solution)/shard_map/ppermute | solution.py:367
  20.2 4.9 %collective-permute-start.6 = (bf16[96,640]{1,0:T(8,128)(2,1)S(1)}, bf16[96,640]{1,0:T(8,128)(2,1)S(1)}, u32[]{:S(2)}, u32[]{:S(2)}) collective-permute-start(bf16[96,640]{1,0:T(8,128)(2,1)S(1)} %shard_map.97.after_ref.mine_ref), channel_id=1, source_target_pairs={{0,4},{1,17},{2,6},{3,19},{4,0},{5,21},{6,2},{7,23},{8,12},{9,25},... | collective-permute-start | bytes 368648 | tf_op jit(solution)/shard_map/ppermute | solution.py:436
  25.2 4.9 %collective-permute-start.7 = (bf16[96,640]{1,0:T(8,128)(2,1)S(1)}, bf16[96,640]{1,0:T(8,128)(2,1)S(1)}, u32[]{:S(2)}, u32[]{:S(2)}) collective-permute-start(bf16[96,640]{1,0:T(8,128)(2,1)S(1)} %shard_map.99.after_ref.mine_ref), channel_id=1, source_target_pairs={{0,8},{1,3},{2,10},{3,1},{4,12},{5,7},{6,14},{7,5},{8,0},{9,11},{1... | collective-permute-start | bytes 368648 | tf_op jit(solution)/shard_map/ppermute | solution.py:436
  30.2 7.2 %collective-permute-start.8 = (bf16[96,640]{1,0:T(8,128)(2,1)S(1)}, bf16[96,640]{1,0:T(8,128)(2,1)S(1)}, u32[]{:S(2)}, u32[]{:S(2)}) collective-permute-start(bf16[96,640]{1,0:T(8,128)(2,1)S(1)} %shard_map.101.mine_ref), channel_id=1, source_target_pairs={{0,16},{1,5},{2,18},{3,7},{4,20},{5,1},{6,22},{7,3},{8,24},{9,13},... | collective-permute-start | bytes 368648 | tf_op jit(solution)/shard_map/ppermute | solution.py:436
  37.4 1.6 %collective-permute-start.9 = (f32[96,640]{1,0:T(8,128)S(1)}, f32[96,640]{1,0:T(8,128)S(1)}, u32[]{:S(2)}, u32[]{:S(2)}) collective-permute-start(f32[96,640]{1,0:T(8,128)S(1)} %shard_map.102.mine_ref), channel_id=1, source_target_pairs={{0,1},{1,0},{2,3},{3,2},{4,5},{5,4},{6,7},{7,6},{8,9},{9,8},{10,11... | collective-permute-start | bytes 737288 | tf_op jit(solution)/shard_map/ppermute | solution.py:471

commit v4 on v3

--- a/solution.py
+++ b/solution.py
@@ -315,12 +315,12 @@
             ).astype(BF)
 
 
-def final_kernel(normaliser, core_ref, mine_ref, other_ref, weight_ref, bias_ref, whole_ref):
+def final_kernel(normaliser, own_ref, mine_ref, other_ref, weight_ref, bias_ref, whole_ref):
     half, columns = mine_ref.shape
     channels = weight_ref.shape[1]
-    core = core_ref[0]
-    whole_ref[pl.ds(core * half, half), :] = mine_ref[...]
-    whole_ref[pl.ds((1 - core) * half, half), :] = other_ref[...]
+    own = own_ref[0]
+    whole_ref[pl.ds(own * half, half), :] = mine_ref[...]
+    whole_ref[pl.ds((1 - own) * half, half), :] = other_ref[...]
     for r in range(3):
         rows = slice(channels * r, channels * (r + 1))
         for t in range(columns // 128):
@@ -419,8 +419,10 @@
     devices = lax.axis_size("space") * lax.axis_size("rep")
     half = 3 * channels // 2
     partner = [(i, i ^ 1) for i in range(devices)]
-    theirs = lax.dynamic_slice_in_dim(terms, (1 - core) * half, half, 0).astype(BF)
-    mine = lax.dynamic_slice_in_dim(terms, core * half, half, 0)
+    me = lax.axis_index("space") * lax.axis_size("rep") + lax.axis_index("rep")
+    own = lax.population_count(me.astype(jnp.int32)) & 1
+    theirs = lax.dynamic_slice_in_dim(terms, (1 - own) * half, half, 0).astype(BF)
+    mine = lax.dynamic_slice_in_dim(terms, own * half, half, 0)
     other = lax.ppermute(theirs, axes, partner)
     sent = ((half, terms.shape[1]), BF)
     mine, first, second = call(
@@ -433,11 +435,11 @@
     total = in_grad = result = None
     rounds = list(zip(bits, bits[turn:] + bits[:turn]))
     for i, steps in enumerate(rounds):
-        other = lax.ppermute(mine, axes, [(j, j ^ steps[j % 2]) for j in range(devices)])
+        pairs = [(j, j ^ 1 ^ steps[j.bit_count() % 2]) for j in range(devices)]
+        other = lax.ppermute(mine, axes, pairs)
         held = []
         if i == 0:
             first, second = exchange_faces(first, second)
-            held = [first, second]
         if i == 1:
             result, total, back = call(
                 back_inner_kernel,
@@ -450,7 +452,7 @@
                 [pltpu.VMEM((count, width, lanes), BF)],
                 flops=2 * 27 * channels * channels * bricks * voxels,
             )
-            held = [total]
+            held = [total, first, second]
         if i == 2:
             in_grad, done = call(
                 back_outer_kernel,
@@ -475,7 +477,7 @@
     weight_grad, bias_grad = call(
         functools.partial(final_kernel, normaliser),
         [(weight.shape, F32), ((1, channels), F32)],
-        [(SMEM, cores), (VMEM, mine), (VMEM, other)],
+        [(SMEM, own[None]), (VMEM, mine), (VMEM, other)],
         [pltpu.VMEM(terms.shape, F32)],
     )
     return result[None], in_grad[None], weight_grad, bias_grad[0]

time: 40.4 us -> 39.5 us (0.978)
  starting transfers between devices: 13.1 us -> 10.7 us
  waiting for transfers between devices: 14.7 us -> 16.2 us
    ppermute x4, waiting for transfers between devices: 6.53 us -> 11 us  [on_device(): other = lax.ppermute(mine, axes, pairs)]
    ppermute x4, waiting for transfers between devices: 5.4 us -> 2.38 us  [exchange_faces(): return (lax.ppermute(first, axes, pairs), lax.ppermute(second, axes, back))]
    ppermute x4, starting transfers between devices: 7.52 us -> 5 us  [on_device(): other = lax.ppermute(mine, axes, pairs)]
  transfers between devices with their start and end apart: 10 -> 10, of which waited for: 8 -> 7; matrix products, arithmetic and copies ran while one was open for 0% -> 0% of each run, Pallas kernels for 17% -> 18%
where the time goes in v4:
time: 39.5 us; the launch traced here: 39.3 us
  waiting for transfers between devices  16.2 us (41%)
  Pallas kernels  11.6 us (29%)
  starting transfers between devices  10.7 us (27%)
  between operations  0.75 us (2%)
    pallas_call x11, Pallas kernels, call(): pl.pallas_call(body, out_shape=shapes, in_specs=[spec for spec, _ in ins]...  11.6 us
    ppermute x4, waiting for transfers between devices, on_device(): other = lax.ppermute(mine, axes, pairs)  11 us
    ppermute x4, starting transfers between devices, exchange_faces(): return (lax.ppermute(first, axes, pairs), lax.ppermute(second, axes, back))  5.59 us
    ppermute x4, starting transfers between devices, on_device(): other = lax.ppermute(mine, axes, pairs)  5 us
    ppermute x4, waiting for transfers between devices, exchange_faces(): return (lax.ppermute(first, axes, pairs), lax.ppermute(second, axes, back))  2.38 us
    ppermute x1, waiting for transfers between devices, on_device(): other = lax.ppermute(mine, axes, partner)  1.5 us
    ppermute x1, waiting for transfers between devices, on_device(): other = lax.ppermute(theirs, axes, partner)  1.29 us
  transfers between devices with their start and end apart: 10, of which 7 were waited for; matrix products, arithmetic and copies ran while one was open for 0% of the time, Pallas kernels for 18%

profile of v4, /device:TPU:0, one launch (start us, length us, event | category | flops | bytes accessed | tf_op | source)
XLA Modules:
  0.0 39.3 jit_solution(6436804494806596775)
XLA Ops:
  0.6 1.2 %shard_map.93 = (bf16[64,256]{1,0:T(8,128)(2,1)S(1)}, bf16[64,256]{1,0:T(8,128)(2,1)S(1)}, s32[32,256]{1,0:T(8,128)S(1)}, bf16[4,64,512]{2,1,0:T(8,128)(2,1)S(1)...) custom-call(s32[1]{0:T(128)} %bitcast.core_ref, ...), custom_call_target="tpu_custom_call" | custom-call | bytes 1606564 | tf_op jit(solution)/shard_map/pallas_call | solution.py:344
  1.9 3.0 %collective-permute-start = (bf16[64,256]{1,0:T(8,128)(2,1)S(1)}, bf16[64,256]{1,0:T(8,128)(2,1)S(1)}, u32[]{:S(2)}, u32[]{:S(2)}) collective-permute-start(bf16[64,256]{1,0:T(8,128)(2,1)S(1)} %get-tuple-element.31), channel_id=1, source_target_pairs={{0,4},{1,0},{2,6},{3,2},{4,8},{5,1},{6,10},{7,3},{8,12},{9,5},{10,... | collective-permute-start | bytes 98312 | tf_op jit(solution)/shard_map/ppermute | solution.py:367
  4.9 0.0 collective-permute-start.1
  4.9 2.4 %shard_map.94 = (bf16[8,576,256]{2,1,0:T(8,128)(2,1)S(1)}, f32[8,64,256]{2,1,0:T(8,128)S(1)}, bf16[8,64,256]{2,1,0:T(8,128)(2,1)S(1)}, f32[8,8,256]{2,1,0:T(8,128)S(1)}, bf16[192,576]{1,0:T(8,128)(2,1)S(1)}) custom-call(s32[32,256]{1,0:T(8,128)S(1)} %get-tuple-element.30.rows_ref, bf16[4,64,512]{2,1,0:T(8,128)(2,1)S(1)} %get-tuple-element.33.feats_ref, ...), custom_call_target="tpu_custom_call" | custom-call | flops 452984832 | bytes 4219136 | tf_op jit(solution)/shard_map/pallas_call | solution.py:344
  7.3 0.0 collective-permute-done.first_ref
  7.3 1.5 %collective-permute-done.1.second_ref = bf16[64,256]{1,0:T(8,128)(2,1)S(1)} collective-permute-done((bf16[64,256]{1,0:T(8,128)(2,1)S(1)}, bf16[64,256]{1,0:T(8,128)(2,1)S(1)}, u32[]{:S(2)}, u32[]{:S(2)}) %collective-permute-start.1) | collective-permute-done | bytes 32800 | tf_op jit(solution)/shard_map/ppermute | solution.py:367
  8.8 2.0 %shard_map.95 = (bf16[8,64,256]{2,1,0:T(8,128)(2,1)S(1)}, bf16[8,64,256]{2,1,0:T(8,128)(2,1)S(1)}, f32[192,640]{1,0:T(8,128)S(1)}) custom-call(s32[1]{0:T(128)} %bitcast.core_ref, s32[32,256]{1,0:T(8,128)S(1)} %get-tuple-element.30.rows_ref, bf16[64,256]{1,0:T(8,128)(2,1)S(1)} %collective-permute-done.first_ref, ...), custom_call_target="tpu_custom_call" | custom-call | flops 452984832 | bytes 4546564 | tf_op jit(solution)/shard_map/pallas_call | solution.py:344
  10.8 0.1 collective-permute-start.2
  10.9 1.3 %collective-permute-done.2.other_ref = bf16[96,640]{1,0:T(8,128)(2,1)S(1)} collective-permute-done((bf16[96,640]{1,0:T(8,128)(2,1)S(1)}, bf16[96,640]{1,0:T(8,128)(2,1)S(1)}, u32[]{:S(2)}, u32[]{:S(2)}) %collective-permute-start.2) | collective-permute-done | bytes 122912 | tf_op jit(solution)/shard_map/ppermute | solution.py:426
  12.3 1.3 %collective-permute-start.3 = (bf16[96,640]{1,0:T(8,128)(2,1)S(1)}, bf16[96,640]{1,0:T(8,128)(2,1)S(1)}, u32[]{:S(2)}, u32[]{:S(2)}) collective-permute-start(bf16[96,640]{1,0:T(8,128)(2,1)S(1)} %get-tuple-element.46.mine_ref), channel_id=1, source_target_pairs={{0,3},{1,8},{2,11},{3,0},{4,13},{5,6},{6,5},{7,14},{8,1},{9,10},{1... | collective-permute-start | bytes 368648 | tf_op jit(solution)/shard_map/ppermute | solution.py:439
  13.6 3.0 %collective-permute-done.3.other_ref = bf16[96,640]{1,0:T(8,128)(2,1)S(1)} collective-permute-done((bf16[96,640]{1,0:T(8,128)(2,1)S(1)}, bf16[96,640]{1,0:T(8,128)(2,1)S(1)}, u32[]{:S(2)}, u32[]{:S(2)}) %collective-permute-start.3) | collective-permute-done | bytes 122912 | tf_op jit(solution)/shard_map/ppermute | solution.py:439
  16.7 2.3 %collective-permute-start.6 = (bf16[96,640]{1,0:T(8,128)(2,1)S(1)}, bf16[96,640]{1,0:T(8,128)(2,1)S(1)}, u32[]{:S(2)}, u32[]{:S(2)}) collective-permute-start(bf16[96,640]{1,0:T(8,128)(2,1)S(1)} %shard_map.97.after_ref.mine_ref), channel_id=1, source_target_pairs={{0,5},{1,16},{2,19},{3,6},{4,21},{5,0},{6,3},{7,22},{8,25},{9,12},... | collective-permute-start | bytes 368648 | tf_op jit(solution)/shard_map/ppermute | solution.py:439
  18.9 2.6 %collective-permute-start.4 = (bf16[64,256]{1,0:T(8,128)(2,1)S(1)}, bf16[64,256]{1,0:T(8,128)(2,1)S(1)}, u32[]{:S(2)}, u32[]{:S(2)}) collective-permute-start(bf16[64,256]{1,0:T(8,128)(2,1)S(1)} %get-tuple-element.48), channel_id=1, source_target_pairs={{0,4},{1,0},{2,6},{3,2},{4,8},{5,1},{6,10},{7,3},{8,12},{9,5},{10,... | collective-permute-start | bytes 98312 | tf_op jit(solution)/shard_map/ppermute | solution.py:367
  21.5 3.0 %shard_map.98 = (bf16[4,64,512]{2,1,0:T(8,128)(2,1)}, f32[640,256]{1,0:T(8,128)S(1)}, bf16[192,576]{1,0:T(8,128)(2,1)S(1)}) custom-call(s32[32,256]{1,0:T(8,128)S(1)} %get-tuple-element.30.rows_ref, bf16[8,64,256]{2,1,0:T(8,128)(2,1)S(1)} %get-tuple-element.43.grad_ref, bf16[8,64,256]{2,1,0:T(8,128)(2,1)S(1)} %get-tuple-element.44.result2_ref, ...), custom_call_target="tpu_custom_call" | custom-call | flops 452984832 | bytes 2039808 | tf_op jit(solution)/shard_map/pallas_call | solution.py:344
  24.5 0.0 collective-permute-done.4.refs_1_.first_ref
  24.5 0.9 %collective-permute-done.5.refs_2_.second_ref = bf16[64,256]{1,0:T(8,128)(2,1)S(1)} collective-permute-done((bf16[64,256]{1,0:T(8,128)(2,1)S(1)}, bf16[64,256]{1,0:T(8,128)(2,1)S(1)}, u32[]{:S(2)}, u32[]{:S(2)}) %collective-permute-start.5) | collective-permute-done | bytes 32800 | tf_op jit(solution)/shard_map/ppermute | solution.py:367
  25.5 0.1 collective-permute-start.7
  25.6 1.6 %shard_map.100 = (bf16[4,64,512]{2,1,0:T(8,128)(2,1)}, f32[8,128]{1,0:T(8,128)S(1)}) custom-call(s32[1]{0:T(128)} %bitcast.core_ref, s32[32,256]{1,0:T(8,128)S(1)} %get-tuple-element.30.rows_ref, bf16[64,256]{1,0:T(8,128)(2,1)S(1)} %collective-permute-done.4.refs_1_.first_ref, bf16[64,256]{1,0:T(8,128)(2,1)S(1)} %collective-permute-done.5.refs_2_.second_ref, ...), custom_call_target="tpu_custom_call" | custom-call | flops 100663296 | bytes 1634308 | tf_op jit(solution)/shard_map/pallas_call | solution.py:344
  27.1 2.7 %collective-permute-done.7.other_ref = bf16[96,640]{1,0:T(8,128)(2,1)S(1)} collective-permute-done((bf16[96,640]{1,0:T(8,128)(2,1)S(1)}, bf16[96,640]{1,0:T(8,128)(2,1)S(1)}, u32[]{:S(2)}, u32[]{:S(2)}) %collective-permute-start.7) | collective-permute-done | bytes 122912 | tf_op jit(solution)/shard_map/ppermute | solution.py:439
  29.9 1.3 %collective-permute-start.8 = (bf16[96,640]{1,0:T(8,128)(2,1)S(1)}, bf16[96,640]{1,0:T(8,128)(2,1)S(1)}, u32[]{:S(2)}, u32[]{:S(2)}) collective-permute-start(bf16[96,640]{1,0:T(8,128)(2,1)S(1)} %shard_map.101.mine_ref), channel_id=1, source_target_pairs={{0,17},{1,4},{2,7},{3,18},{4,1},{5,20},{6,23},{7,2},{8,13},{9,24},... | collective-permute-start | bytes 368648 | tf_op jit(solution)/shard_map/ppermute | solution.py:439
  31.2 5.2 %collective-permute-done.8.other_ref = bf16[96,640]{1,0:T(8,128)(2,1)S(1)} collective-permute-done((bf16[96,640]{1,0:T(8,128)(2,1)S(1)}, bf16[96,640]{1,0:T(8,128)(2,1)S(1)}, u32[]{:S(2)}, u32[]{:S(2)}) %collective-permute-start.8) | collective-permute-done | bytes 122912 | tf_op jit(solution)/shard_map/ppermute | solution.py:439
  36.5 0.1 collective-permute-start.9
  36.6 1.5 %collective-permute-done.9.other_ref = f32[96,640]{1,0:T(8,128)S(1)} collective-permute-done((f32[96,640]{1,0:T(8,128)S(1)}, f32[96,640]{1,0:T(8,128)S(1)}, u32[]{:S(2)}, u32[]{:S(2)}) %collective-permute-start.9) | collective-permute-done | bytes 245792 | tf_op jit(solution)/shard_map/ppermute | solution.py:473
  38.1 1.2 %shard_map.103 = (f32[27,64,64]{2,1,0:T(8,128)}, f32[1,64]{1,0:T(1,128)}) custom-call(s32[1]{0:T(128)} %bitcast.8.own_ref, f32[96,640]{1,0:T(8,128)S(1)} %shard_map.102.mine_ref, f32[96,640]{1,0:T(8,128)S(1)} %collective-permute-done.9.other_ref), custom_call_target="tpu_custom_call" | custom-call | bytes 934148 | tf_op jit(solution)/shard_map/pallas_call | solution.py:344
  (9 shorter events, 0.2 us)
Async XLA Ops:
  1.9 5.4 %collective-permute-start = (bf16[64,256]{1,0:T(8,128)(2,1)S(1)}, bf16[64,256]{1,0:T(8,128)(2,1)S(1)}, u32[]{:S(2)}, u32[]{:S(2)}) collective-permute-start(bf16[64,256]{1,0:T(8,128)(2,1)S(1)} %get-tuple-element.31), channel_id=1, source_target_pairs={{0,4},{1,0},{2,6},{3,2},{4,8},{5,1},{6,10},{7,3},{8,12},{9,5},{10,... | collective-permute-start | bytes 98312 | tf_op jit(solution)/shard_map/ppermute | solution.py:367
  4.9 3.9 %collective-permute-start.1 = (bf16[64,256]{1,0:T(8,128)(2,1)S(1)}, bf16[64,256]{1,0:T(8,128)(2,1)S(1)}, u32[]{:S(2)}, u32[]{:S(2)}) collective-permute-start(bf16[64,256]{1,0:T(8,128)(2,1)S(1)} %get-tuple-element.32), channel_id=1, source_target_pairs={{4,0},{0,1},{6,2},{2,3},{8,4},{1,5},{10,6},{3,7},{12,8},{5,9},{14,... | collective-permute-start | bytes 98312 | tf_op jit(solution)/shard_map/ppermute | solution.py:367
  10.8 1.4 %collective-permute-start.2 = (bf16[96,640]{1,0:T(8,128)(2,1)S(1)}, bf16[96,640]{1,0:T(8,128)(2,1)S(1)}, u32[]{:S(2)}, u32[]{:S(2)}) collective-permute-start(bf16[96,640]{1,0:T(8,128)(2,1)S(1)} %dynamic-slice_convert_fusion), channel_id=1, source_target_pairs={{0,1},{1,0},{2,3},{3,2},{4,5},{5,4},{6,7},{7,6},{8,9},{9,8},{10,11... | collective-permute-start | bytes 368648 | tf_op jit(solution)/shard_map/ppermute | solution.py:426
  12.3 4.4 %collective-permute-start.3 = (bf16[96,640]{1,0:T(8,128)(2,1)S(1)}, bf16[96,640]{1,0:T(8,128)(2,1)S(1)}, u32[]{:S(2)}, u32[]{:S(2)}) collective-permute-start(bf16[96,640]{1,0:T(8,128)(2,1)S(1)} %get-tuple-element.46.mine_ref), channel_id=1, source_target_pairs={{0,3},{1,8},{2,11},{3,0},{4,13},{5,6},{6,5},{7,14},{8,1},{9,10},{1... | collective-permute-start | bytes 368648 | tf_op jit(solution)/shard_map/ppermute | solution.py:439
  16.7 8.8 %collective-permute-start.6 = (bf16[96,640]{1,0:T(8,128)(2,1)S(1)}, bf16[96,640]{1,0:T(8,128)(2,1)S(1)}, u32[]{:S(2)}, u32[]{:S(2)}) collective-permute-start(bf16[96,640]{1,0:T(8,128)(2,1)S(1)} %shard_map.97.after_ref.mine_ref), channel_id=1, source_target_pairs={{0,5},{1,16},{2,19},{3,6},{4,21},{5,0},{6,3},{7,22},{8,25},{9,12},... | collective-permute-start | bytes 368648 | tf_op jit(solution)/shard_map/ppermute | solution.py:439
  18.9 5.6 %collective-permute-start.4 = (bf16[64,256]{1,0:T(8,128)(2,1)S(1)}, bf16[64,256]{1,0:T(8,128)(2,1)S(1)}, u32[]{:S(2)}, u32[]{:S(2)}) collective-permute-start(bf16[64,256]{1,0:T(8,128)(2,1)S(1)} %get-tuple-element.48), channel_id=1, source_target_pairs={{0,4},{1,0},{2,6},{3,2},{4,8},{5,1},{6,10},{7,3},{8,12},{9,5},{10,... | collective-permute-start | bytes 98312 | tf_op jit(solution)/shard_map/ppermute | solution.py:367
  21.5 3.9 %collective-permute-start.5 = (bf16[64,256]{1,0:T(8,128)(2,1)S(1)}, bf16[64,256]{1,0:T(8,128)(2,1)S(1)}, u32[]{:S(2)}, u32[]{:S(2)}) collective-permute-start(bf16[64,256]{1,0:T(8,128)(2,1)S(1)} %get-tuple-element.49), channel_id=1, source_target_pairs={{4,0},{0,1},{6,2},{2,3},{8,4},{1,5},{10,6},{3,7},{12,8},{5,9},{14,... | collective-permute-start | bytes 98312 | tf_op jit(solution)/shard_map/ppermute | solution.py:367
  25.5 4.4 %collective-permute-start.7 = (bf16[96,640]{1,0:T(8,128)(2,1)S(1)}, bf16[96,640]{1,0:T(8,128)(2,1)S(1)}, u32[]{:S(2)}, u32[]{:S(2)}) collective-permute-start(bf16[96,640]{1,0:T(8,128)(2,1)S(1)} %shard_map.99.after_ref.mine_ref), channel_id=1, source_target_pairs={{0,9},{1,2},{2,1},{3,10},{4,7},{5,12},{6,15},{7,4},{8,11},{9,0},{1... | collective-permute-start | bytes 368648 | tf_op jit(solution)/shard_map/ppermute | solution.py:439
  29.9 6.6 %collective-permute-start.8 = (bf16[96,640]{1,0:T(8,128)(2,1)S(1)}, bf16[96,640]{1,0:T(8,128)(2,1)S(1)}, u32[]{:S(2)}, u32[]{:S(2)}) collective-permute-start(bf16[96,640]{1,0:T(8,128)(2,1)S(1)} %shard_map.101.mine_ref), channel_id=1, source_target_pairs={{0,17},{1,4},{2,7},{3,18},{4,1},{5,20},{6,23},{7,2},{8,13},{9,24},... | collective-permute-start | bytes 368648 | tf_op jit(solution)/shard_map/ppermute | solution.py:439
  36.5 1.6 %collective-permute-start.9 = (f32[96,640]{1,0:T(8,128)S(1)}, f32[96,640]{1,0:T(8,128)S(1)}, u32[]{:S(2)}, u32[]{:S(2)}) collective-permute-start(f32[96,640]{1,0:T(8,128)S(1)} %shard_map.102.mine_ref), channel_id=1, source_target_pairs={{0,1},{1,0},{2,3},{3,2},{4,5},{5,4},{6,7},{7,6},{8,9},{9,8},{10,11... | collective-permute-start | bytes 737288 | tf_op jit(solution)/shard_map/ppermute | solution.py:473

commit v5 on v4

--- a/solution.py
+++ b/solution.py
@@ -215,8 +215,8 @@
 
 
 def outer_kernel(
-    core_ref, rows_ref, first_ref, second_ref, moved_ref, pre_ref, cot2_ref, occ2_ref, weight_ref,
-    result_ref, grad_ref, terms_ref, padded_ref,
+    core_ref, own_ref, rows_ref, first_ref, second_ref, moved_ref, pre_ref, cot2_ref, occ2_ref,
+    weight_ref, result_ref, grad_ref, mine_ref, theirs_ref, padded_ref, terms_ref,
 ):
     count, channels, lanes = pre_ref.shape
     bricks = lanes // PLANE
@@ -252,16 +252,40 @@
     spare = terms_ref.shape[1] - width
     terms_ref[channels:, width:] = jnp.zeros((2 * channels, spare), F32)
     terms_ref[0:channels, width:] = jnp.sum(bias, axis=1, keepdims=True) * spread(spare)
+    half = mine_ref.shape[0]
+    own = own_ref[0]
+    mine_ref[...] = terms_ref[pl.ds(own * half, half), :]
+    theirs_ref[0:half, :] = terms_ref[pl.ds((1 - own) * half, half), :].astype(BF)
+    even = core_ref[0] == 0
+    part = channels // 2
+    low, high = grad_ref[0].astype(F32), grad_ref[count - 1].astype(F32)
+    face = jnp.where(even, low, high).astype(BF)
+    theirs_ref[half:, 0:lanes] = face[:part]
+    theirs_ref[half:, lanes : 2 * lanes] = face[part:]
+    theirs_ref[half:, 2 * lanes :] = jnp.zeros((part, theirs_ref.shape[1] - 2 * lanes), BF)
 
 
 def spread(count):
     return 1.0 + lax.broadcasted_iota(jnp.int32, (1, count), 1).astype(F32) * (1.0 / count)
 
 
-def first_sum_kernel(core_ref, mine_ref, other_ref, grad_ref, out_ref, first_ref, second_ref):
-    out_ref[...] = (mine_ref[...] + other_ref[...].astype(F32)).astype(BF)
-    last = grad_ref.shape[0] - 1
-    store_faces(core_ref, grad_ref[0], grad_ref[last], first_ref, second_ref)
+def first_sum_kernel(core_ref, mine_ref, other_ref, grad_ref, out_ref, faces_ref):
+    half = mine_ref.shape[0]
+    out_ref[...] = (mine_ref[...] + other_ref[0:half, :].astype(F32)).astype(BF)
+    count, channels, lanes = grad_ref.shape
+    part = channels // 2
+    even = core_ref[0] == 0
+    low, high = grad_ref[0].astype(F32), grad_ref[count - 1].astype(F32)
+    faces_ref[0:channels, :] = jnp.where(even, high, low).astype(BF)
+    faces_ref[channels : channels + part, :] = other_ref[half:, 0:lanes]
+    faces_ref[channels + part :, :] = other_ref[half:, lanes : 2 * lanes]
+
+
+def faces_sum_kernel(mine_ref, other_ref, faces_ref, out_ref, own_ref, sibling_ref):
+    channels = own_ref.shape[0]
+    out_ref[...] = (mine_ref[...].astype(F32) + other_ref[...].astype(F32)).astype(BF)
+    own_ref[...] = faces_ref[0:channels, :]
+    sibling_ref[...] = faces_ref[channels:, :]
 
 
 def sum_kernel(mine_ref, other_ref, *refs):
@@ -352,7 +376,7 @@
     )(*[pltpu.with_memory_space_constraint(x, pltpu.HBM) if s is HBM else x for s, x in ins])
 
 
-def exchange_faces(first, second):
+def face_pairs():
     spaces, reps = lax.axis_size("space"), lax.axis_size("rep")
     pairs = []
     for space in range(spaces):
@@ -362,9 +386,7 @@
             if not 0 <= there < spaces:
                 there, to = space, rep ^ 1
             pairs.append((space * reps + rep, there * reps + to))
-    back = [(j, i) for i, j in pairs]
-    axes = ("space", "rep")
-    return lax.ppermute(first, axes, pairs), lax.ppermute(second, axes, back)
+    return pairs
 
 
 def on_device(feats, cotangent, weight, bias, neighbours, occupancy):
@@ -384,7 +406,10 @@
         [(SMEM, cores), (HBM, x), (HBM, occ), (HBM, near), (HBM, cot), (HBM, weight), (HBM, bias[None])],
         [pltpu.SMEM(near.shape, jnp.int32), pltpu.SemaphoreType.DMA((6,))],
     )
-    first, second = exchange_faces(first, second)
+    axes = ("space", "rep")
+    pairs = face_pairs()
+    first = lax.ppermute(first, axes, pairs)
+    second = lax.ppermute(second, axes, [(j, i) for i, j in pairs])
     moved, pre, cot2, occ2, ahead = call(
         inner_kernel,
         [
@@ -401,46 +426,52 @@
         ],
         flops=2 * 27 * channels * channels * bricks * voxels,
     )
-    result2, grad, terms = call(
+    devices = lax.axis_size("space") * lax.axis_size("rep")
+    me = lax.axis_index("space") * lax.axis_size("rep") + lax.axis_index("rep")
+    own = (lax.population_count(me.astype(jnp.int32)) & 1)[None]
+    half, columns = 3 * channels // 2, width + 64
+    result2, grad, mine, theirs = call(
         outer_kernel,
         [
             ((count, channels, lanes), BF),
             ((count, channels, lanes), BF),
-            ((3 * channels, width + 64), F32),
+            ((half, columns), F32),
+            ((half + channels // 2, columns), BF),
         ],
         [
-            (SMEM, cores), (VMEM, rows), (VMEM, first), (VMEM, second), (VMEM, moved), (VMEM, pre),
-            (VMEM, cot2), (VMEM, occ2), (VMEM, ahead),
+            (SMEM, cores), (SMEM, own), (VMEM, rows), (VMEM, first), (VMEM, second), (VMEM, moved),
+            (VMEM, pre), (VMEM, cot2), (VMEM, occ2), (VMEM, ahead),
         ],
-        [pltpu.VMEM((channels * (count + 2), lanes), BF)],
+        [
+            pltpu.VMEM((channels * (count + 2), lanes), BF),
+            pltpu.VMEM((3 * channels, columns), F32),
+        ],
         flops=2 * 27 * channels * channels * bricks * voxels,
     )
-    axes = ("space", "rep")
-    devices = lax.axis_size("space") * lax.axis_size("rep")
-    half = 3 * channels // 2
     partner = [(i, i ^ 1) for i in range(devices)]
-    me = lax.axis_index("space") * lax.axis_size("rep") + lax.axis_index("rep")
-    own = lax.population_count(me.astype(jnp.int32)) & 1
-    theirs = lax.dynamic_slice_in_dim(terms, (1 - own) * half, half, 0).astype(BF)
-    mine = lax.dynamic_slice_in_dim(terms, own * half, half, 0)
     other = lax.ppermute(theirs, axes, partner)
-    sent = ((half, terms.shape[1]), BF)
-    mine, first, second = call(
+    sent = ((half, columns), BF)
+    mine, faces = call(
         first_sum_kernel,
-        [sent, plane, plane],
+        [sent, ((2 * channels, lanes), BF)],
         [(SMEM, cores), (VMEM, mine), (VMEM, other), (VMEM, grad)],
     )
     bits = [1 << i for i in range(1, (devices).bit_length() - 1)]
     turn = len(bits) // 2
-    total = in_grad = result = None
     rounds = list(zip(bits, bits[turn:] + bits[:turn]))
     for i, steps in enumerate(rounds):
-        pairs = [(j, j ^ 1 ^ steps[j.bit_count() % 2]) for j in range(devices)]
-        other = lax.ppermute(mine, axes, pairs)
+        joined = [(j, j ^ 1 ^ steps[j.bit_count() % 2]) for j in range(devices)]
+        other = lax.ppermute(mine, axes, joined)
         held = []
         if i == 0:
-            first, second = exchange_faces(first, second)
+            faces = lax.ppermute(faces, axes, pairs)
         if i == 1:
+            mine, first, second = call(
+                faces_sum_kernel, [sent, plane, plane], [(VMEM, mine), (VMEM, other), (VMEM, faces)]
+            )
+            continue
+        if i == 2:
+            second = lax.ppermute(second, axes, partner)
             result, total, back = call(
                 back_inner_kernel,
                 [
@@ -452,14 +483,14 @@
                 [pltpu.VMEM((count, width, lanes), BF)],
                 flops=2 * 27 * channels * channels * bricks * voxels,
             )
-            held = [total, first, second]
-        if i == 2:
+            held = [total, second]
+        if i == 3:
             in_grad, done = call(
                 back_outer_kernel,
                 [((bricks, channels, voxels), BF), ((8, 128), F32)],
                 [
-                    (SMEM, cores), (VMEM, rows), (VMEM, first), (VMEM, second), (VMEM, total), (VMEM, cot),
-                    (VMEM, occ), (VMEM, back), (ANY, mine),
+                    (SMEM, cores), (VMEM, rows), (VMEM, first), (VMEM, second), (VMEM, total),
+                    (VMEM, cot), (VMEM, occ), (VMEM, back), (ANY, mine),
                 ],
                 flops=2 * 6 * channels * channels * bricks * voxels,
             )
@@ -477,8 +508,8 @@
     weight_grad, bias_grad = call(
         functools.partial(final_kernel, normaliser),
         [(weight.shape, F32), ((1, channels), F32)],
-        [(SMEM, own[None]), (VMEM, mine), (VMEM, other)],
-        [pltpu.VMEM(terms.shape, F32)],
+        [(SMEM, own), (VMEM, mine), (VMEM, other)],
+        [pltpu.VMEM((3 * channels, columns), F32)],
     )
     return result[None], in_grad[None], weight_grad, bias_grad[0]
 

time: 39.5 us -> 37.9 us (0.959)
  the two profiles are of different devices: /device:TPU:0 before, /device:TPU:5 now
where the time goes in v5:
time: 37.9 us; the launch traced here: 37.7 us
  starting transfers between devices  13 us (34%)
  waiting for transfers between devices  12.3 us (32%)
  Pallas kernels  11.6 us (31%)
  between operations  0.72 us (2%)
    pallas_call x11, Pallas kernels, call(): pl.pallas_call(body, out_shape=shapes, in_specs=[spec for spec, _ in ins]...  11.6 us
    ppermute x4, starting transfers between devices, on_device(): other = lax.ppermute(mine, axes, joined)  8.83 us
    ppermute x4, waiting for transfers between devices, on_device(): other = lax.ppermute(mine, axes, joined)  6.17 us
    ppermute x1, waiting for transfers between devices, on_device(): faces = lax.ppermute(faces, axes, pairs)  3.61 us
    ppermute x1, starting transfers between devices, on_device(): other = lax.ppermute(theirs, axes, partner)  2.23 us
    ppermute x1, waiting for transfers between devices, on_device(): other = lax.ppermute(mine, axes, partner)  1.5 us
    ppermute x1, waiting for transfers between devices, on_device(): other = lax.ppermute(theirs, axes, partner)  1.03 us
    ppermute x1, starting transfers between devices, on_device(): second = lax.ppermute(second, axes, [(j, i) for i, j in pairs])  0.79 us
  transfers between devices with their start and end apart: 10, of which 5 were waited for; matrix products, arithmetic and copies ran while one was open for 0% of the time, Pallas kernels for 19%

profile of v5, /device:TPU:5, one launch (start us, length us, event | category | flops | bytes accessed | tf_op | source)
XLA Modules:
  0.0 37.7 jit_solution(3888376526225770845)
XLA Ops:
  0.6 1.2 %shard_map.93 = (bf16[64,256]{1,0:T(8,128)(2,1)S(1)}, bf16[64,256]{1,0:T(8,128)(2,1)S(1)}, s32[32,256]{1,0:T(8,128)S(1)}, bf16[4,64,512]{2,1,0:T(8,128)(2,1)S(1)...) custom-call(s32[1]{0:T(128)} %bitcast.core_ref, ...), custom_call_target="tpu_custom_call" | custom-call | bytes 1606564 | tf_op jit(solution)/shard_map/pallas_call | solution.py:368
  1.9 0.7 %collective-permute-start = (bf16[64,256]{1,0:T(8,128)(2,1)S(1)}, bf16[64,256]{1,0:T(8,128)(2,1)S(1)}, u32[]{:S(2)}, u32[]{:S(2)}) collective-permute-start(bf16[64,256]{1,0:T(8,128)(2,1)S(1)} %get-tuple-element.34), channel_id=1, source_target_pairs={{0,4},{1,0},{2,6},{3,2},{4,8},{5,1},{6,10},{7,3},{8,12},{9,5},{10,... | collective-permute-start | bytes 98312 | tf_op jit(solution)/shard_map/ppermute | solution.py:411
  2.6 0.8 %collective-permute-start.1 = (bf16[64,256]{1,0:T(8,128)(2,1)S(1)}, bf16[64,256]{1,0:T(8,128)(2,1)S(1)}, u32[]{:S(2)}, u32[]{:S(2)}) collective-permute-start(bf16[64,256]{1,0:T(8,128)(2,1)S(1)} %get-tuple-element.35), channel_id=1, source_target_pairs={{4,0},{0,1},{6,2},{2,3},{8,4},{1,5},{10,6},{3,7},{12,8},{5,9},{14,... | collective-permute-start | bytes 98312 | tf_op jit(solution)/shard_map/ppermute | solution.py:412
  3.4 2.4 %shard_map.94 = (bf16[8,576,256]{2,1,0:T(8,128)(2,1)S(1)}, f32[8,64,256]{2,1,0:T(8,128)S(1)}, bf16[8,64,256]{2,1,0:T(8,128)(2,1)S(1)}, f32[8,8,256]{2,1,0:T(8,128)S(1)}, bf16[192,576]{1,0:T(8,128)(2,1)S(1)}) custom-call(s32[32,256]{1,0:T(8,128)S(1)} %get-tuple-element.33.rows_ref, bf16[4,64,512]{2,1,0:T(8,128)(2,1)S(1)} %get-tuple-element.36.feats_ref, ...), custom_call_target="tpu_custom_call" | custom-call | flops 452984832 | bytes 4219136 | tf_op jit(solution)/shard_map/pallas_call | solution.py:368
  5.8 0.0 collective-permute-done.first_ref
  5.9 0.0 collective-permute-done.1.second_ref
  5.9 2.0 %shard_map.95 = (bf16[8,64,256]{2,1,0:T(8,128)(2,1)S(1)}, bf16[8,64,256]{2,1,0:T(8,128)(2,1)S(1)}, f32[96,640]{1,0:T(8,128)S(1)}, bf16[128,640]{1,0:T(8,128)(2,1)S(1)}) custom-call(s32[1]{0:T(128)} %bitcast.core_ref, s32[1]{0:T(128)} %bitcast.6.own_ref, s32[32,256]{1,0:T(8,128)S(1)} %get-tuple-element.33.rows_ref, ...), custom_call_target="tpu_custom_call" | custom-call | flops 452984832 | bytes 4464648 | tf_op jit(solution)/shard_map/pallas_call | solution.py:368
  7.9 2.2 %collective-permute-start.2 = (bf16[128,640]{1,0:T(8,128)(2,1)S(1)}, bf16[128,640]{1,0:T(8,128)(2,1)S(1)}, u32[]{:S(2)}, u32[]{:S(2)}) collective-permute-start(bf16[128,640]{1,0:T(8,128)(2,1)S(1)} %get-tuple-element.49), channel_id=1, source_target_pairs={{0,1},{1,0},{2,3},{3,2},{4,5},{5,4},{6,7},{7,6},{8,9},{9,8},{10,11... | collective-permute-start | bytes 491528 | tf_op jit(solution)/shard_map/ppermute | solution.py:452
  10.1 1.0 %collective-permute-done.2.other_ref = bf16[128,640]{1,0:T(8,128)(2,1)S(1)} collective-permute-done((bf16[128,640]{1,0:T(8,128)(2,1)S(1)}, bf16[128,640]{1,0:T(8,128)(2,1)S(1)}, u32[]{:S(2)}, u32[]{:S(2)}) %collective-permute-start.2) | collective-permute-done | bytes 163872 | tf_op jit(solution)/shard_map/ppermute | solution.py:452
  11.2 0.5 %collective-permute-start.3 = (bf16[96,640]{1,0:T(8,128)(2,1)S(1)}, bf16[96,640]{1,0:T(8,128)(2,1)S(1)}, u32[]{:S(2)}, u32[]{:S(2)}) collective-permute-start(bf16[96,640]{1,0:T(8,128)(2,1)S(1)} %get-tuple-element.50.mine_ref), channel_id=1, source_target_pairs={{0,3},{1,8},{2,11},{3,0},{4,13},{5,6},{6,5},{7,14},{8,1},{9,10},{1... | collective-permute-start | bytes 368648 | tf_op jit(solution)/shard_map/ppermute | solution.py:464
  11.7 3.8 %collective-permute-done.3.other_ref = bf16[96,640]{1,0:T(8,128)(2,1)S(1)} collective-permute-done((bf16[96,640]{1,0:T(8,128)(2,1)S(1)}, bf16[96,640]{1,0:T(8,128)(2,1)S(1)}, u32[]{:S(2)}, u32[]{:S(2)}) %collective-permute-start.3) | collective-permute-done | bytes 122912 | tf_op jit(solution)/shard_map/ppermute | solution.py:464
  15.6 2.5 %collective-permute-start.4 = (bf16[96,640]{1,0:T(8,128)(2,1)S(1)}, bf16[96,640]{1,0:T(8,128)(2,1)S(1)}, u32[]{:S(2)}, u32[]{:S(2)}) collective-permute-start(bf16[96,640]{1,0:T(8,128)(2,1)S(1)} %shard_map.97.mine_ref), channel_id=1, source_target_pairs={{0,5},{1,16},{2,19},{3,6},{4,21},{5,0},{6,3},{7,22},{8,25},{9,12},... | collective-permute-start | bytes 368648 | tf_op jit(solution)/shard_map/ppermute | solution.py:464
  18.1 0.4 collective-permute-start.5
  18.4 3.6 %collective-permute-done.5.faces_ref = bf16[128,256]{1,0:T(8,128)(2,1)S(1)} collective-permute-done((bf16[128,256]{1,0:T(8,128)(2,1)S(1)}, bf16[128,256]{1,0:T(8,128)(2,1)S(1)}, u32[]{:S(2)}, u32[]{:S(2)}) %collective-permute-start.5) | collective-permute-done | bytes 65568 | tf_op jit(solution)/shard_map/ppermute | solution.py:467
  22.0 0.0 collective-permute-done.4.other_ref
  22.1 3.1 %collective-permute-start.7 = (bf16[96,640]{1,0:T(8,128)(2,1)S(1)}, bf16[96,640]{1,0:T(8,128)(2,1)S(1)}, u32[]{:S(2)}, u32[]{:S(2)}) collective-permute-start(bf16[96,640]{1,0:T(8,128)(2,1)S(1)} %get-tuple-element.52.after_ref.mine_ref), channel_id=1, source_target_pairs={{0,9},{1,2},{2,1},{3,10},{4,7},{5,12},{6,15},{7,4},{8,11},{9,0},{1... | collective-permute-start | bytes 368648 | tf_op jit(solution)/shard_map/ppermute | solution.py:464
  25.2 0.0 collective-permute-start.6
  25.2 3.0 %shard_map.99 = (bf16[4,64,512]{2,1,0:T(8,128)(2,1)}, f32[640,256]{1,0:T(8,128)S(1)}, bf16[192,576]{1,0:T(8,128)(2,1)S(1)}) custom-call(s32[32,256]{1,0:T(8,128)S(1)} %get-tuple-element.33.rows_ref, bf16[8,64,256]{2,1,0:T(8,128)(2,1)S(1)} %get-tuple-element.46.grad_ref, bf16[8,64,256]{2,1,0:T(8,128)(2,1)S(1)} %get-tuple-element.47.result2_ref, ...), custom_call_target="tpu_custom_call" | custom-call | flops 452984832 | bytes 2039808 | tf_op jit(solution)/shard_map/pallas_call | solution.py:368
  28.3 2.7 %collective-permute-start.8 = (bf16[96,640]{1,0:T(8,128)(2,1)S(1)}, bf16[96,640]{1,0:T(8,128)(2,1)S(1)}, u32[]{:S(2)}, u32[]{:S(2)}) collective-permute-start(bf16[96,640]{1,0:T(8,128)(2,1)S(1)} %shard_map.100.after_ref.mine_ref), channel_id=1, source_target_pairs={{0,17},{1,4},{2,7},{3,18},{4,1},{5,20},{6,23},{7,2},{8,13},{9,24},... | collective-permute-start | bytes 368648 | tf_op jit(solution)/shard_map/ppermute | solution.py:464
  31.0 1.6 %shard_map.101 = (bf16[4,64,512]{2,1,0:T(8,128)(2,1)}, f32[8,128]{1,0:T(8,128)S(1)}) custom-call(s32[1]{0:T(128)} %bitcast.core_ref, s32[32,256]{1,0:T(8,128)S(1)} %get-tuple-element.33.rows_ref, bf16[64,256]{1,0:T(8,128)(2,1)S(1)} %get-tuple-element.54.first_ref, bf16[64,256]{1,0:T(8,128)(2,1)S(1)} %collective-permute-done.6.refs_1_.second_ref, ...), custom_call_target="tpu_custom_call" | custom-call | flops 100663296 | bytes 1634308 | tf_op jit(solution)/shard_map/pallas_call | solution.py:368
  32.5 2.3 %collective-permute-done.8.other_ref = bf16[96,640]{1,0:T(8,128)(2,1)S(1)} collective-permute-done((bf16[96,640]{1,0:T(8,128)(2,1)S(1)}, bf16[96,640]{1,0:T(8,128)(2,1)S(1)}, u32[]{:S(2)}, u32[]{:S(2)}) %collective-permute-start.8) | collective-permute-done | bytes 122912 | tf_op jit(solution)/shard_map/ppermute | solution.py:464
  34.9 0.1 collective-permute-start.9
  35.0 1.5 %collective-permute-done.9.other_ref = f32[96,640]{1,0:T(8,128)S(1)} collective-permute-done((f32[96,640]{1,0:T(8,128)S(1)}, f32[96,640]{1,0:T(8,128)S(1)}, u32[]{:S(2)}, u32[]{:S(2)}) %collective-permute-start.9) | collective-permute-done | bytes 245792 | tf_op jit(solution)/shard_map/ppermute | solution.py:504
  36.5 1.2 %shard_map.103 = (f32[27,64,64]{2,1,0:T(8,128)}, f32[1,64]{1,0:T(1,128)}) custom-call(s32[1]{0:T(128)} %bitcast.6.own_ref, f32[96,640]{1,0:T(8,128)S(1)} %shard_map.102.mine_ref, f32[96,640]{1,0:T(8,128)S(1)} %collective-permute-done.9.other_ref), custom_call_target="tpu_custom_call" | custom-call | bytes 934148 | tf_op jit(solution)/shard_map/pallas_call | solution.py:368
  (7 shorter events, 0.2 us)
Async XLA Ops:
  1.9 4.0 %collective-permute-start = (bf16[64,256]{1,0:T(8,128)(2,1)S(1)}, bf16[64,256]{1,0:T(8,128)(2,1)S(1)}, u32[]{:S(2)}, u32[]{:S(2)}) collective-permute-start(bf16[64,256]{1,0:T(8,128)(2,1)S(1)} %get-tuple-element.34), channel_id=1, source_target_pairs={{0,4},{1,0},{2,6},{3,2},{4,8},{5,1},{6,10},{7,3},{8,12},{9,5},{10,... | collective-permute-start | bytes 98312 | tf_op jit(solution)/shard_map/ppermute | solution.py:411
  2.6 3.2 %collective-permute-start.1 = (bf16[64,256]{1,0:T(8,128)(2,1)S(1)}, bf16[64,256]{1,0:T(8,128)(2,1)S(1)}, u32[]{:S(2)}, u32[]{:S(2)}) collective-permute-start(bf16[64,256]{1,0:T(8,128)(2,1)S(1)} %get-tuple-element.35), channel_id=1, source_target_pairs={{4,0},{0,1},{6,2},{2,3},{8,4},{1,5},{10,6},{3,7},{12,8},{5,9},{14,... | collective-permute-start | bytes 98312 | tf_op jit(solution)/shard_map/ppermute | solution.py:412
  7.9 3.3 %collective-permute-start.2 = (bf16[128,640]{1,0:T(8,128)(2,1)S(1)}, bf16[128,640]{1,0:T(8,128)(2,1)S(1)}, u32[]{:S(2)}, u32[]{:S(2)}) collective-permute-start(bf16[128,640]{1,0:T(8,128)(2,1)S(1)} %get-tuple-element.49), channel_id=1, source_target_pairs={{0,1},{1,0},{2,3},{3,2},{4,5},{5,4},{6,7},{7,6},{8,9},{9,8},{10,11... | collective-permute-start | bytes 491528 | tf_op jit(solution)/shard_map/ppermute | solution.py:452
  11.2 4.4 %collective-permute-start.3 = (bf16[96,640]{1,0:T(8,128)(2,1)S(1)}, bf16[96,640]{1,0:T(8,128)(2,1)S(1)}, u32[]{:S(2)}, u32[]{:S(2)}) collective-permute-start(bf16[96,640]{1,0:T(8,128)(2,1)S(1)} %get-tuple-element.50.mine_ref), channel_id=1, source_target_pairs={{0,3},{1,8},{2,11},{3,0},{4,13},{5,6},{6,5},{7,14},{8,1},{9,10},{1... | collective-permute-start | bytes 368648 | tf_op jit(solution)/shard_map/ppermute | solution.py:464
  15.6 6.4 %collective-permute-start.4 = (bf16[96,640]{1,0:T(8,128)(2,1)S(1)}, bf16[96,640]{1,0:T(8,128)(2,1)S(1)}, u32[]{:S(2)}, u32[]{:S(2)}) collective-permute-start(bf16[96,640]{1,0:T(8,128)(2,1)S(1)} %shard_map.97.mine_ref), channel_id=1, source_target_pairs={{0,5},{1,16},{2,19},{3,6},{4,21},{5,0},{6,3},{7,22},{8,25},{9,12},... | collective-permute-start | bytes 368648 | tf_op jit(solution)/shard_map/ppermute | solution.py:464
  18.1 4.0 %collective-permute-start.5 = (bf16[128,256]{1,0:T(8,128)(2,1)S(1)}, bf16[128,256]{1,0:T(8,128)(2,1)S(1)}, u32[]{:S(2)}, u32[]{:S(2)}) collective-permute-start(bf16[128,256]{1,0:T(8,128)(2,1)S(1)} %get-tuple-element.51), channel_id=1, source_target_pairs={{0,4},{1,0},{2,6},{3,2},{4,8},{5,1},{6,10},{7,3},{8,12},{9,5},{10,... | collective-permute-start | bytes 196616 | tf_op jit(solution)/shard_map/ppermute | solution.py:467
  22.1 6.2 %collective-permute-start.7 = (bf16[96,640]{1,0:T(8,128)(2,1)S(1)}, bf16[96,640]{1,0:T(8,128)(2,1)S(1)}, u32[]{:S(2)}, u32[]{:S(2)}) collective-permute-start(bf16[96,640]{1,0:T(8,128)(2,1)S(1)} %get-tuple-element.52.after_ref.mine_ref), channel_id=1, source_target_pairs={{0,9},{1,2},{2,1},{3,10},{4,7},{5,12},{6,15},{7,4},{8,11},{9,0},{1... | collective-permute-start | bytes 368648 | tf_op jit(solution)/shard_map/ppermute | solution.py:464
  25.2 3.0 %collective-permute-start.6 = (bf16[64,256]{1,0:T(8,128)(2,1)S(1)}, bf16[64,256]{1,0:T(8,128)(2,1)S(1)}, u32[]{:S(2)}, u32[]{:S(2)}) collective-permute-start(bf16[64,256]{1,0:T(8,128)(2,1)S(1)} %get-tuple-element.55), channel_id=1, source_target_pairs={{0,1},{1,0},{2,3},{3,2},{4,5},{5,4},{6,7},{7,6},{8,9},{9,8},{10,11... | collective-permute-start | bytes 98312 | tf_op jit(solution)/shard_map/ppermute | solution.py:474
  28.3 6.6 %collective-permute-start.8 = (bf16[96,640]{1,0:T(8,128)(2,1)S(1)}, bf16[96,640]{1,0:T(8,128)(2,1)S(1)}, u32[]{:S(2)}, u32[]{:S(2)}) collective-permute-start(bf16[96,640]{1,0:T(8,128)(2,1)S(1)} %shard_map.100.after_ref.mine_ref), channel_id=1, source_target_pairs={{0,17},{1,4},{2,7},{3,18},{4,1},{5,20},{6,23},{7,2},{8,13},{9,24},... | collective-permute-start | bytes 368648 | tf_op jit(solution)/shard_map/ppermute | solution.py:464
  34.9 1.6 %collective-permute-start.9 = (f32[96,640]{1,0:T(8,128)S(1)}, f32[96,640]{1,0:T(8,128)S(1)}, u32[]{:S(2)}, u32[]{:S(2)}) collective-permute-start(f32[96,640]{1,0:T(8,128)S(1)} %shard_map.102.mine_ref), channel_id=1, source_target_pairs={{0,1},{1,0},{2,3},{3,2},{4,5},{5,4},{6,7},{7,6},{8,9},{9,8},{10,11... | collective-permute-start | bytes 737288 | tf_op jit(solution)/shard_map/ppermute | solution.py:504

commit v6 on v5

--- a/solution.py
+++ b/solution.py
@@ -115,14 +115,10 @@
 
 
 def stage_kernel(
-    core_ref, feats_ref, occ_ref, near_ref, cot_ref, weight_ref, bias_ref,
-    first_ref, second_ref, rows_ref, x_ref, keep_ref, cot_out_ref, weight_out_ref, bias_out_ref,
+    core_ref, feats_ref, occ_ref, near_ref, first_ref, second_ref, rows_ref, x_ref, keep_ref,
     near_held_ref, sems,
 ):
-    pairs = (
-        (near_ref, near_held_ref), (occ_ref, keep_ref), (feats_ref, x_ref), (cot_ref, cot_out_ref),
-        (weight_ref, weight_out_ref), (bias_ref, bias_out_ref),
-    )
+    pairs = ((near_ref, near_held_ref), (occ_ref, keep_ref), (feats_ref, x_ref))
     copies = [pltpu.make_async_copy(a, b, sems.at[i]) for i, (a, b) in enumerate(pairs)]
     for copy in copies:
         copy.start()
@@ -138,8 +134,6 @@
         tiles = [x_ref[m, :, at].astype(F32) * keep[m : m + 1, at] for m in range(bricks)]
         faces.append(to_planes(tiles)[i].astype(BF))
     store_faces(core_ref, faces[0], faces[1], first_ref, second_ref)
-    for copy in copies[3:]:
-        copy.wait()
 
 
 def ahead_weights(weight_ref, ahead_ref):
@@ -182,10 +176,15 @@
 
 
 def inner_kernel(
-    rows_ref, feats_ref, cot_ref, occ_ref, weight_ref, bias_ref,
-    moved_ref, pre_ref, cot2_ref, occ2_ref, ahead_ref, planes_ref, total_ref,
+    rows_ref, feats_ref, occ_ref, cot_from_ref, weight_from_ref, bias_from_ref,
+    moved_ref, pre_ref, cot2_ref, occ2_ref, ahead_ref, cot_ref, weight_ref,
+    planes_ref, total_ref, bias_ref, sems,
 ):
     bricks, channels, voxels = feats_ref.shape
+    pairs = ((cot_from_ref, cot_ref), (weight_from_ref, weight_ref), (bias_from_ref, bias_ref))
+    copies = [pltpu.make_async_copy(a, b, sems.at[i]) for i, (a, b) in enumerate(pairs)]
+    for copy in copies:
+        copy.start()
     keep = occ_ref[...].astype(F32)
     for t in range(voxels // 128):
         at = slice(128 * t, 128 * t + 128)
@@ -193,13 +192,18 @@
         first, second = to_planes([feats_ref[m, :, at].astype(F32) * kept[m] for m in range(bricks)])
         planes_ref[2 * t] = first.astype(BF)
         planes_ref[2 * t + 1] = second.astype(BF)
-        first, second = to_planes([cot_ref[m, :, at].astype(F32) * kept[m] for m in range(bricks)])
-        cot2_ref[2 * t] = first.astype(BF)
-        cot2_ref[2 * t + 1] = second.astype(BF)
         first, second = to_planes([kept[m][:8] for m in range(bricks)])
         occ2_ref[2 * t] = first
         occ2_ref[2 * t + 1] = second
     shifted(planes_ref, moved_ref, rows_ref, bricks, channels)
+    for copy in copies:
+        copy.wait()
+    for t in range(voxels // 128):
+        at = slice(128 * t, 128 * t + 128)
+        kept = [jnp.broadcast_to(keep[m : m + 1, at], (channels, 128)) for m in range(bricks)]
+        first, second = to_planes([cot_ref[m, :, at].astype(F32) * kept[m] for m in range(bricks)])
+        cot2_ref[2 * t] = first.astype(BF)
+        cot2_ref[2 * t + 1] = second.astype(BF)
     ahead_weights(weight_ref, ahead_ref)
     count = planes_ref.shape[0]
     at = (channels, channels)
@@ -214,19 +218,41 @@
     pre_ref[...] = total_ref[channels : channels * (count + 1), :].reshape(pre_ref.shape)
 
 
+def half_terms(padded_ref, moved_ref, low_ref, high_ref, start, half):
+    count, channels = moved_ref.shape[0], padded_ref.shape[0] // (moved_ref.shape[0] + 4)
+
+    def rows(x):
+        return padded_ref[pl.ds(pl.multiple_of(channels * (x + 1) + start, 32), half), :]
+
+    terms = dot_t(rows(-1), low_ref[...])
+    for x in range(count):
+        terms = terms + dot_t(rows(x), moved_ref[x])
+    return terms + dot_t(rows(count), high_ref[...])
+
+
+def store_terms(terms, copies_ref, start, out_ref):
+    half, width = terms.shape
+    channels = copies_ref.shape[0]
+    out_ref[0:half, 0:width] = terms.astype(out_ref.dtype)
+    copies = jnp.where(start == 0, copies_ref[...], 0.0)
+    copies = jnp.concatenate([copies, jnp.zeros((half - channels, copies.shape[1]), F32)], axis=0)
+    out_ref[0:half, width:] = copies.astype(out_ref.dtype)
+
+
 def outer_kernel(
     core_ref, own_ref, rows_ref, first_ref, second_ref, moved_ref, pre_ref, cot2_ref, occ2_ref,
-    weight_ref, result_ref, grad_ref, mine_ref, theirs_ref, padded_ref, terms_ref,
+    weight_ref,
+    result_ref, grad_ref, theirs_ref, padded_ref, moved_low_ref, moved_high_ref, copies_ref,
 ):
     count, channels, lanes = pre_ref.shape
     bricks = lanes // PLANE
     low, high = load_faces(core_ref, first_ref, second_ref)
-    moved_low = shifted_face(low, rows_ref, -1, bricks)
-    moved_high = shifted_face(high, rows_ref, 1, bricks)
-    add_low = dot(weight_ref[2 * channels : 3 * channels, :], moved_low)
-    add_high = dot(weight_ref[0:channels, :], moved_high)
-    padded_ref[0:channels, :] = jnp.zeros((channels, lanes), BF)
-    padded_ref[channels * (count + 1) :, :] = jnp.zeros((channels, lanes), BF)
+    moved_low_ref[...] = shifted_face(low, rows_ref, -1, bricks)
+    moved_high_ref[...] = shifted_face(high, rows_ref, 1, bricks)
+    add_low = dot(weight_ref[2 * channels : 3 * channels, :], moved_low_ref[...])
+    add_high = dot(weight_ref[0:channels, :], moved_high_ref[...])
+    padded_ref[0 : 2 * channels, :] = jnp.zeros((2 * channels, lanes), BF)
+    padded_ref[channels * (count + 2) :, :] = jnp.zeros((2 * channels, lanes), BF)
     bias = jnp.zeros((channels, lanes), F32)
     for x in range(count):
         pre = pre_ref[x]
@@ -240,29 +266,27 @@
         result_ref[x] = (masked + keep * pre * sig).astype(BF)
         grad = (cot2_ref[x].astype(F32) * sig * (1.0 + pre * (1.0 - sig))).astype(BF)
         grad_ref[x] = grad
-        padded_ref[channels * (x + 1) : channels * (x + 2), :] = grad
+        padded_ref[channels * (x + 2) : channels * (x + 3), :] = grad
         bias = bias + grad.astype(F32)
-    terms = dot_t(padded_ref[0 : 3 * channels, :], moved_ref[0])
-    for x in range(1, count):
-        terms = terms + dot_t(padded_ref[channels * x : channels * (x + 3), :], moved_ref[x])
-    width = 9 * channels
-    terms_ref[:, 0:width] = terms
-    terms_ref[2 * channels : 3 * channels, 0:width] += dot_t(grad_ref[0], moved_low)
-    terms_ref[0:channels, 0:width] += dot_t(grad_ref[count - 1], moved_high)
-    spare = terms_ref.shape[1] - width
-    terms_ref[channels:, width:] = jnp.zeros((2 * channels, spare), F32)
-    terms_ref[0:channels, width:] = jnp.sum(bias, axis=1, keepdims=True) * spread(spare)
-    half = mine_ref.shape[0]
-    own = own_ref[0]
-    mine_ref[...] = terms_ref[pl.ds(own * half, half), :]
-    theirs_ref[0:half, :] = terms_ref[pl.ds((1 - own) * half, half), :].astype(BF)
+    copies_ref[...] = jnp.sum(bias, axis=1, keepdims=True) * spread(copies_ref.shape[1])
+    part = channels // 2
+    half = theirs_ref.shape[0] - part
+    start = (1 - own_ref[0]) * half
+    terms = half_terms(padded_ref, moved_ref, moved_low_ref, moved_high_ref, start, half)
+    store_terms(terms, copies_ref, start, theirs_ref)
     even = core_ref[0] == 0
-    part = channels // 2
     low, high = grad_ref[0].astype(F32), grad_ref[count - 1].astype(F32)
     face = jnp.where(even, low, high).astype(BF)
     theirs_ref[half:, 0:lanes] = face[:part]
     theirs_ref[half:, lanes : 2 * lanes] = face[part:]
     theirs_ref[half:, 2 * lanes :] = jnp.zeros((part, theirs_ref.shape[1] - 2 * lanes), BF)
+
+
+def own_kernel(own_ref, padded_ref, moved_ref, low_ref, high_ref, copies_ref, mine_ref):
+    half = mine_ref.shape[0]
+    start = own_ref[0] * half
+    terms = half_terms(padded_ref, moved_ref, low_ref, high_ref, start, half)
+    store_terms(terms, copies_ref, start, mine_ref)
 
 
 def spread(count):
@@ -397,20 +421,17 @@
     plane = ((channels, lanes), BF)
     core = (lax.axis_index("rep") % 2).astype(jnp.int32)
     cores = core[None]
-    first, second, rows, x, occ, cot, weight, bias = call(
+    first, second, rows, x, occ = call(
         stage_kernel,
-        [
-            plane, plane, ((32, lanes), jnp.int32), (x.shape, BF), (occ.shape, jnp.int32), (x.shape, BF),
-            (weight.shape, BF), ((1, channels), F32),
-        ],
-        [(SMEM, cores), (HBM, x), (HBM, occ), (HBM, near), (HBM, cot), (HBM, weight), (HBM, bias[None])],
-        [pltpu.SMEM(near.shape, jnp.int32), pltpu.SemaphoreType.DMA((6,))],
+        [plane, plane, ((32, lanes), jnp.int32), (x.shape, BF), (occ.shape, jnp.int32)],
+        [(SMEM, cores), (HBM, x), (HBM, occ), (HBM, near)],
+        [pltpu.SMEM(near.shape, jnp.int32), pltpu.SemaphoreType.DMA((3,))],
     )
     axes = ("space", "rep")
     pairs = face_pairs()
     first = lax.ppermute(first, axes, pairs)
     second = lax.ppermute(second, axes, [(j, i) for i, j in pairs])
-    moved, pre, cot2, occ2, ahead = call(
+    moved, pre, cot2, occ2, ahead, cot, weight = call(
         inner_kernel,
         [
             ((count, width, lanes), BF),
@@ -418,11 +439,15 @@
             ((count, channels, lanes), BF),
             ((count, 8, lanes), F32),
             ((3 * channels, width), BF),
+            (cot.shape, BF),
+            (weight.shape, BF),
         ],
-        [(VMEM, rows), (VMEM, x), (VMEM, cot), (VMEM, occ), (VMEM, weight), (VMEM, bias)],
+        [(VMEM, rows), (VMEM, x), (VMEM, occ), (HBM, cot), (HBM, weight), (HBM, bias[None])],
         [
             pltpu.VMEM((count, channels, lanes), BF),
             pltpu.VMEM((channels * (count + 2), lanes), F32),
+            pltpu.VMEM((1, channels), F32),
+            pltpu.SemaphoreType.DMA((3,)),
         ],
         flops=2 * 27 * channels * channels * bricks * voxels,
     )
@@ -430,26 +455,34 @@
     me = lax.axis_index("space") * lax.axis_size("rep") + lax.axis_index("rep")
     own = (lax.population_count(me.astype(jnp.int32)) & 1)[None]
     half, columns = 3 * channels // 2, width + 64
-    result2, grad, mine, theirs = call(
+    result2, grad, theirs, padded, moved_low, moved_high, copies = call(
         outer_kernel,
         [
             ((count, channels, lanes), BF),
             ((count, channels, lanes), BF),
-            ((half, columns), F32),
             ((half + channels // 2, columns), BF),
+            ((channels * (count + 4), lanes), BF),
+            ((width, lanes), BF),
+            ((width, lanes), BF),
+            ((channels, columns - width), F32),
         ],
         [
             (SMEM, cores), (SMEM, own), (VMEM, rows), (VMEM, first), (VMEM, second), (VMEM, moved),
             (VMEM, pre), (VMEM, cot2), (VMEM, occ2), (VMEM, ahead),
         ],
-        [
-            pltpu.VMEM((channels * (count + 2), lanes), BF),
-            pltpu.VMEM((3 * channels, columns), F32),
-        ],
         flops=2 * 27 * channels * channels * bricks * voxels,
     )
     partner = [(i, i ^ 1) for i in range(devices)]
     other = lax.ppermute(theirs, axes, partner)
+    (mine,) = call(
+        own_kernel,
+        [((half, columns), F32)],
+        [
+            (SMEM, own), (VMEM, padded), (VMEM, moved), (VMEM, moved_low), (VMEM, moved_high),
+            (VMEM, copies),
+        ],
+        flops=27 * channels * channels * bricks * voxels,
+    )
     sent = ((half, columns), BF)
     mine, faces = call(
         first_sum_kernel,
@@ -457,21 +490,13 @@
         [(SMEM, cores), (VMEM, mine), (VMEM, other), (VMEM, grad)],
     )
     bits = [1 << i for i in range(1, (devices).bit_length() - 1)]
-    turn = len(bits) // 2
-    rounds = list(zip(bits, bits[turn:] + bits[:turn]))
+    rounds = list(zip(bits[:1] + bits[-1:] + bits[1:-1], bits[-1:] + bits[1:-1] + bits[:1]))
     for i, steps in enumerate(rounds):
         joined = [(j, j ^ 1 ^ steps[j.bit_count() % 2]) for j in range(devices)]
         other = lax.ppermute(mine, axes, joined)
         held = []
         if i == 0:
             faces = lax.ppermute(faces, axes, pairs)
-        if i == 1:
-            mine, first, second = call(
-                faces_sum_kernel, [sent, plane, plane], [(VMEM, mine), (VMEM, other), (VMEM, faces)]
-            )
-            continue
-        if i == 2:
-            second = lax.ppermute(second, axes, partner)
             result, total, back = call(
                 back_inner_kernel,
                 [
@@ -483,7 +508,10 @@
                 [pltpu.VMEM((count, width, lanes), BF)],
                 flops=2 * 27 * channels * channels * bricks * voxels,
             )
-            held = [total, second]
+            held = [total]
+        if i == 2:
+            first, second = faces[:channels], lax.ppermute(faces[channels:], axes, partner)
+            held = [second]
         if i == 3:
             in_grad, done = call(
                 back_outer_kernel,

time: 37.9 us -> 35.6 us (0.939)
  the two profiles are of different devices: /device:TPU:5 before, /device:TPU:0 now
where the time goes in v6:
time: 35.6 us; the launch traced here: 35.4 us
  starting transfers between devices  13 us (37%)
  Pallas kernels  12.6 us (35%)
  waiting for transfers between devices  9.06 us (25%)
  between operations  0.73 us (2%)
    pallas_call x12, Pallas kernels, call(): pl.pallas_call(body, out_shape=shapes, in_specs=[spec for spec, _ in ins]...  12.6 us
    ppermute x4, starting transfers between devices, on_device(): other = lax.ppermute(mine, axes, joined)  8.24 us
    ppermute x4, waiting for transfers between devices, on_device(): other = lax.ppermute(mine, axes, joined)  5.06 us
    ppermute x1, starting transfers between devices, on_device(): first = lax.ppermute(first, axes, pairs)  3 us
    ppermute x1, starting transfers between devices, on_device(): faces = lax.ppermute(faces, axes, pairs)  1.28 us
    ppermute x1, waiting for transfers between devices, on_device(): other = lax.ppermute(mine, axes, partner)  1.25 us
    ppermute x1, waiting for transfers between devices, on_device(): second = lax.ppermute(second, axes, [(j, i) for i, j in pairs])  1.2 us
    ppermute x1, waiting for transfers between devices, on_device(): lax.ppermute(faces[channels:], axes, partner)  1.19 us
  transfers between devices with their start and end apart: 10, of which 7 were waited for; matrix products, arithmetic and copies ran while one was open for 0% of the time, Pallas kernels for 24%

profile of v6, /device:TPU:0, one launch (start us, length us, event | category | flops | bytes accessed | tf_op | source)
XLA Modules:
  0.0 35.4 jit_solution(2949833476811715118)
XLA Ops:
  0.6 1.1 %shard_map.93 = (bf16[64,256]{1,0:T(8,128)(2,1)S(1)}, bf16[64,256]{1,0:T(8,128)(2,1)S(1)}, s32[32,256]{1,0:T(8,128)S(1)}, bf16[4,64,512]{2,1,0:T(8,128)(2,1)S(1)}, s32[4,512]{1,0:T(4,128)S(1)}) custom-call(s32[1]{0:T(128)} %bitcast.core_ref, bf16[4,64,512]{2,1,0:T(8,128)(2,1)} %bitcast.10, s32[4,512]{1,0:T(4,128)} %bitcast.11, s32[4,26]{1,0:T(4,128)} %bitcast.12), custom_call_target="tpu_custom_call" | custom-call | bytes 639396 | tf_op jit(solution)/shard_map/pallas_call | solution.py:392
  1.7 3.0 %collective-permute-start = (bf16[64,256]{1,0:T(8,128)(2,1)S(1)}, bf16[64,256]{1,0:T(8,128)(2,1)S(1)}, u32[]{:S(2)}, u32[]{:S(2)}) collective-permute-start(bf16[64,256]{1,0:T(8,128)(2,1)S(1)} %get-tuple-element.33), channel_id=1, source_target_pairs={{0,4},{1,0},{2,6},{3,2},{4,8},{5,1},{6,10},{7,3},{8,12},{9,5},{10,... | collective-permute-start | bytes 98312 | tf_op jit(solution)/shard_map/ppermute | solution.py:432
  4.7 2.7 %shard_map.94 = (bf16[8,576,256]{2,1,0:T(8,128)(2,1)S(1)}, f32[8,64,256]{2,1,0:T(8,128)S(1)}, bf16[8,64,256]{2,1,0:T(8,128)(2,1)S(1)}, f32[8,8,256]{2,1,0:T(8,12...) custom-call(s32[32,256]{1,0:T(8,128)S(1)} %get-tuple-element.32.rows_ref, ...), custom_call_target="tpu_custom_call" | custom-call | flops 452984832 | bytes 4702464 | tf_op jit(solution)/shard_map/pallas_call | solution.py:392
  7.5 1.2 %collective-permute-done.1.second_ref = bf16[64,256]{1,0:T(8,128)(2,1)S(1)} collective-permute-done((bf16[64,256]{1,0:T(8,128)(2,1)S(1)}, bf16[64,256]{1,0:T(8,128)(2,1)S(1)}, u32[]{:S(2)}, u32[]{:S(2)}) %collective-permute-start.1) | collective-permute-done | bytes 32800 | tf_op jit(solution)/shard_map/ppermute | solution.py:433
  8.7 1.9 %shard_map.95 = (bf16[8,64,256]{2,1,0:T(8,128)(2,1)S(1)}, bf16[8,64,256]{2,1,0:T(8,128)(2,1)S(1)}, bf16[128,640]{1,0:T(8,128)(2,1)S(1)}, bf16[768,256]{1,0:T(8,1...) custom-call(s32[1]{0:T(128)} %bitcast.core_ref, s32[1]{0:T(128)} %bitcast.4.own_ref, ...), custom_call_target="tpu_custom_call" | custom-call | flops 452984832 | bytes 5218312 | tf_op jit(solution)/shard_map/pallas_call | solution.py:392
  10.5 0.1 collective-permute-start.2
  10.6 1.0 %shard_map.96.mine_ref = f32[96,640]{1,0:T(8,128)S(1)} custom-call(s32[1]{0:T(128)} %bitcast.4.own_ref, bf16[768,256]{1,0:T(8,128)(2,1)S(1)} %get-tuple-element.45.padded_ref, bf16[8,576,256]{2,1,0:T(8,128)(2,1)S(1)} %get-tuple-element.37.moved_ref, bf16[576,256]{1,0:T(8,128)(2,1)S(1)} %get-tuple-element.46.low_ref, ...), custom_call_target="tpu_custom_call" | custom-call | flops 226492416 | bytes 3604484 | tf_op jit(solution)/shard_map/pallas_call | solution.py:392
  11.6 0.4 %collective-permute-done.2.other_ref = bf16[128,640]{1,0:T(8,128)(2,1)S(1)} collective-permute-done((bf16[128,640]{1,0:T(8,128)(2,1)S(1)}, bf16[128,640]{1,0:T(8,128)(2,1)S(1)}, u32[]{:S(2)}, u32[]{:S(2)}) %collective-permute-start.2) | collective-permute-done | bytes 163872 | tf_op jit(solution)/shard_map/ppermute | solution.py:476
  12.0 1.3 %collective-permute-start.5 = (bf16[96,640]{1,0:T(8,128)(2,1)S(1)}, bf16[96,640]{1,0:T(8,128)(2,1)S(1)}, u32[]{:S(2)}, u32[]{:S(2)}) collective-permute-start(bf16[96,640]{1,0:T(8,128)(2,1)S(1)} %get-tuple-element.50.after_ref.mine_ref), channel_id=1, source_target_pairs={{0,3},{1,16},{2,19},{3,0},{4,21},{5,6},{6,5},{7,22},{8,25},{9,10},... | collective-permute-start | bytes 368648 | tf_op jit(solution)/shard_map/ppermute | solution.py:496
  13.4 3.0 %shard_map.98 = (bf16[4,64,512]{2,1,0:T(8,128)(2,1)}, f32[640,256]{1,0:T(8,128)S(1)}, bf16[192,576]{1,0:T(8,128)(2,1)S(1)}) custom-call(s32[32,256]{1,0:T(8,128)S(1)} %get-tuple-element.32.rows_ref, bf16[8,64,256]{2,1,0:T(8,128)(2,1)S(1)} %get-tuple-element.42.grad_ref, bf16[8,64,256]{2,1,0:T(8,128)(2,1)S(1)} %get-tuple-element.43.result2_ref, ...), custom_call_target="tpu_custom_call" | custom-call | flops 452984832 | bytes 2039808 | tf_op jit(solution)/shard_map/pallas_call | solution.py:392
  16.4 0.0 collective-permute-done.5.other_ref
  16.4 3.0 %collective-permute-start.6 = (bf16[96,640]{1,0:T(8,128)(2,1)S(1)}, bf16[96,640]{1,0:T(8,128)(2,1)S(1)}, u32[]{:S(2)}, u32[]{:S(2)}) collective-permute-start(bf16[96,640]{1,0:T(8,128)(2,1)S(1)} %shard_map.99.mine_ref), channel_id=1, source_target_pairs={{0,17},{1,4},{2,7},{3,18},{4,1},{5,20},{6,23},{7,2},{8,13},{9,24},... | collective-permute-start | bytes 368648 | tf_op jit(solution)/shard_map/ppermute | solution.py:496
  19.4 1.3 %collective-permute-start.3 = (bf16[128,256]{1,0:T(8,128)(2,1)S(1)}, bf16[128,256]{1,0:T(8,128)(2,1)S(1)}, u32[]{:S(2)}, u32[]{:S(2)}) collective-permute-start(bf16[128,256]{1,0:T(8,128)(2,1)S(1)} %get-tuple-element.52), channel_id=1, source_target_pairs={{0,4},{1,0},{2,6},{3,2},{4,8},{5,1},{6,10},{7,3},{8,12},{9,5},{10,... | collective-permute-start | bytes 196616 | tf_op jit(solution)/shard_map/ppermute | solution.py:499
  20.7 1.3 %collective-permute-done.6.other_ref = bf16[96,640]{1,0:T(8,128)(2,1)S(1)} collective-permute-done((bf16[96,640]{1,0:T(8,128)(2,1)S(1)}, bf16[96,640]{1,0:T(8,128)(2,1)S(1)}, u32[]{:S(2)}, u32[]{:S(2)}) %collective-permute-start.6) | collective-permute-done | bytes 122912 | tf_op jit(solution)/shard_map/ppermute | solution.py:496
  22.0 3.6 %collective-permute-start.7 = (bf16[96,640]{1,0:T(8,128)(2,1)S(1)}, bf16[96,640]{1,0:T(8,128)(2,1)S(1)}, u32[]{:S(2)}, u32[]{:S(2)}) collective-permute-start(bf16[96,640]{1,0:T(8,128)(2,1)S(1)} %shard_map.100.mine_ref), channel_id=1, source_target_pairs={{0,5},{1,8},{2,11},{3,6},{4,13},{5,0},{6,3},{7,14},{8,1},{9,12},{1... | collective-permute-start | bytes 368648 | tf_op jit(solution)/shard_map/ppermute | solution.py:496
  25.6 0.1 collective-permute-start.4
  25.7 1.2 %collective-permute-done.4.refs_0_.second_ref = bf16[64,256]{1,0:T(8,128)(2,1)S(1)} collective-permute-done((bf16[64,256]{1,0:T(8,128)(2,1)S(1)}, bf16[64,256]{1,0:T(8,128)(2,1)S(1)}, u32[]{:S(2)}, u32[]{:S(2)}) %collective-permute-start.4) | collective-permute-done | bytes 32800 | tf_op jit(solution)/shard_map/ppermute | solution.py:513
  26.9 1.3 %collective-permute-done.7.other_ref = bf16[96,640]{1,0:T(8,128)(2,1)S(1)} collective-permute-done((bf16[96,640]{1,0:T(8,128)(2,1)S(1)}, bf16[96,640]{1,0:T(8,128)(2,1)S(1)}, u32[]{:S(2)}, u32[]{:S(2)}) %collective-permute-start.7) | collective-permute-done | bytes 122912 | tf_op jit(solution)/shard_map/ppermute | solution.py:496
  28.2 0.3 collective-permute-start.8
  28.6 1.6 %shard_map.102 = (bf16[4,64,512]{2,1,0:T(8,128)(2,1)}, f32[8,128]{1,0:T(8,128)S(1)}) custom-call(s32[1]{0:T(128)} %bitcast.core_ref, s32[32,256]{1,0:T(8,128)S(1)} %get-tuple-element.32.rows_ref, bf16[64,256]{1,0:T(8,128)(2,1)S(1)} %get-tuple-element.61.first_ref, bf16[64,256]{1,0:T(8,128)(2,1)S(1)} %collective-permute-done.4.refs_0_.second_ref, ...), custom_call_target="tpu_custom_call" | custom-call | flops 100663296 | bytes 1634308 | tf_op jit(solution)/shard_map/pallas_call | solution.py:392
  30.1 2.5 %collective-permute-done.8.other_ref = bf16[96,640]{1,0:T(8,128)(2,1)S(1)} collective-permute-done((bf16[96,640]{1,0:T(8,128)(2,1)S(1)}, bf16[96,640]{1,0:T(8,128)(2,1)S(1)}, u32[]{:S(2)}, u32[]{:S(2)}) %collective-permute-start.8) | collective-permute-done | bytes 122912 | tf_op jit(solution)/shard_map/ppermute | solution.py:496
  32.6 0.3 collective-permute-start.9
  33.0 1.2 %collective-permute-done.9.other_ref = f32[96,640]{1,0:T(8,128)S(1)} collective-permute-done((f32[96,640]{1,0:T(8,128)S(1)}, f32[96,640]{1,0:T(8,128)S(1)}, u32[]{:S(2)}, u32[]{:S(2)}) %collective-permute-start.9) | collective-permute-done | bytes 245792 | tf_op jit(solution)/shard_map/ppermute | solution.py:532
  34.2 1.2 %shard_map.104 = (f32[27,64,64]{2,1,0:T(8,128)}, f32[1,64]{1,0:T(1,128)}) custom-call(s32[1]{0:T(128)} %bitcast.4.own_ref, f32[96,640]{1,0:T(8,128)S(1)} %shard_map.103.mine_ref, f32[96,640]{1,0:T(8,128)S(1)} %collective-permute-done.9.other_ref), custom_call_target="tpu_custom_call" | custom-call | bytes 934148 | tf_op jit(solution)/shard_map/pallas_call | solution.py:392
  (9 shorter events, 0.2 us)
Async XLA Ops:
  1.7 5.7 %collective-permute-start = (bf16[64,256]{1,0:T(8,128)(2,1)S(1)}, bf16[64,256]{1,0:T(8,128)(2,1)S(1)}, u32[]{:S(2)}, u32[]{:S(2)}) collective-permute-start(bf16[64,256]{1,0:T(8,128)(2,1)S(1)} %get-tuple-element.33), channel_id=1, source_target_pairs={{0,4},{1,0},{2,6},{3,2},{4,8},{5,1},{6,10},{7,3},{8,12},{9,5},{10,... | collective-permute-start | bytes 98312 | tf_op jit(solution)/shard_map/ppermute | solution.py:432
  4.7 3.9 %collective-permute-start.1 = (bf16[64,256]{1,0:T(8,128)(2,1)S(1)}, bf16[64,256]{1,0:T(8,128)(2,1)S(1)}, u32[]{:S(2)}, u32[]{:S(2)}) collective-permute-start(bf16[64,256]{1,0:T(8,128)(2,1)S(1)} %get-tuple-element.34), channel_id=1, source_target_pairs={{4,0},{0,1},{6,2},{2,3},{8,4},{1,5},{10,6},{3,7},{12,8},{5,9},{14,... | collective-permute-start | bytes 98312 | tf_op jit(solution)/shard_map/ppermute | solution.py:433
  10.5 1.5 %collective-permute-start.2 = (bf16[128,640]{1,0:T(8,128)(2,1)S(1)}, bf16[128,640]{1,0:T(8,128)(2,1)S(1)}, u32[]{:S(2)}, u32[]{:S(2)}) collective-permute-start(bf16[128,640]{1,0:T(8,128)(2,1)S(1)} %get-tuple-element.49), channel_id=1, source_target_pairs={{0,1},{1,0},{2,3},{3,2},{4,5},{5,4},{6,7},{7,6},{8,9},{9,8},{10,11... | collective-permute-start | bytes 491528 | tf_op jit(solution)/shard_map/ppermute | solution.py:476
  12.0 4.4 %collective-permute-start.5 = (bf16[96,640]{1,0:T(8,128)(2,1)S(1)}, bf16[96,640]{1,0:T(8,128)(2,1)S(1)}, u32[]{:S(2)}, u32[]{:S(2)}) collective-permute-start(bf16[96,640]{1,0:T(8,128)(2,1)S(1)} %get-tuple-element.50.after_ref.mine_ref), channel_id=1, source_target_pairs={{0,3},{1,16},{2,19},{3,0},{4,21},{5,6},{6,5},{7,22},{8,25},{9,10},... | collective-permute-start | bytes 368648 | tf_op jit(solution)/shard_map/ppermute | solution.py:496
  16.4 5.5 %collective-permute-start.6 = (bf16[96,640]{1,0:T(8,128)(2,1)S(1)}, bf16[96,640]{1,0:T(8,128)(2,1)S(1)}, u32[]{:S(2)}, u32[]{:S(2)}) collective-permute-start(bf16[96,640]{1,0:T(8,128)(2,1)S(1)} %shard_map.99.mine_ref), channel_id=1, source_target_pairs={{0,17},{1,4},{2,7},{3,18},{4,1},{5,20},{6,23},{7,2},{8,13},{9,24},... | collective-permute-start | bytes 368648 | tf_op jit(solution)/shard_map/ppermute | solution.py:496
  19.4 6.2 %collective-permute-start.3 = (bf16[128,256]{1,0:T(8,128)(2,1)S(1)}, bf16[128,256]{1,0:T(8,128)(2,1)S(1)}, u32[]{:S(2)}, u32[]{:S(2)}) collective-permute-start(bf16[128,256]{1,0:T(8,128)(2,1)S(1)} %get-tuple-element.52), channel_id=1, source_target_pairs={{0,4},{1,0},{2,6},{3,2},{4,8},{5,1},{6,10},{7,3},{8,12},{9,5},{10,... | collective-permute-start | bytes 196616 | tf_op jit(solution)/shard_map/ppermute | solution.py:499
  22.0 6.2 %collective-permute-start.7 = (bf16[96,640]{1,0:T(8,128)(2,1)S(1)}, bf16[96,640]{1,0:T(8,128)(2,1)S(1)}, u32[]{:S(2)}, u32[]{:S(2)}) collective-permute-start(bf16[96,640]{1,0:T(8,128)(2,1)S(1)} %shard_map.100.mine_ref), channel_id=1, source_target_pairs={{0,5},{1,8},{2,11},{3,6},{4,13},{5,0},{6,3},{7,14},{8,1},{9,12},{1... | collective-permute-start | bytes 368648 | tf_op jit(solution)/shard_map/ppermute | solution.py:496
  25.6 1.3 %collective-permute-start.4 = (bf16[64,256]{1,0:T(8,128)(2,1)S(1)}, bf16[64,256]{1,0:T(8,128)(2,1)S(1)}, u32[]{:S(2)}, u32[]{:S(2)}) collective-permute-start(bf16[64,256]{1,0:T(8,128)(2,1)S(1)} %get-tuple-element.60), channel_id=1, source_target_pairs={{0,1},{1,0},{2,3},{3,2},{4,5},{5,4},{6,7},{7,6},{8,9},{9,8},{10,11... | collective-permute-start | bytes 98312 | tf_op jit(solution)/shard_map/ppermute | solution.py:513
  28.2 4.4 %collective-permute-start.8 = (bf16[96,640]{1,0:T(8,128)(2,1)S(1)}, bf16[96,640]{1,0:T(8,128)(2,1)S(1)}, u32[]{:S(2)}, u32[]{:S(2)}) collective-permute-start(bf16[96,640]{1,0:T(8,128)(2,1)S(1)} %shard_map.101.after_ref.mine_ref), channel_id=1, source_target_pairs={{0,9},{1,2},{2,1},{3,10},{4,7},{5,12},{6,15},{7,4},{8,11},{9,0},{1... | collective-permute-start | bytes 368648 | tf_op jit(solution)/shard_map/ppermute | solution.py:496
  32.6 1.6 %collective-permute-start.9 = (f32[96,640]{1,0:T(8,128)S(1)}, f32[96,640]{1,0:T(8,128)S(1)}, u32[]{:S(2)}, u32[]{:S(2)}) collective-permute-start(f32[96,640]{1,0:T(8,128)S(1)} %shard_map.103.mine_ref), channel_id=1, source_target_pairs={{0,1},{1,0},{2,3},{3,2},{4,5},{5,4},{6,7},{7,6},{8,9},{9,8},{10,11... | collective-permute-start | bytes 737288 | tf_op jit(solution)/shard_map/ppermute | solution.py:532

commit v7 on v6

--- a/solution.py
+++ b/solution.py
@@ -84,6 +84,10 @@
     source = base + (y & 7) * 8 + (z & 7)
     row = lax.broadcasted_iota(jnp.int32, (size, size), 0)
     return jnp.where(row == source, 1.0, 0.0).astype(BF)
+
+
+def phase(scalar_ref):
+    return pl.when(scalar_ref[0] >= 0)
 
 
 def dot(x, y):
@@ -166,6 +170,16 @@
             )
 
 
+def add_products(core_ref, weight_ref, moved_ref, total_ref):
+    channels = weight_ref.shape[0] // 3
+
+    @phase(core_ref)
+    def _():
+        for x in range(moved_ref.shape[0]):
+            at = slice(channels * x, channels * (x + 3))
+            total_ref[at, :] += dot(weight_ref[...], moved_ref[x])
+
+
 def shifted_face(face, rows_ref, dx, bricks):
     rows = slot_rows(rows_ref, dx)
     parts = []
@@ -176,7 +190,7 @@
 
 
 def inner_kernel(
-    rows_ref, feats_ref, occ_ref, cot_from_ref, weight_from_ref, bias_from_ref,
+    core_ref, rows_ref, feats_ref, occ_ref, cot_from_ref, weight_from_ref, bias_from_ref,
     moved_ref, pre_ref, cot2_ref, occ2_ref, ahead_ref, cot_ref, weight_ref,
     planes_ref, total_ref, bias_ref, sems,
 ):
@@ -212,9 +226,7 @@
     start = jnp.broadcast_to(column, (channels, bricks * PLANE))
     for x in range(count + 2):
         total_ref[channels * x : channels * (x + 1), :] = start
-    for x in range(count):
-        at = slice(channels * x, channels * (x + 3))
-        total_ref[at, :] += dot(ahead_ref[...], moved_ref[x])
+    add_products(core_ref, ahead_ref, moved_ref, total_ref)
     pre_ref[...] = total_ref[channels : channels * (count + 1), :].reshape(pre_ref.shape)
 
 
@@ -231,12 +243,18 @@
 
 
 def store_terms(terms, copies_ref, start, out_ref):
-    half, width = terms.shape
-    channels = copies_ref.shape[0]
-    out_ref[0:half, 0:width] = terms.astype(out_ref.dtype)
+    half = terms.shape[0]
+    unit = half // 3
+    full = terms.shape[1] // 128
+    for t in range(full):
+        out_ref[half * t : half * (t + 1), :] = terms[:, 128 * t : 128 * t + 128].astype(out_ref.dtype)
+    last = terms[:, 128 * full :]
     copies = jnp.where(start == 0, copies_ref[...], 0.0)
-    copies = jnp.concatenate([copies, jnp.zeros((half - channels, copies.shape[1]), F32)], axis=0)
-    out_ref[0:half, width:] = copies.astype(out_ref.dtype)
+    one = jnp.concatenate([last[:unit], last[unit : 2 * unit]], axis=1)
+    two = jnp.concatenate([last[2 * unit :], copies], axis=1)
+    at = half * full
+    out_ref[at : at + unit, :] = one.astype(out_ref.dtype)
+    out_ref[at + unit : at + 2 * unit, :] = two.astype(out_ref.dtype)
 
 
 def outer_kernel(
@@ -268,48 +286,43 @@
         grad_ref[x] = grad
         padded_ref[channels * (x + 2) : channels * (x + 3), :] = grad
         bias = bias + grad.astype(F32)
-    copies_ref[...] = jnp.sum(bias, axis=1, keepdims=True) * spread(copies_ref.shape[1])
-    part = channels // 2
-    half = theirs_ref.shape[0] - part
+    at = (channels, channels)
+    same = lax.broadcasted_iota(jnp.int32, at, 0) == lax.broadcasted_iota(jnp.int32, at, 1)
+    row = jnp.sum(jnp.where(same, jnp.sum(bias, axis=1, keepdims=True), 0.0), axis=0, keepdims=True)
+    copies_ref[...] = row * spread(copies_ref.shape)
+    half = 3 * channels // 2
     start = (1 - own_ref[0]) * half
     terms = half_terms(padded_ref, moved_ref, moved_low_ref, moved_high_ref, start, half)
     store_terms(terms, copies_ref, start, theirs_ref)
     even = core_ref[0] == 0
     low, high = grad_ref[0].astype(F32), grad_ref[count - 1].astype(F32)
     face = jnp.where(even, low, high).astype(BF)
-    theirs_ref[half:, 0:lanes] = face[:part]
-    theirs_ref[half:, lanes : 2 * lanes] = face[part:]
-    theirs_ref[half:, 2 * lanes :] = jnp.zeros((part, theirs_ref.shape[1] - 2 * lanes), BF)
+    size = theirs_ref.shape[0] - channels * (lanes // 128)
+    for t in range(lanes // 128):
+        theirs_ref[size + channels * t : size + channels * (t + 1), :] = face[:, 128 * t : 128 * t + 128]
 
 
 def own_kernel(own_ref, padded_ref, moved_ref, low_ref, high_ref, copies_ref, mine_ref):
-    half = mine_ref.shape[0]
+    half = 3 * copies_ref.shape[1] // 2
     start = own_ref[0] * half
     terms = half_terms(padded_ref, moved_ref, low_ref, high_ref, start, half)
     store_terms(terms, copies_ref, start, mine_ref)
 
 
-def spread(count):
-    return 1.0 + lax.broadcasted_iota(jnp.int32, (1, count), 1).astype(F32) * (1.0 / count)
+def spread(shape):
+    return 1.0 + lax.broadcasted_iota(jnp.int32, shape, 0).astype(F32) * (1.0 / shape[0])
 
 
 def first_sum_kernel(core_ref, mine_ref, other_ref, grad_ref, out_ref, faces_ref):
-    half = mine_ref.shape[0]
-    out_ref[...] = (mine_ref[...] + other_ref[0:half, :].astype(F32)).astype(BF)
+    size = mine_ref.shape[0]
+    out_ref[...] = (mine_ref[...] + other_ref[0:size, :].astype(F32)).astype(BF)
     count, channels, lanes = grad_ref.shape
-    part = channels // 2
     even = core_ref[0] == 0
     low, high = grad_ref[0].astype(F32), grad_ref[count - 1].astype(F32)
     faces_ref[0:channels, :] = jnp.where(even, high, low).astype(BF)
-    faces_ref[channels : channels + part, :] = other_ref[half:, 0:lanes]
-    faces_ref[channels + part :, :] = other_ref[half:, lanes : 2 * lanes]
-
-
-def faces_sum_kernel(mine_ref, other_ref, faces_ref, out_ref, own_ref, sibling_ref):
-    channels = own_ref.shape[0]
-    out_ref[...] = (mine_ref[...].astype(F32) + other_ref[...].astype(F32)).astype(BF)
-    own_ref[...] = faces_ref[0:channels, :]
-    sibling_ref[...] = faces_ref[channels:, :]
+    for t in range(lanes // 128):
+        rows = slice(size + channels * t, size + channels * (t + 1))
+        faces_ref[channels:, 128 * t : 128 * t + 128] = other_ref[rows, :]
 
 
 def sum_kernel(mine_ref, other_ref, *refs):
@@ -318,7 +331,7 @@
 
 
 def back_inner_kernel(
-    rows_ref, grad_ref, result2_ref, weight_ref, after_ref,
+    core_ref, rows_ref, grad_ref, result2_ref, weight_ref, after_ref,
     result_ref, total_ref, back_ref, moved_ref,
 ):
     count, channels, lanes = grad_ref.shape
@@ -326,9 +339,7 @@
     back_weights(weight_ref, back_ref)
     shifted(grad_ref, moved_ref, rows_ref, bricks, channels)
     total_ref[...] = jnp.zeros(total_ref.shape, F32)
-    for x in range(count):
-        at = slice(channels * x, channels * (x + 3))
-        total_ref[at, :] += dot(back_ref[...], moved_ref[x])
+    add_products(core_ref, back_ref, moved_ref, total_ref)
     for t in range(count // 2):
         out = from_planes(result2_ref[2 * t].astype(F32), result2_ref[2 * t + 1].astype(F32))
         for m in range(bricks):
@@ -363,29 +374,57 @@
             ).astype(BF)
 
 
-def final_kernel(normaliser, own_ref, mine_ref, other_ref, weight_ref, bias_ref, whole_ref):
-    half, columns = mine_ref.shape
-    channels = weight_ref.shape[1]
-    own = own_ref[0]
-    whole_ref[pl.ds(own * half, half), :] = mine_ref[...]
-    whole_ref[pl.ds((1 - own) * half, half), :] = other_ref[...]
-    for r in range(3):
-        rows = slice(channels * r, channels * (r + 1))
-        for t in range(columns // 128):
-            tile = whole_ref[rows, 128 * t : 128 * t + 128] * normaliser
-            weight_ref[9 * (2 - r) + 2 * t] = tile[:, :channels]
-            if 2 * t + 1 < 9:
-                weight_ref[9 * (2 - r) + 2 * t + 1] = pltpu.roll(tile, 128 - channels, 1)[:, :channels]
-            elif r == 0:
-                copies = pltpu.roll(tile, 128 - channels, 1)[:, :channels]
-                copies = copies / (spread(channels) * channels)
-                column = jnp.sum(copies, axis=1, keepdims=True)
-                at = (channels, channels)
-                same = lax.broadcasted_iota(jnp.int32, at, 0) == lax.broadcasted_iota(jnp.int32, at, 1)
-                bias_ref[...] = jnp.sum(jnp.where(same, column, 0.0), axis=0, keepdims=True)
-
-
-def call(body, outs, ins, scratch=(), flops=0):
+def arrived_bias(scale, source_ref, channels):
+    unit = channels // 2
+    rows = source_ref.shape[0]
+    tile = pltpu.roll(source_ref[rows - unit : rows, :], 128 - channels, 1)[:, :channels]
+    return jnp.sum(tile * (scale / (spread(tile.shape) * unit)), axis=0, keepdims=True)
+
+
+def store_half(scale, mine, source_ref, weight_ref, held_ref, sems):
+    half, unit, channels = 3 * held_ref.shape[3] // 2, held_ref.shape[2], held_ref.shape[3]
+    copies = []
+    for j in range(3):
+        for t in range(4):
+            rows = slice(half * t + unit * j, half * t + unit * (j + 1))
+            tile = source_ref[rows, :] * scale
+            held_ref[j, 2 * t] = tile[:, :channels]
+            held_ref[j, 2 * t + 1] = pltpu.roll(tile, 128 - channels, 1)[:, :channels]
+        at = 4 * half + unit * (j // 2)
+        tile = source_ref[at : at + unit, :] * scale
+        if j == 1:
+            tile = pltpu.roll(tile, 128 - channels, 1)
+        held_ref[j, 8] = tile[:, :channels]
+        u = 3 * mine + j
+        place = weight_ref.at[
+            pl.ds(9 * (2 - u // 2), 9), pl.ds(pl.multiple_of(unit * (u % 2), unit), unit), :
+        ]
+        copies.append(pltpu.make_async_copy(held_ref.at[j], place, sems.at[j]))
+        copies[-1].start()
+    return copies
+
+
+def own_half_kernel(scale, own_ref, source_ref, weight_ref, bias_ref, held_ref, sems):
+    copies = store_half(scale, own_ref[0], source_ref, weight_ref, held_ref, sems)
+    bias_ref[...] = arrived_bias(scale, source_ref, held_ref.shape[3])
+    for copy in copies:
+        copy.wait()
+
+
+def other_half_kernel(
+    scale, own_ref, source_ref, begun_ref, own_bias_ref,
+    weight_ref, bias_ref, held_ref, bias_held_ref, sems,
+):
+    bias = arrived_bias(scale, source_ref, held_ref.shape[3])
+    bias_held_ref[...] = jnp.where(own_ref[0] == 0, own_bias_ref[...], bias)
+    copies = [pltpu.make_async_copy(bias_held_ref, bias_ref, sems.at[3])]
+    copies[0].start()
+    copies += store_half(scale, 1 - own_ref[0], source_ref, weight_ref, held_ref, sems)
+    for copy in copies:
+        copy.wait()
+
+
+def call(body, outs, ins, scratch=(), flops=0, out_specs=None, aliases=None):
     shapes = [jax.ShapeDtypeStruct(shape, dtype) for shape, dtype in outs]
     moved = sum(math.prod(s.shape) * s.dtype.itemsize for s in shapes)
     moved += sum(math.prod(x.shape) * x.dtype.itemsize for _, x in ins)
@@ -393,7 +432,8 @@
         body,
         out_shape=shapes,
         in_specs=[spec for spec, _ in ins],
-        out_specs=[VMEM] * len(shapes),
+        out_specs=out_specs or [VMEM] * len(shapes),
+        input_output_aliases=aliases or {},
         scratch_shapes=list(scratch),
         compiler_params=pltpu.CompilerParams(vmem_limit_bytes=32 << 20),
         cost_estimate=pl.CostEstimate(flops=flops, bytes_accessed=moved, transcendentals=0),
@@ -442,7 +482,7 @@
             (cot.shape, BF),
             (weight.shape, BF),
         ],
-        [(VMEM, rows), (VMEM, x), (VMEM, occ), (HBM, cot), (HBM, weight), (HBM, bias[None])],
+        [(SMEM, cores), (VMEM, rows), (VMEM, x), (VMEM, occ), (HBM, cot), (HBM, weight), (HBM, bias[None])],
         [
             pltpu.VMEM((count, channels, lanes), BF),
             pltpu.VMEM((channels * (count + 2), lanes), F32),
@@ -454,17 +494,17 @@
     devices = lax.axis_size("space") * lax.axis_size("rep")
     me = lax.axis_index("space") * lax.axis_size("rep") + lax.axis_index("rep")
     own = (lax.population_count(me.astype(jnp.int32)) & 1)[None]
-    half, columns = 3 * channels // 2, width + 64
+    size = 3 * channels // 2 * (width // 128) + channels
     result2, grad, theirs, padded, moved_low, moved_high, copies = call(
         outer_kernel,
         [
             ((count, channels, lanes), BF),
             ((count, channels, lanes), BF),
-            ((half + channels // 2, columns), BF),
+            ((size + channels * lanes // 128, 128), BF),
             ((channels * (count + 4), lanes), BF),
             ((width, lanes), BF),
             ((width, lanes), BF),
-            ((channels, columns - width), F32),
+            ((channels // 2, channels), F32),
         ],
         [
             (SMEM, cores), (SMEM, own), (VMEM, rows), (VMEM, first), (VMEM, second), (VMEM, moved),
@@ -476,14 +516,14 @@
     other = lax.ppermute(theirs, axes, partner)
     (mine,) = call(
         own_kernel,
-        [((half, columns), F32)],
+        [((size, 128), F32)],
         [
             (SMEM, own), (VMEM, padded), (VMEM, moved), (VMEM, moved_low), (VMEM, moved_high),
             (VMEM, copies),
         ],
         flops=27 * channels * channels * bricks * voxels,
     )
-    sent = ((half, columns), BF)
+    sent = ((size, 128), BF)
     mine, faces = call(
         first_sum_kernel,
         [sent, ((2 * channels, lanes), BF)],
@@ -504,7 +544,10 @@
                     ((channels * (count + 2), lanes), F32),
                     ((3 * channels, width), BF),
                 ],
-                [(VMEM, rows), (VMEM, grad), (VMEM, result2), (VMEM, weight), (ANY, mine)],
+                [
+                    (SMEM, cores), (VMEM, rows), (VMEM, grad), (VMEM, result2), (VMEM, weight),
+                    (ANY, mine),
+                ],
                 [pltpu.VMEM((count, width, lanes), BF)],
                 flops=2 * 27 * channels * channels * bricks * voxels,
             )
@@ -533,11 +576,22 @@
     normaliser = 1.0 / math.sqrt(
         feats.shape[0] * lax.axis_size("rep") * bricks * lax.axis_size("space") * voxels
     )
+    held = pltpu.VMEM((3, 9, channels // 2, channels), F32)
+    outs = [(weight.shape, F32), ((1, channels), F32)]
     weight_grad, bias_grad = call(
-        functools.partial(final_kernel, normaliser),
-        [(weight.shape, F32), ((1, channels), F32)],
-        [(SMEM, own), (VMEM, mine), (VMEM, other)],
-        [pltpu.VMEM((3 * channels, columns), F32)],
+        functools.partial(own_half_kernel, normaliser),
+        outs,
+        [(SMEM, own), (VMEM, mine)],
+        [held, pltpu.SemaphoreType.DMA((3,))],
+        out_specs=[HBM, VMEM],
+    )
+    weight_grad, bias_grad = call(
+        functools.partial(other_half_kernel, normaliser),
+        outs,
+        [(SMEM, own), (VMEM, other), (ANY, weight_grad), (VMEM, bias_grad)],
+        [held, pltpu.VMEM((1, channels), F32), pltpu.SemaphoreType.DMA((4,))],
+        out_specs=[HBM, HBM],
+        aliases={2: 0},
     )
     return result[None], in_grad[None], weight_grad, bias_grad[0]
 

time: 35.6 us -> 34.8 us (0.978)
  Pallas kernels: 12.6 us -> 12.2 us
    ppermute x1, waiting for transfers between devices: 1.25 us -> 0.44 us  [on_device(): other = lax.ppermute(mine, axes, partner)]
    ppermute x1, waiting for transfers between devices: 1.2 us -> 1.71 us  [on_device(): second = lax.ppermute(second, axes, [(j, i) for i, j in pairs])]
    pallas_call x12 -> x13, Pallas kernels: 12.6 us -> 12.2 us  [call(): pl.pallas_call(body, out_shape=shapes, in_specs=[spec for spec, _ in ins]...]
  transfers between devices with their start and end apart: 10 -> 10, of which waited for: 7 -> 8; matrix products, arithmetic and copies ran while one was open for 0% -> 0% of each run, Pallas kernels for 24% -> 23%
where the time goes in v7:
time: 34.8 us; the launch traced here: 34.7 us
  starting transfers between devices  12.8 us (37%)
  Pallas kernels  12.2 us (35%)
  waiting for transfers between devices  8.94 us (26%)
  between operations  0.72 us (2%)
    pallas_call x13, Pallas kernels, call(): pl.pallas_call(body, out_shape=shapes, in_specs=[spec for spec, _ in ins]...  12.2 us
    ppermute x4, starting transfers between devices, on_device(): other = lax.ppermute(mine, axes, joined)  8.32 us
    ppermute x4, waiting for transfers between devices, on_device(): other = lax.ppermute(mine, axes, joined)  5.28 us
    ppermute x1, starting transfers between devices, on_device(): first = lax.ppermute(first, axes, pairs)  3 us
    ppermute x1, waiting for transfers between devices, on_device(): second = lax.ppermute(second, axes, [(j, i) for i, j in pairs])  1.71 us
    ppermute x1, waiting for transfers between devices, on_device(): lax.ppermute(faces[channels:], axes, partner)  1.19 us
    ppermute x1, starting transfers between devices, on_device(): faces = lax.ppermute(faces, axes, pairs)  1.19 us
  transfers between devices with their start and end apart: 10, of which 8 were waited for; matrix products, arithmetic and copies ran while one was open for 0% of the time, Pallas kernels for 23%

profile of v7, /device:TPU:0, one launch (start us, length us, event | category | flops | bytes accessed | tf_op | source)
XLA Modules:
  0.0 34.7 jit_solution(13704597061229886137)
XLA Ops:
  0.6 1.1 %shard_map.93 = (bf16[64,256]{1,0:T(8,128)(2,1)S(1)}, bf16[64,256]{1,0:T(8,128)(2,1)S(1)}, s32[32,256]{1,0:T(8,128)S(1)}, bf16[4,64,512]{2,1,0:T(8,128)(2,1)S(1)}, s32[4,512]{1,0:T(4,128)S(1)}) custom-call(s32[1]{0:T(128)} %bitcast.core_ref, bf16[4,64,512]{2,1,0:T(8,128)(2,1)} %bitcast.10, s32[4,512]{1,0:T(4,128)} %bitcast.11, s32[4,26]{1,0:T(4,128)} %bitcast.12), custom_call_target="tpu_custom_call" | custom-call | bytes 639396 | tf_op jit(solution)/shard_map/pallas_call | solution.py:431
  1.7 3.0 %collective-permute-start = (bf16[64,256]{1,0:T(8,128)(2,1)S(1)}, bf16[64,256]{1,0:T(8,128)(2,1)S(1)}, u32[]{:S(2)}, u32[]{:S(2)}) collective-permute-start(bf16[64,256]{1,0:T(8,128)(2,1)S(1)} %get-tuple-element.35), channel_id=1, source_target_pairs={{0,4},{1,0},{2,6},{3,2},{4,8},{5,1},{6,10},{7,3},{8,12},{9,5},{10,... | collective-permute-start | bytes 98312 | tf_op jit(solution)/shard_map/ppermute | solution.py:472
  4.7 2.2 %shard_map.94 = (bf16[8,576,256]{2,1,0:T(8,128)(2,1)S(1)}, f32[8,64,256]{2,1,0:T(8,128)S(1)}, bf16[8,64,256]{2,1,0:T(8,128)(2,1)S(1)}, f32[8,8,256]{2,1,0:T(8,12...) custom-call(s32[1]{0:T(128)} %bitcast.core_ref, ...), custom_call_target="tpu_custom_call" | custom-call | flops 452984832 | bytes 4702468 | tf_op jit(solution)/shard_map/pallas_call | solution.py:431
  6.9 1.7 %collective-permute-done.1.second_ref = bf16[64,256]{1,0:T(8,128)(2,1)S(1)} collective-permute-done((bf16[64,256]{1,0:T(8,128)(2,1)S(1)}, bf16[64,256]{1,0:T(8,128)(2,1)S(1)}, u32[]{:S(2)}, u32[]{:S(2)}) %collective-permute-start.1) | collective-permute-done | bytes 32800 | tf_op jit(solution)/shard_map/ppermute | solution.py:473
  8.7 2.0 %shard_map.95 = (bf16[8,64,256]{2,1,0:T(8,128)(2,1)S(1)}, bf16[8,64,256]{2,1,0:T(8,128)(2,1)S(1)}, bf16[576,128]{1,0:T(8,128)(2,1)S(1)}, bf16[768,256]{1,0:T(8,1...) custom-call(s32[1]{0:T(128)} %bitcast.core_ref, s32[1]{0:T(128)} %bitcast.4.own_ref, ...), custom_call_target="tpu_custom_call" | custom-call | flops 452984832 | bytes 5193736 | tf_op jit(solution)/shard_map/pallas_call | solution.py:431
  10.6 1.1 %shard_map.96.mine_ref = f32[448,128]{1,0:T(8,128)S(1)} custom-call(s32[1]{0:T(128)} %bitcast.4.own_ref, bf16[768,256]{1,0:T(8,128)(2,1)S(1)} %get-tuple-element.47.padded_ref, bf16[8,576,256]{2,1,0:T(8,128)(2,1)S(1)} %get-tuple-element.39.moved_ref, bf16[576,256]{1,0:T(8,128)(2,1)S(1)} %get-tuple-element.48.low_ref, ...), custom_call_target="tpu_custom_call" | custom-call | flops 226492416 | bytes 3579908 | tf_op jit(solution)/shard_map/pallas_call | solution.py:431
  11.7 0.3 collective-permute-done.2.other_ref
  12.0 1.4 %collective-permute-start.5 = (bf16[448,128]{1,0:T(8,128)(2,1)S(1)}, bf16[448,128]{1,0:T(8,128)(2,1)S(1)}, u32[]{:S(2)}, u32[]{:S(2)}) collective-permute-start(bf16[448,128]{1,0:T(8,128)(2,1)S(1)} %get-tuple-element.52.after_ref.mine_ref), channel_id=1, source_target_pairs={{0,3},{1,16},{2,19},{3,0},{4,21},{5,6},{6,5},{7,22},{8,25},{9,10},... | collective-permute-start | bytes 344072 | tf_op jit(solution)/shard_map/ppermute | solution.py:536
  13.4 2.4 %shard_map.98 = (bf16[4,64,512]{2,1,0:T(8,128)(2,1)}, f32[640,256]{1,0:T(8,128)S(1)}, bf16[192,576]{1,0:T(8,128)(2,1)S(1)}) custom-call(s32[1]{0:T(128)} %bitcast.core_ref, s32[32,256]{1,0:T(8,128)S(1)} %get-tuple-element.34.rows_ref, bf16[8,64,256]{2,1,0:T(8,128)(2,1)S(1)} %get-tuple-element.44.grad_ref, ...), custom_call_target="tpu_custom_call" | custom-call | flops 452984832 | bytes 2031620 | tf_op jit(solution)/shard_map/pallas_call | solution.py:431
  15.8 0.5 %collective-permute-done.5.other_ref = bf16[448,128]{1,0:T(8,128)(2,1)S(1)} collective-permute-done((bf16[448,128]{1,0:T(8,128)(2,1)S(1)}, bf16[448,128]{1,0:T(8,128)(2,1)S(1)}, u32[]{:S(2)}, u32[]{:S(2)}) %collective-permute-start.5) | collective-permute-done | bytes 114720 | tf_op jit(solution)/shard_map/ppermute | solution.py:536
  16.4 2.8 %collective-permute-start.6 = (bf16[448,128]{1,0:T(8,128)(2,1)S(1)}, bf16[448,128]{1,0:T(8,128)(2,1)S(1)}, u32[]{:S(2)}, u32[]{:S(2)}) collective-permute-start(bf16[448,128]{1,0:T(8,128)(2,1)S(1)} %shard_map.99.mine_ref), channel_id=1, source_target_pairs={{0,17},{1,4},{2,7},{3,18},{4,1},{5,20},{6,23},{7,2},{8,13},{9,24},... | collective-permute-start | bytes 344072 | tf_op jit(solution)/shard_map/ppermute | solution.py:536
  19.2 1.2 %collective-permute-start.3 = (bf16[128,256]{1,0:T(8,128)(2,1)S(1)}, bf16[128,256]{1,0:T(8,128)(2,1)S(1)}, u32[]{:S(2)}, u32[]{:S(2)}) collective-permute-start(bf16[128,256]{1,0:T(8,128)(2,1)S(1)} %get-tuple-element.54), channel_id=1, source_target_pairs={{0,4},{1,0},{2,6},{3,2},{4,8},{5,1},{6,10},{7,3},{8,12},{9,5},{10,... | collective-permute-start | bytes 196616 | tf_op jit(solution)/shard_map/ppermute | solution.py:539
  20.4 1.3 %collective-permute-done.6.other_ref = bf16[448,128]{1,0:T(8,128)(2,1)S(1)} collective-permute-done((bf16[448,128]{1,0:T(8,128)(2,1)S(1)}, bf16[448,128]{1,0:T(8,128)(2,1)S(1)}, u32[]{:S(2)}, u32[]{:S(2)}) %collective-permute-start.6) | collective-permute-done | bytes 114720 | tf_op jit(solution)/shard_map/ppermute | solution.py:536
  21.7 3.7 %collective-permute-start.7 = (bf16[448,128]{1,0:T(8,128)(2,1)S(1)}, bf16[448,128]{1,0:T(8,128)(2,1)S(1)}, u32[]{:S(2)}, u32[]{:S(2)}) collective-permute-start(bf16[448,128]{1,0:T(8,128)(2,1)S(1)} %shard_map.100.mine_ref), channel_id=1, source_target_pairs={{0,5},{1,8},{2,11},{3,6},{4,13},{5,0},{6,3},{7,14},{8,1},{9,12},{1... | collective-permute-start | bytes 344072 | tf_op jit(solution)/shard_map/ppermute | solution.py:536
  25.4 0.1 collective-permute-start.4
  25.5 1.2 %collective-permute-done.4.refs_0_.second_ref = bf16[64,256]{1,0:T(8,128)(2,1)S(1)} collective-permute-done((bf16[64,256]{1,0:T(8,128)(2,1)S(1)}, bf16[64,256]{1,0:T(8,128)(2,1)S(1)}, u32[]{:S(2)}, u32[]{:S(2)}) %collective-permute-start.4) | collective-permute-done | bytes 32800 | tf_op jit(solution)/shard_map/ppermute | solution.py:556
  26.7 1.2 %collective-permute-done.7.other_ref = bf16[448,128]{1,0:T(8,128)(2,1)S(1)} collective-permute-done((bf16[448,128]{1,0:T(8,128)(2,1)S(1)}, bf16[448,128]{1,0:T(8,128)(2,1)S(1)}, u32[]{:S(2)}, u32[]{:S(2)}) %collective-permute-start.7) | collective-permute-done | bytes 114720 | tf_op jit(solution)/shard_map/ppermute | solution.py:536
  27.9 0.4 %collective-permute-start.8 = (bf16[448,128]{1,0:T(8,128)(2,1)S(1)}, bf16[448,128]{1,0:T(8,128)(2,1)S(1)}, u32[]{:S(2)}, u32[]{:S(2)}) collective-permute-start(bf16[448,128]{1,0:T(8,128)(2,1)S(1)} %shard_map.101.after_ref.mine_ref), channel_id=1, source_target_pairs={{0,9},{1,2},{2,1},{3,10},{4,7},{5,12},{6,15},{7,4},{8,11},{9,0},{1... | collective-permute-start | bytes 344072 | tf_op jit(solution)/shard_map/ppermute | solution.py:536
  28.3 1.6 %shard_map.102 = (bf16[4,64,512]{2,1,0:T(8,128)(2,1)}, f32[8,128]{1,0:T(8,128)S(1)}) custom-call(s32[1]{0:T(128)} %bitcast.core_ref, s32[32,256]{1,0:T(8,128)S(1)} %get-tuple-element.34.rows_ref, bf16[64,256]{1,0:T(8,128)(2,1)S(1)} %get-tuple-element.65.first_ref, bf16[64,256]{1,0:T(8,128)(2,1)S(1)} %collective-permute-done.4.refs_0_.second_ref, ...), custom_call_target="tpu_custom_call" | custom-call | flops 100663296 | bytes 1626116 | tf_op jit(solution)/shard_map/pallas_call | solution.py:431
  29.9 2.3 %collective-permute-done.8.other_ref = bf16[448,128]{1,0:T(8,128)(2,1)S(1)} collective-permute-done((bf16[448,128]{1,0:T(8,128)(2,1)S(1)}, bf16[448,128]{1,0:T(8,128)(2,1)S(1)}, u32[]{:S(2)}, u32[]{:S(2)}) %collective-permute-start.8) | collective-permute-done | bytes 114720 | tf_op jit(solution)/shard_map/ppermute | solution.py:536
  32.2 0.2 collective-permute-start.9
  32.5 0.9 %shard_map.104 = (f32[27,64,64]{2,1,0:T(8,128)}, f32[1,64]{1,0:T(1,128)S(1)}) custom-call(s32[1]{0:T(128)} %bitcast.4.own_ref, f32[448,128]{1,0:T(8,128)S(1)} %shard_map.103.source_ref), custom_call_target="tpu_custom_call" | custom-call | bytes 672004 | tf_op jit(solution)/shard_map/pallas_call | solution.py:431
  33.3 0.4 %collective-permute-done.9.source_ref = f32[448,128]{1,0:T(8,128)S(1)} collective-permute-done((f32[448,128]{1,0:T(8,128)S(1)}, f32[448,128]{1,0:T(8,128)S(1)}, u32[]{:S(2)}, u32[]{:S(2)}) %collective-permute-start.9) | collective-permute-done | bytes 229408 | tf_op jit(solution)/shard_map/ppermute | solution.py:575
  33.8 0.9 %shard_map.105 = (f32[27,64,64]{2,1,0:T(8,128)}, f32[1,64]{1,0:T(1,128)}) custom-call(s32[1]{0:T(128)} %bitcast.4.own_ref, f32[448,128]{1,0:T(8,128)S(1)} %collective-permute-done.9.source_ref, f32[27,64,64]{2,1,0:T(8,128)} %get-tuple-element.60.begun_ref, f32[1,64]{1,0:T(1,128)S(1)} %get-tuple-element.61.own_bias_ref), custom_call_target="tpu_custom_call", output_to_operand_aliasing={{0}: (2, {})} | custom-call | bytes 1114628 | tf_op jit(solution)/shard_map/pallas_call | solution.py:431
  (10 shorter events, 0.2 us)
Async XLA Ops:
  1.7 5.2 %collective-permute-start = (bf16[64,256]{1,0:T(8,128)(2,1)S(1)}, bf16[64,256]{1,0:T(8,128)(2,1)S(1)}, u32[]{:S(2)}, u32[]{:S(2)}) collective-permute-start(bf16[64,256]{1,0:T(8,128)(2,1)S(1)} %get-tuple-element.35), channel_id=1, source_target_pairs={{0,4},{1,0},{2,6},{3,2},{4,8},{5,1},{6,10},{7,3},{8,12},{9,5},{10,... | collective-permute-start | bytes 98312 | tf_op jit(solution)/shard_map/ppermute | solution.py:472
  4.7 3.9 %collective-permute-start.1 = (bf16[64,256]{1,0:T(8,128)(2,1)S(1)}, bf16[64,256]{1,0:T(8,128)(2,1)S(1)}, u32[]{:S(2)}, u32[]{:S(2)}) collective-permute-start(bf16[64,256]{1,0:T(8,128)(2,1)S(1)} %get-tuple-element.36), channel_id=1, source_target_pairs={{4,0},{0,1},{6,2},{2,3},{8,4},{1,5},{10,6},{3,7},{12,8},{5,9},{14,... | collective-permute-start | bytes 98312 | tf_op jit(solution)/shard_map/ppermute | solution.py:473
  10.6 1.4 %collective-permute-start.2 = (bf16[576,128]{1,0:T(8,128)(2,1)S(1)}, bf16[576,128]{1,0:T(8,128)(2,1)S(1)}, u32[]{:S(2)}, u32[]{:S(2)}) collective-permute-start(bf16[576,128]{1,0:T(8,128)(2,1)S(1)} %get-tuple-element.51), channel_id=1, source_target_pairs={{0,1},{1,0},{2,3},{3,2},{4,5},{5,4},{6,7},{7,6},{8,9},{9,8},{10,11... | collective-permute-start | bytes 442376 | tf_op jit(solution)/shard_map/ppermute | solution.py:516
  12.0 4.3 %collective-permute-start.5 = (bf16[448,128]{1,0:T(8,128)(2,1)S(1)}, bf16[448,128]{1,0:T(8,128)(2,1)S(1)}, u32[]{:S(2)}, u32[]{:S(2)}) collective-permute-start(bf16[448,128]{1,0:T(8,128)(2,1)S(1)} %get-tuple-element.52.after_ref.mine_ref), channel_id=1, source_target_pairs={{0,3},{1,16},{2,19},{3,0},{4,21},{5,6},{6,5},{7,22},{8,25},{9,10},... | collective-permute-start | bytes 344072 | tf_op jit(solution)/shard_map/ppermute | solution.py:536
  16.4 5.3 %collective-permute-start.6 = (bf16[448,128]{1,0:T(8,128)(2,1)S(1)}, bf16[448,128]{1,0:T(8,128)(2,1)S(1)}, u32[]{:S(2)}, u32[]{:S(2)}) collective-permute-start(bf16[448,128]{1,0:T(8,128)(2,1)S(1)} %shard_map.99.mine_ref), channel_id=1, source_target_pairs={{0,17},{1,4},{2,7},{3,18},{4,1},{5,20},{6,23},{7,2},{8,13},{9,24},... | collective-permute-start | bytes 344072 | tf_op jit(solution)/shard_map/ppermute | solution.py:536
  19.2 6.2 %collective-permute-start.3 = (bf16[128,256]{1,0:T(8,128)(2,1)S(1)}, bf16[128,256]{1,0:T(8,128)(2,1)S(1)}, u32[]{:S(2)}, u32[]{:S(2)}) collective-permute-start(bf16[128,256]{1,0:T(8,128)(2,1)S(1)} %get-tuple-element.54), channel_id=1, source_target_pairs={{0,4},{1,0},{2,6},{3,2},{4,8},{5,1},{6,10},{7,3},{8,12},{9,5},{10,... | collective-permute-start | bytes 196616 | tf_op jit(solution)/shard_map/ppermute | solution.py:539
  21.7 6.2 %collective-permute-start.7 = (bf16[448,128]{1,0:T(8,128)(2,1)S(1)}, bf16[448,128]{1,0:T(8,128)(2,1)S(1)}, u32[]{:S(2)}, u32[]{:S(2)}) collective-permute-start(bf16[448,128]{1,0:T(8,128)(2,1)S(1)} %shard_map.100.mine_ref), channel_id=1, source_target_pairs={{0,5},{1,8},{2,11},{3,6},{4,13},{5,0},{6,3},{7,14},{8,1},{9,12},{1... | collective-permute-start | bytes 344072 | tf_op jit(solution)/shard_map/ppermute | solution.py:536
  25.4 1.3 %collective-permute-start.4 = (bf16[64,256]{1,0:T(8,128)(2,1)S(1)}, bf16[64,256]{1,0:T(8,128)(2,1)S(1)}, u32[]{:S(2)}, u32[]{:S(2)}) collective-permute-start(bf16[64,256]{1,0:T(8,128)(2,1)S(1)} %get-tuple-element.64), channel_id=1, source_target_pairs={{0,1},{1,0},{2,3},{3,2},{4,5},{5,4},{6,7},{7,6},{8,9},{9,8},{10,11... | collective-permute-start | bytes 98312 | tf_op jit(solution)/shard_map/ppermute | solution.py:556
  27.9 4.3 %collective-permute-start.8 = (bf16[448,128]{1,0:T(8,128)(2,1)S(1)}, bf16[448,128]{1,0:T(8,128)(2,1)S(1)}, u32[]{:S(2)}, u32[]{:S(2)}) collective-permute-start(bf16[448,128]{1,0:T(8,128)(2,1)S(1)} %shard_map.101.after_ref.mine_ref), channel_id=1, source_target_pairs={{0,9},{1,2},{2,1},{3,10},{4,7},{5,12},{6,15},{7,4},{8,11},{9,0},{1... | collective-permute-start | bytes 344072 | tf_op jit(solution)/shard_map/ppermute | solution.py:536
  32.2 1.6 %collective-permute-start.9 = (f32[448,128]{1,0:T(8,128)S(1)}, f32[448,128]{1,0:T(8,128)S(1)}, u32[]{:S(2)}, u32[]{:S(2)}) collective-permute-start(f32[448,128]{1,0:T(8,128)S(1)} %shard_map.103.source_ref), channel_id=1, source_target_pairs={{0,1},{1,0},{2,3},{3,2},{4,5},{5,4},{6,7},{7,6},{8,9},{9,8},{10,11... | collective-permute-start | bytes 688136 | tf_op jit(solution)/shard_map/ppermute | solution.py:575

commit v8 on v7

--- a/solution.py
+++ b/solution.py
@@ -98,20 +98,6 @@
     return lax.dot_general(x, y, (((1,), (1,)), ((), ())), preferred_element_type=F32)
 
 
-def store_faces(core_ref, low, high, first_ref, second_ref):
-    even = core_ref[0] == 0
-
-    @pl.when(even)
-    def _():
-        first_ref[...] = high
-        second_ref[...] = low
-
-    @pl.when(jnp.logical_not(even))
-    def _():
-        first_ref[...] = low
-        second_ref[...] = high
-
-
 def load_faces(core_ref, first_ref, second_ref):
     even = core_ref[0] == 0
     first, second = first_ref[...].astype(F32), second_ref[...].astype(F32)
@@ -119,10 +105,13 @@
 
 
 def stage_kernel(
-    core_ref, feats_ref, occ_ref, near_ref, first_ref, second_ref, rows_ref, x_ref, keep_ref,
-    near_held_ref, sems,
-):
-    pairs = ((near_ref, near_held_ref), (occ_ref, keep_ref), (feats_ref, x_ref))
+    core_ref, feats_ref, occ_ref, near_ref, cot_from_ref, weight_from_ref, bias_from_ref,
+    first_ref, rows_ref, x_ref, keep_ref, cot_ref, weight_ref, bias_ref, near_held_ref, sems,
+):
+    pairs = (
+        (near_ref, near_held_ref), (occ_ref, keep_ref), (feats_ref, x_ref), (cot_from_ref, cot_ref),
+        (weight_from_ref, weight_ref), (bias_from_ref, bias_ref),
+    )
     copies = [pltpu.make_async_copy(a, b, sems.at[i]) for i, (a, b) in enumerate(pairs)]
     for copy in copies:
         copy.start()
@@ -136,8 +125,26 @@
     for i, start in enumerate((0, voxels - 128)):
         at = slice(start, start + 128)
         tiles = [x_ref[m, :, at].astype(F32) * keep[m : m + 1, at] for m in range(bricks)]
-        faces.append(to_planes(tiles)[i].astype(BF))
-    store_faces(core_ref, faces[0], faces[1], first_ref, second_ref)
+        faces.append(to_planes(tiles)[i])
+    first_ref[...] = jnp.where(core_ref[0] == 0, faces[1], faces[0]).astype(BF)
+    for copy in copies[3:]:
+        copy.wait()
+
+
+def planes_kernel(core_ref, feats_ref, occ_ref, planes_ref, occ2_ref, second_ref):
+    bricks, channels, voxels = feats_ref.shape
+    keep = occ_ref[...].astype(F32)
+    for t in range(voxels // 128):
+        at = slice(128 * t, 128 * t + 128)
+        kept = [jnp.broadcast_to(keep[m : m + 1, at], (channels, 128)) for m in range(bricks)]
+        first, second = to_planes([feats_ref[m, :, at].astype(F32) * kept[m] for m in range(bricks)])
+        planes_ref[2 * t] = first.astype(BF)
+        planes_ref[2 * t + 1] = second.astype(BF)
+        first, second = to_planes([kept[m][:8] for m in range(bricks)])
+        occ2_ref[2 * t] = first
+        occ2_ref[2 * t + 1] = second
+    low, high = planes_ref[0].astype(F32), planes_ref[planes_ref.shape[0] - 1].astype(F32)
+    second_ref[...] = jnp.where(core_ref[0] == 0, low, high).astype(BF)
 
 
 def ahead_weights(weight_ref, ahead_ref):
@@ -154,10 +161,9 @@
         back_ref[channels * r : channels * (r + 1), :] = jnp.concatenate(blocks, axis=1).astype(BF)
 
 
-def shifted(planes_ref, moved_ref, rows_ref, bricks, channels):
+def shifted(flat, moved_ref, rows_ref, bricks, channels):
     rows = slot_rows(rows_ref, 0)
-    count = planes_ref.shape[0]
-    flat = planes_ref[...].reshape(count * channels, bricks * PLANE)
+    count = moved_ref.shape[0]
     for b in range(3):
         for c in range(3):
             k = 3 * b + c
@@ -180,8 +186,7 @@
             total_ref[at, :] += dot(weight_ref[...], moved_ref[x])
 
 
-def shifted_face(face, rows_ref, dx, bricks):
-    rows = slot_rows(rows_ref, dx)
+def shifted_face(face, rows, bricks):
     parts = []
     for b in range(3):
         for c in range(3):
@@ -189,29 +194,19 @@
     return jnp.concatenate(parts, axis=0)
 
 
+def side_rows(rows_ref, low):
+    below, above = slot_rows(rows_ref, -1), slot_rows(rows_ref, 1)
+    return {key: jnp.where(low, below[key], above[key]) for key in below}
+
+
 def inner_kernel(
-    core_ref, rows_ref, feats_ref, occ_ref, cot_from_ref, weight_from_ref, bias_from_ref,
-    moved_ref, pre_ref, cot2_ref, occ2_ref, ahead_ref, cot_ref, weight_ref,
-    planes_ref, total_ref, bias_ref, sems,
-):
-    bricks, channels, voxels = feats_ref.shape
-    pairs = ((cot_from_ref, cot_ref), (weight_from_ref, weight_ref), (bias_from_ref, bias_ref))
-    copies = [pltpu.make_async_copy(a, b, sems.at[i]) for i, (a, b) in enumerate(pairs)]
-    for copy in copies:
-        copy.start()
+    core_ref, rows_ref, planes_ref, occ_ref, cot_ref, weight_ref, bias_ref,
+    moved_ref, pre_ref, cot2_ref, ahead_ref, total_ref,
+):
+    bricks, channels, voxels = cot_ref.shape
+    flat = planes_ref[...].reshape(planes_ref.shape[0] * channels, bricks * PLANE)
+    shifted(flat, moved_ref, rows_ref, bricks, channels)
     keep = occ_ref[...].astype(F32)
-    for t in range(voxels // 128):
-        at = slice(128 * t, 128 * t + 128)
-        kept = [jnp.broadcast_to(keep[m : m + 1, at], (channels, 128)) for m in range(bricks)]
-        first, second = to_planes([feats_ref[m, :, at].astype(F32) * kept[m] for m in range(bricks)])
-        planes_ref[2 * t] = first.astype(BF)
-        planes_ref[2 * t + 1] = second.astype(BF)
-        first, second = to_planes([kept[m][:8] for m in range(bricks)])
-        occ2_ref[2 * t] = first
-        occ2_ref[2 * t + 1] = second
-    shifted(planes_ref, moved_ref, rows_ref, bricks, channels)
-    for copy in copies:
-        copy.wait()
     for t in range(voxels // 128):
         at = slice(128 * t, 128 * t + 128)
         kept = [jnp.broadcast_to(keep[m : m + 1, at], (channels, 128)) for m in range(bricks)]
@@ -230,16 +225,16 @@
     pre_ref[...] = total_ref[channels : channels * (count + 1), :].reshape(pre_ref.shape)
 
 
-def half_terms(padded_ref, moved_ref, low_ref, high_ref, start, half):
-    count, channels = moved_ref.shape[0], padded_ref.shape[0] // (moved_ref.shape[0] + 4)
-
-    def rows(x):
-        return padded_ref[pl.ds(pl.multiple_of(channels * (x + 1) + start, 32), half), :]
-
-    terms = dot_t(rows(-1), low_ref[...])
-    for x in range(count):
-        terms = terms + dot_t(rows(x), moved_ref[x])
-    return terms + dot_t(rows(count), high_ref[...])
+def terms_of(padded_ref, x, start, half, moved):
+    channels = moved.shape[0] // 9
+    rows = pl.ds(pl.multiple_of(channels * (x + 1) + start, 32), half)
+    return dot_t(padded_ref[rows, :], moved)
+
+
+def activate(pre, masked, cot, keep):
+    sig = jax.nn.sigmoid(pre)
+    result = (masked + keep * pre * sig).astype(BF)
+    return result, (cot * sig * (1.0 + pre * (1.0 - sig))).astype(BF)
 
 
 def store_terms(terms, copies_ref, start, out_ref):
@@ -257,55 +252,96 @@
     out_ref[at + unit : at + 2 * unit, :] = two.astype(out_ref.dtype)
 
 
-def outer_kernel(
-    core_ref, own_ref, rows_ref, first_ref, second_ref, moved_ref, pre_ref, cot2_ref, occ2_ref,
-    weight_ref,
-    result_ref, grad_ref, theirs_ref, padded_ref, moved_low_ref, moved_high_ref, copies_ref,
+def first_outer_kernel(
+    core_ref, own_ref, rows_ref, face_ref, moved_ref, pre_ref, cot2_ref, occ2_ref, weight_ref,
+    result_ref, padded_ref, face_moved_ref, partial_ref, bias_ref,
 ):
     count, channels, lanes = pre_ref.shape
     bricks = lanes // PLANE
-    low, high = load_faces(core_ref, first_ref, second_ref)
-    moved_low_ref[...] = shifted_face(low, rows_ref, -1, bricks)
-    moved_high_ref[...] = shifted_face(high, rows_ref, 1, bricks)
-    add_low = dot(weight_ref[2 * channels : 3 * channels, :], moved_low_ref[...])
-    add_high = dot(weight_ref[0:channels, :], moved_high_ref[...])
+    even = core_ref[0] == 0
+    face_moved_ref[...] = shifted_face(face_ref[...], side_rows(rows_ref, even), bricks)
+    at = pl.multiple_of(jnp.where(even, 2 * channels, 0), channels)
+    add = dot(weight_ref[pl.ds(at, channels), :], face_moved_ref[...])
     padded_ref[0 : 2 * channels, :] = jnp.zeros((2 * channels, lanes), BF)
     padded_ref[channels * (count + 2) :, :] = jnp.zeros((2 * channels, lanes), BF)
     bias = jnp.zeros((channels, lanes), F32)
     for x in range(count):
         pre = pre_ref[x]
-        if x == 0:
-            pre = pre + add_low
-        if x == count - 1:
-            pre = pre + add_high
+        if x in (0, count - 1):
+            pre = pre + add
         keep = jnp.broadcast_to(occ2_ref[x][0:1], (channels, lanes))
-        sig = jax.nn.sigmoid(pre)
         masked = moved_ref[x, 4 * channels : 5 * channels, :].astype(F32)
-        result_ref[x] = (masked + keep * pre * sig).astype(BF)
-        grad = (cot2_ref[x].astype(F32) * sig * (1.0 + pre * (1.0 - sig))).astype(BF)
-        grad_ref[x] = grad
+        result, grad = activate(pre, masked, cot2_ref[x].astype(F32), keep)
+        if x in (0, count - 1):
+            there = even if x == 0 else jnp.logical_not(even)
+            grad = jnp.where(there, grad.astype(F32), 0.0).astype(BF)
+        result_ref[x] = result
         padded_ref[channels * (x + 2) : channels * (x + 3), :] = grad
         bias = bias + grad.astype(F32)
-    at = (channels, channels)
-    same = lax.broadcasted_iota(jnp.int32, at, 0) == lax.broadcasted_iota(jnp.int32, at, 1)
-    row = jnp.sum(jnp.where(same, jnp.sum(bias, axis=1, keepdims=True), 0.0), axis=0, keepdims=True)
+    bias_ref[...] = bias
+    half = partial_ref.shape[0]
+    start = (1 - own_ref[0]) * half
+    terms = terms_of(padded_ref, jnp.where(even, -1, count), start, half, face_moved_ref[...])
+    for x in range(count):
+        terms = terms + terms_of(padded_ref, x, start, half, moved_ref[x])
+    partial_ref[...] = terms
+
+
+def second_outer_kernel(
+    core_ref, own_ref, rows_ref, face_ref, moved_ref, pre_ref, cot2_ref, occ2_ref, weight_ref,
+    begun_ref, partial_ref, bias_ref,
+    result_ref, padded_ref, face_moved_ref, theirs_ref, copies_ref,
+    late_ref,
+):
+    count, channels, lanes = pre_ref.shape
+    bricks = lanes // PLANE
+    even = core_ref[0] == 0
+    plane = jnp.where(even, count - 1, 0)
+    inward = jnp.where(even, -1, 1)
+    face_moved_ref[...] = shifted_face(
+        face_ref[...], side_rows(rows_ref, jnp.logical_not(even)), bricks
+    )
+    at = pl.multiple_of(jnp.where(even, 0, 2 * channels), channels)
+    add = dot(weight_ref[pl.ds(at, channels), :], face_moved_ref[...])
+    keep = jnp.broadcast_to(occ2_ref[plane][0:1], (channels, lanes))
+    masked = moved_ref[plane, 4 * channels : 5 * channels, :].astype(F32)
+    cot = cot2_ref[plane].astype(F32)
+    result, grad = activate(pre_ref[plane] + add, masked, cot, keep)
+    result_ref[...] = result
+    padded_ref[...] = begun_ref[...]
+    padded_ref[pl.ds(pl.multiple_of(channels * (plane + 2), channels), channels), :] = grad
+    late_ref[...] = jnp.zeros(late_ref.shape, BF)
+    late_ref[2 * channels : 3 * channels, :] = grad
+    same = lax.broadcasted_iota(jnp.int32, (channels, channels), 0)
+    same = same == lax.broadcasted_iota(jnp.int32, (channels, channels), 1)
+    bias = jnp.sum(bias_ref[...] + grad.astype(F32), axis=1, keepdims=True)
+    row = jnp.sum(jnp.where(same, bias, 0.0), axis=0, keepdims=True)
     copies_ref[...] = row * spread(copies_ref.shape)
-    half = 3 * channels // 2
+    half = partial_ref.shape[0]
     start = (1 - own_ref[0]) * half
-    terms = half_terms(padded_ref, moved_ref, moved_low_ref, moved_high_ref, start, half)
+    terms = partial_ref[...] + terms_of(late_ref, -inward, start, half, face_moved_ref[...])
+    terms = terms + terms_of(late_ref, 0, start, half, moved_ref[plane])
+    terms = terms + terms_of(late_ref, inward, start, half, moved_ref[plane + inward])
     store_terms(terms, copies_ref, start, theirs_ref)
-    even = core_ref[0] == 0
-    low, high = grad_ref[0].astype(F32), grad_ref[count - 1].astype(F32)
+    low = padded_ref[2 * channels : 3 * channels, :].astype(F32)
+    high = padded_ref[channels * (count + 1) : channels * (count + 2), :].astype(F32)
     face = jnp.where(even, low, high).astype(BF)
     size = theirs_ref.shape[0] - channels * (lanes // 128)
     for t in range(lanes // 128):
         theirs_ref[size + channels * t : size + channels * (t + 1), :] = face[:, 128 * t : 128 * t + 128]
 
 
-def own_kernel(own_ref, padded_ref, moved_ref, low_ref, high_ref, copies_ref, mine_ref):
+def own_kernel(
+    core_ref, own_ref, padded_ref, moved_ref, first_ref, second_ref, copies_ref, mine_ref
+):
+    count = moved_ref.shape[0]
     half = 3 * copies_ref.shape[1] // 2
     start = own_ref[0] * half
-    terms = half_terms(padded_ref, moved_ref, low_ref, high_ref, start, half)
+    even = core_ref[0] == 0
+    terms = terms_of(padded_ref, jnp.where(even, -1, count), start, half, first_ref[...])
+    for x in range(count):
+        terms = terms + terms_of(padded_ref, x, start, half, moved_ref[x])
+    terms = terms + terms_of(padded_ref, jnp.where(even, count, -1), start, half, second_ref[...])
     store_terms(terms, copies_ref, start, mine_ref)
 
 
@@ -313,12 +349,14 @@
     return 1.0 + lax.broadcasted_iota(jnp.int32, shape, 0).astype(F32) * (1.0 / shape[0])
 
 
-def first_sum_kernel(core_ref, mine_ref, other_ref, grad_ref, out_ref, faces_ref):
+def first_sum_kernel(core_ref, mine_ref, other_ref, padded_ref, out_ref, faces_ref):
     size = mine_ref.shape[0]
     out_ref[...] = (mine_ref[...] + other_ref[0:size, :].astype(F32)).astype(BF)
-    count, channels, lanes = grad_ref.shape
+    channels, lanes = faces_ref.shape[0] // 2, faces_ref.shape[1]
+    end = padded_ref.shape[0] - 2 * channels
     even = core_ref[0] == 0
-    low, high = grad_ref[0].astype(F32), grad_ref[count - 1].astype(F32)
+    low = padded_ref[2 * channels : 3 * channels, :].astype(F32)
+    high = padded_ref[end - channels : end, :].astype(F32)
     faces_ref[0:channels, :] = jnp.where(even, high, low).astype(BF)
     for t in range(lanes // 128):
         rows = slice(size + channels * t, size + channels * (t + 1))
@@ -331,17 +369,25 @@
 
 
 def back_inner_kernel(
-    core_ref, rows_ref, grad_ref, result2_ref, weight_ref, after_ref,
+    core_ref, rows_ref, padded_ref, result2_ref, late_ref, weight_ref, after_ref,
     result_ref, total_ref, back_ref, moved_ref,
 ):
-    count, channels, lanes = grad_ref.shape
+    count, channels, lanes = result2_ref.shape
     bricks = lanes // PLANE
     back_weights(weight_ref, back_ref)
-    shifted(grad_ref, moved_ref, rows_ref, bricks, channels)
+    flat = padded_ref[2 * channels : channels * (count + 2), :]
+    shifted(flat, moved_ref, rows_ref, bricks, channels)
     total_ref[...] = jnp.zeros(total_ref.shape, F32)
     add_products(core_ref, back_ref, moved_ref, total_ref)
+    even = core_ref[0] == 0
+    late = late_ref[...].astype(F32)
     for t in range(count // 2):
-        out = from_planes(result2_ref[2 * t].astype(F32), result2_ref[2 * t + 1].astype(F32))
+        first, second = result2_ref[2 * t].astype(F32), result2_ref[2 * t + 1].astype(F32)
+        if t == 0:
+            first = jnp.where(even, first, late)
+        if t == count // 2 - 1:
+            second = jnp.where(even, late, second)
+        out = from_planes(first, second)
         for m in range(bricks):
             result_ref[m, :, 128 * t : 128 * t + 128] = out[m].astype(BF)
 
@@ -354,8 +400,8 @@
     count = voxels // PLANE
     done_ref[...] = jnp.zeros(done_ref.shape, F32)
     low, high = load_faces(core_ref, first_ref, second_ref)
-    moved_low = shifted_face(low, rows_ref, -1, bricks)
-    moved_high = shifted_face(high, rows_ref, 1, bricks)
+    moved_low = shifted_face(low, slot_rows(rows_ref, -1), bricks)
+    moved_high = shifted_face(high, slot_rows(rows_ref, 1), bricks)
     add_low = dot(weight_ref[2 * channels : 3 * channels, :], moved_low)
     add_high = dot(weight_ref[0:channels, :], moved_high)
     keep = occ_ref[...].astype(F32)
@@ -461,56 +507,73 @@
     plane = ((channels, lanes), BF)
     core = (lax.axis_index("rep") % 2).astype(jnp.int32)
     cores = core[None]
-    first, second, rows, x, occ = call(
+    first, rows, x, occ, cot, weight, bias = call(
         stage_kernel,
-        [plane, plane, ((32, lanes), jnp.int32), (x.shape, BF), (occ.shape, jnp.int32)],
-        [(SMEM, cores), (HBM, x), (HBM, occ), (HBM, near)],
-        [pltpu.SMEM(near.shape, jnp.int32), pltpu.SemaphoreType.DMA((3,))],
+        [
+            plane, ((32, lanes), jnp.int32), (x.shape, BF), (occ.shape, jnp.int32), (x.shape, BF),
+            (weight.shape, BF), ((1, channels), F32),
+        ],
+        [
+            (SMEM, cores), (HBM, x), (HBM, occ), (HBM, near), (HBM, cot), (HBM, weight),
+            (HBM, bias[None]),
+        ],
+        [pltpu.SMEM(near.shape, jnp.int32), pltpu.SemaphoreType.DMA((6,))],
     )
     axes = ("space", "rep")
     pairs = face_pairs()
     first = lax.ppermute(first, axes, pairs)
+    planes, occ2, second = call(
+        planes_kernel,
+        [((count, channels, lanes), BF), ((count, 8, lanes), F32), plane],
+        [(SMEM, cores), (VMEM, x), (VMEM, occ)],
+    )
     second = lax.ppermute(second, axes, [(j, i) for i, j in pairs])
-    moved, pre, cot2, occ2, ahead, cot, weight = call(
+    moved, pre, cot2, ahead = call(
         inner_kernel,
         [
             ((count, width, lanes), BF),
             ((count, channels, lanes), F32),
             ((count, channels, lanes), BF),
-            ((count, 8, lanes), F32),
             ((3 * channels, width), BF),
-            (cot.shape, BF),
-            (weight.shape, BF),
         ],
-        [(SMEM, cores), (VMEM, rows), (VMEM, x), (VMEM, occ), (HBM, cot), (HBM, weight), (HBM, bias[None])],
         [
-            pltpu.VMEM((count, channels, lanes), BF),
-            pltpu.VMEM((channels * (count + 2), lanes), F32),
-            pltpu.VMEM((1, channels), F32),
-            pltpu.SemaphoreType.DMA((3,)),
+            (SMEM, cores), (VMEM, rows), (VMEM, planes), (VMEM, occ), (VMEM, cot), (VMEM, weight),
+            (VMEM, bias),
         ],
+        [pltpu.VMEM((channels * (count + 2), lanes), F32)],
         flops=2 * 27 * channels * channels * bricks * voxels,
     )
     devices = lax.axis_size("space") * lax.axis_size("rep")
     me = lax.axis_index("space") * lax.axis_size("rep") + lax.axis_index("rep")
     own = (lax.population_count(me.astype(jnp.int32)) & 1)[None]
     size = 3 * channels // 2 * (width // 128) + channels
-    result2, grad, theirs, padded, moved_low, moved_high, copies = call(
-        outer_kernel,
+    field = [(VMEM, moved), (VMEM, pre), (VMEM, cot2), (VMEM, occ2), (VMEM, ahead)]
+    result2, begun, moved_first, partial, bias_part = call(
+        first_outer_kernel,
         [
             ((count, channels, lanes), BF),
-            ((count, channels, lanes), BF),
-            ((size + channels * lanes // 128, 128), BF),
             ((channels * (count + 4), lanes), BF),
             ((width, lanes), BF),
+            ((3 * channels // 2, width), F32),
+            ((channels, lanes), F32),
+        ],
+        [(SMEM, cores), (SMEM, own), (VMEM, rows), (VMEM, first)] + field,
+        flops=14 * channels * channels * bricks * voxels,
+    )
+    late, padded, moved_second, theirs, copies = call(
+        second_outer_kernel,
+        [
+            plane,
+            ((channels * (count + 4), lanes), BF),
             ((width, lanes), BF),
+            ((size + channels * lanes // 128, 128), BF),
             ((channels // 2, channels), F32),
         ],
-        [
-            (SMEM, cores), (SMEM, own), (VMEM, rows), (VMEM, first), (VMEM, second), (VMEM, moved),
-            (VMEM, pre), (VMEM, cot2), (VMEM, occ2), (VMEM, ahead),
-        ],
-        flops=2 * 27 * channels * channels * bricks * voxels,
+        [(SMEM, cores), (SMEM, own), (VMEM, rows), (VMEM, second)]
+        + field
+        + [(VMEM, begun), (VMEM, partial), (VMEM, bias_part)],
+        [pltpu.VMEM((5 * channels, lanes), BF)],
+        flops=14 * channels * channels * bricks * voxels,
     )
     partner = [(i, i ^ 1) for i in range(devices)]
     other = lax.ppermute(theirs, axes, partner)
@@ -518,8 +581,8 @@
         own_kernel,
         [((size, 128), F32)],
         [
-            (SMEM, own), (VMEM, padded), (VMEM, moved), (VMEM, moved_low), (VMEM, moved_high),
-            (VMEM, copies),
+            (SMEM, cores), (SMEM, own), (VMEM, padded), (VMEM, moved), (VMEM, moved_first),
+            (VMEM, moved_second), (VMEM, copies),
         ],
         flops=27 * channels * channels * bricks * voxels,
     )
@@ -527,7 +590,7 @@
     mine, faces = call(
         first_sum_kernel,
         [sent, ((2 * channels, lanes), BF)],
-        [(SMEM, cores), (VMEM, mine), (VMEM, other), (VMEM, grad)],
+        [(SMEM, cores), (VMEM, mine), (VMEM, other), (VMEM, padded)],
     )
     bits = [1 << i for i in range(1, (devices).bit_length() - 1)]
     rounds = list(zip(bits[:1] + bits[-1:] + bits[1:-1], bits[-1:] + bits[1:-1] + bits[:1]))
@@ -545,8 +608,8 @@
                     ((3 * channels, width), BF),
                 ],
                 [
-                    (SMEM, cores), (VMEM, rows), (VMEM, grad), (VMEM, result2), (VMEM, weight),
-                    (ANY, mine),
+                    (SMEM, cores), (VMEM, rows), (VMEM, padded), (VMEM, result2), (VMEM, late),
+                    (VMEM, weight), (ANY, mine),
                 ],
                 [pltpu.VMEM((count, width, lanes), BF)],
                 flops=2 * 27 * channels * channels * bricks * voxels,

time: 34.8 us -> 34.5 us (level)
  waiting for transfers between devices: 8.94 us -> 7.35 us
  starting transfers between devices: 12.8 us -> 13.7 us
    ppermute x1, waiting for transfers between devices: 1.71 us -> 0.66 us  [on_device(): second = lax.ppermute(second, axes, [(j, i) for i, j in pairs])]
    ppermute x1, starting transfers between devices: 0.23 us -> 0.73 us  [on_device(): other = lax.ppermute(mine, axes, partner)]
    ppermute x4, starting transfers between devices: 8.32 us -> 8.73 us  [on_device(): other = lax.ppermute(mine, axes, joined)]
    ppermute x4, waiting for transfers between devices: 5.28 us -> 4.93 us  [on_device(): other = lax.ppermute(mine, axes, joined)]
    pallas_call x13 -> x15, Pallas kernels: 12.2 us -> 12.5 us  [call(): pl.pallas_call(body, out_shape=shapes, in_specs=[spec for spec, _ in ins]...]
  transfers between devices with their start and end apart: 10 -> 10, of which waited for: 8 -> 8; matrix products, arithmetic and copies ran while one was open for 0% -> 0% of each run, Pallas kernels for 23% -> 27%
where the time goes in v8:
time: 34.5 us; the launch traced here: 34.3 us
  starting transfers between devices  13.7 us (40%)
  Pallas kernels  12.5 us (36%)
  waiting for transfers between devices  7.35 us (21%)
  between operations  0.75 us (2%)
    pallas_call x15, Pallas kernels, call(): pl.pallas_call(body, out_shape=shapes, in_specs=[spec for spec, _ in ins]...  12.5 us
    ppermute x4, starting transfers between devices, on_device(): other = lax.ppermute(mine, axes, joined)  8.73 us
    ppermute x4, waiting for transfers between devices, on_device(): other = lax.ppermute(mine, axes, joined)  4.93 us
    ppermute x1, starting transfers between devices, on_device(): first = lax.ppermute(first, axes, pairs)  3 us
    ppermute x1, waiting for transfers between devices, on_device(): lax.ppermute(faces[channels:], axes, partner)  1.19 us
    ppermute x1, starting transfers between devices, on_device(): faces = lax.ppermute(faces, axes, pairs)  1.14 us
    ppermute x1, starting transfers between devices, on_device(): other = lax.ppermute(mine, axes, partner)  0.73 us
  transfers between devices with their start and end apart: 10, of which 8 were waited for; matrix products, arithmetic and copies ran while one was open for 0% of the time, Pallas kernels for 27%

profile of v8, /device:TPU:0, one launch (start us, length us, event | category | flops | bytes accessed | tf_op | source)
XLA Modules:
  0.0 34.3 jit_solution(16211756733200698379)
XLA Ops:
  0.6 1.2 %shard_map.93 = (bf16[64,256]{1,0:T(8,128)(2,1)S(1)}, s32[32,256]{1,0:T(8,128)S(1)}, bf16[4,64,512]{2,1,0:T(8,128)(2,1)S(1)}, s32[4,512]{1,0:T(4,128)S(1)}, bf16...) custom-call(s32[1]{0:T(128)} %bitcast.core_ref, bf16[4,64,512]{2,1,0:T(8,128)(2,1)} %bitcast.10, ...), custom_call_target="tpu_custom_call" | custom-call | bytes 1573796 | tf_op jit(solution)/shard_map/pallas_call | solution.py:477
  1.9 3.0 %collective-permute-start.1 = (bf16[64,256]{1,0:T(8,128)(2,1)S(1)}, bf16[64,256]{1,0:T(8,128)(2,1)S(1)}, u32[]{:S(2)}, u32[]{:S(2)}) collective-permute-start(bf16[64,256]{1,0:T(8,128)(2,1)S(1)} %get-tuple-element.52), channel_id=1, source_target_pairs={{0,4},{1,0},{2,6},{3,2},{4,8},{5,1},{6,10},{7,3},{8,12},{9,5},{10,... | collective-permute-start | bytes 98312 | tf_op jit(solution)/shard_map/ppermute | solution.py:524
  5.1 1.5 %shard_map.95 = (bf16[8,576,256]{2,1,0:T(8,128)(2,1)S(1)}, f32[8,64,256]{2,1,0:T(8,128)S(1)}, bf16[8,64,256]{2,1,0:T(8,128)(2,1)S(1)}, bf16[192,576]{1,0:T(8,128)(2,1)S(1)}) custom-call(s32[1]{0:T(128)} %bitcast.core_ref, s32[32,256]{1,0:T(8,128)S(1)} %get-tuple-element.39.rows_ref, bf16[8,64,256]{2,1,0:T(8,128)(2,1)S(1)} %get-tuple-element.43.planes_ref, ...), custom_call_target="tpu_custom_call" | custom-call | flops 452984832 | bytes 4153604 | tf_op jit(solution)/shard_map/pallas_call | solution.py:477
  6.7 1.7 %shard_map.96 = (bf16[8,64,256]{2,1,0:T(8,128)(2,1)S(1)}, bf16[768,256]{1,0:T(8,128)(2,1)S(1)}, bf16[576,256]{1,0:T(8,128)(2,1)S(1)}, f32[96,576]{1,0:T(8,128)S(1)}, f32[64,256]{1,0:T(8,128)S(1)}) custom-call(s32[1]{0:T(128)} %bitcast.core_ref, s32[1]{0:T(128)} %bitcast.6.own_ref, s32[32,256]{1,0:T(8,128)S(1)} %get-tuple-element.39.rows_ref, ...), custom_call_target="tpu_custom_call" | custom-call | flops 117440512 | bytes 4734984 | tf_op jit(solution)/shard_map/pallas_call | solution.py:477
  8.4 0.7 %collective-permute-done.face_ref = bf16[64,256]{1,0:T(8,128)(2,1)S(1)} collective-permute-done((bf16[64,256]{1,0:T(8,128)(2,1)S(1)}, bf16[64,256]{1,0:T(8,128)(2,1)S(1)}, u32[]{:S(2)}, u32[]{:S(2)}) %collective-permute-start) | collective-permute-done | bytes 32800 | tf_op jit(solution)/shard_map/ppermute | solution.py:530
  9.0 1.0 %shard_map.97 = (bf16[64,256]{1,0:T(8,128)(2,1)S(1)}, bf16[768,256]{1,0:T(8,128)(2,1)S(1)}, bf16[576,256]{1,0:T(8,128)(2,1)S(1)}, bf16[576,128]{1,0:T(8,128)(2,1)S(1)}, f32[32,64]{1,0:T(8,128)S(1)}) custom-call(s32[1]{0:T(128)} %bitcast.core_ref, s32[1]{0:T(128)} %bitcast.6.own_ref, s32[32,256]{1,0:T(8,128)S(1)} %get-tuple-element.39.rows_ref, ...), custom_call_target="tpu_custom_call" | custom-call | flops 117440512 | bytes 5054472 | tf_op jit(solution)/shard_map/pallas_call | solution.py:477
  10.0 1.0 %shard_map.98.mine_ref = f32[448,128]{1,0:T(8,128)S(1)} custom-call(s32[1]{0:T(128)} %bitcast.core_ref, s32[1]{0:T(128)} %bitcast.6.own_ref, bf16[768,256]{1,0:T(8,128)(2,1)S(1)} %get-tuple-element.56.padded_ref, bf16[8,576,256]{2,1,0:T(8,128)(2,1)S(1)} %get-tuple-element.47.moved_ref, bf16[576,256]{1,0:T(8,128)(2,1)S(1)} %get-tuple-element.59.first_ref, ...), custom_call_target="tpu_custom_call" | custom-call | flops 226492416 | bytes 3579912 | tf_op jit(solution)/shard_map/pallas_call | solution.py:477
  11.1 0.3 collective-permute-done.2.other_ref
  11.4 1.4 %collective-permute-start.5 = (bf16[448,128]{1,0:T(8,128)(2,1)S(1)}, bf16[448,128]{1,0:T(8,128)(2,1)S(1)}, u32[]{:S(2)}, u32[]{:S(2)}) collective-permute-start(bf16[448,128]{1,0:T(8,128)(2,1)S(1)} %get-tuple-element.63.after_ref.mine_ref), channel_id=1, source_target_pairs={{0,3},{1,16},{2,19},{3,0},{4,21},{5,6},{6,5},{7,22},{8,25},{9,10},... | collective-permute-start | bytes 344072 | tf_op jit(solution)/shard_map/ppermute | solution.py:599
  12.8 2.4 %shard_map.100 = (bf16[4,64,512]{2,1,0:T(8,128)(2,1)}, f32[640,256]{1,0:T(8,128)S(1)}, bf16[192,576]{1,0:T(8,128)(2,1)S(1)}) custom-call(s32[1]{0:T(128)} %bitcast.core_ref, s32[32,256]{1,0:T(8,128)S(1)} %get-tuple-element.39.rows_ref, bf16[768,256]{1,0:T(8,128)(2,1)S(1)} %get-tuple-element.56.padded_ref, ...), custom_call_target="tpu_custom_call" | custom-call | flops 452984832 | bytes 2195460 | tf_op jit(solution)/shard_map/pallas_call | solution.py:477
  15.2 0.5 %collective-permute-done.5.other_ref = bf16[448,128]{1,0:T(8,128)(2,1)S(1)} collective-permute-done((bf16[448,128]{1,0:T(8,128)(2,1)S(1)}, bf16[448,128]{1,0:T(8,128)(2,1)S(1)}, u32[]{:S(2)}, u32[]{:S(2)}) %collective-permute-start.5) | collective-permute-done | bytes 114720 | tf_op jit(solution)/shard_map/ppermute | solution.py:599
  15.7 3.8 %collective-permute-start.6 = (bf16[448,128]{1,0:T(8,128)(2,1)S(1)}, bf16[448,128]{1,0:T(8,128)(2,1)S(1)}, u32[]{:S(2)}, u32[]{:S(2)}) collective-permute-start(bf16[448,128]{1,0:T(8,128)(2,1)S(1)} %shard_map.101.mine_ref), channel_id=1, source_target_pairs={{0,17},{1,4},{2,7},{3,18},{4,1},{5,20},{6,23},{7,2},{8,13},{9,24},... | collective-permute-start | bytes 344072 | tf_op jit(solution)/shard_map/ppermute | solution.py:599
  19.5 1.1 %collective-permute-start.3 = (bf16[128,256]{1,0:T(8,128)(2,1)S(1)}, bf16[128,256]{1,0:T(8,128)(2,1)S(1)}, u32[]{:S(2)}, u32[]{:S(2)}) collective-permute-start(bf16[128,256]{1,0:T(8,128)(2,1)S(1)} %get-tuple-element.65), channel_id=1, source_target_pairs={{0,4},{1,0},{2,6},{3,2},{4,8},{5,1},{6,10},{7,3},{8,12},{9,5},{10,... | collective-permute-start | bytes 196616 | tf_op jit(solution)/shard_map/ppermute | solution.py:602
  20.7 1.3 %collective-permute-done.6.other_ref = bf16[448,128]{1,0:T(8,128)(2,1)S(1)} collective-permute-done((bf16[448,128]{1,0:T(8,128)(2,1)S(1)}, bf16[448,128]{1,0:T(8,128)(2,1)S(1)}, u32[]{:S(2)}, u32[]{:S(2)}) %collective-permute-start.6) | collective-permute-done | bytes 114720 | tf_op jit(solution)/shard_map/ppermute | solution.py:599
  22.0 2.7 %collective-permute-start.7 = (bf16[448,128]{1,0:T(8,128)(2,1)S(1)}, bf16[448,128]{1,0:T(8,128)(2,1)S(1)}, u32[]{:S(2)}, u32[]{:S(2)}) collective-permute-start(bf16[448,128]{1,0:T(8,128)(2,1)S(1)} %shard_map.102.mine_ref), channel_id=1, source_target_pairs={{0,5},{1,8},{2,11},{3,6},{4,13},{5,0},{6,3},{7,14},{8,1},{9,12},{1... | collective-permute-start | bytes 344072 | tf_op jit(solution)/shard_map/ppermute | solution.py:599
  24.9 1.2 %collective-permute-done.4.refs_0_.second_ref = bf16[64,256]{1,0:T(8,128)(2,1)S(1)} collective-permute-done((bf16[64,256]{1,0:T(8,128)(2,1)S(1)}, bf16[64,256]{1,0:T(8,128)(2,1)S(1)}, u32[]{:S(2)}, u32[]{:S(2)}) %collective-permute-start.4) | collective-permute-done | bytes 32800 | tf_op jit(solution)/shard_map/ppermute | solution.py:619
  26.1 1.2 %collective-permute-done.7.other_ref = bf16[448,128]{1,0:T(8,128)(2,1)S(1)} collective-permute-done((bf16[448,128]{1,0:T(8,128)(2,1)S(1)}, bf16[448,128]{1,0:T(8,128)(2,1)S(1)}, u32[]{:S(2)}, u32[]{:S(2)}) %collective-permute-start.7) | collective-permute-done | bytes 114720 | tf_op jit(solution)/shard_map/ppermute | solution.py:599
  27.3 0.8 %collective-permute-start.8 = (bf16[448,128]{1,0:T(8,128)(2,1)S(1)}, bf16[448,128]{1,0:T(8,128)(2,1)S(1)}, u32[]{:S(2)}, u32[]{:S(2)}) collective-permute-start(bf16[448,128]{1,0:T(8,128)(2,1)S(1)} %shard_map.103.after_ref.mine_ref), channel_id=1, source_target_pairs={{0,9},{1,2},{2,1},{3,10},{4,7},{5,12},{6,15},{7,4},{8,11},{9,0},{1... | collective-permute-start | bytes 344072 | tf_op jit(solution)/shard_map/ppermute | solution.py:599
  28.1 1.6 %shard_map.104 = (bf16[4,64,512]{2,1,0:T(8,128)(2,1)}, f32[8,128]{1,0:T(8,128)S(1)}) custom-call(s32[1]{0:T(128)} %bitcast.core_ref, s32[32,256]{1,0:T(8,128)S(1)} %get-tuple-element.39.rows_ref, bf16[64,256]{1,0:T(8,128)(2,1)S(1)} %get-tuple-element.75.first_ref, bf16[64,256]{1,0:T(8,128)(2,1)S(1)} %collective-permute-done.4.refs_0_.second_ref, ...), custom_call_target="tpu_custom_call" | custom-call | flops 100663296 | bytes 1626116 | tf_op jit(solution)/shard_map/pallas_call | solution.py:477
  29.7 1.9 %collective-permute-done.8.other_ref = bf16[448,128]{1,0:T(8,128)(2,1)S(1)} collective-permute-done((bf16[448,128]{1,0:T(8,128)(2,1)S(1)}, bf16[448,128]{1,0:T(8,128)(2,1)S(1)}, u32[]{:S(2)}, u32[]{:S(2)}) %collective-permute-start.8) | collective-permute-done | bytes 114720 | tf_op jit(solution)/shard_map/ppermute | solution.py:599
  31.6 0.7 %collective-permute-start.9 = (f32[448,128]{1,0:T(8,128)S(1)}, f32[448,128]{1,0:T(8,128)S(1)}, u32[]{:S(2)}, u32[]{:S(2)}) collective-permute-start(f32[448,128]{1,0:T(8,128)S(1)} %shard_map.105.source_ref), channel_id=1, source_target_pairs={{0,1},{1,0},{2,3},{3,2},{4,5},{5,4},{6,7},{7,6},{8,9},{9,8},{10,11... | collective-permute-start | bytes 688136 | tf_op jit(solution)/shard_map/ppermute | solution.py:638
  32.3 0.9 %shard_map.106 = (f32[27,64,64]{2,1,0:T(8,128)}, f32[1,64]{1,0:T(1,128)S(1)}) custom-call(s32[1]{0:T(128)} %bitcast.6.own_ref, f32[448,128]{1,0:T(8,128)S(1)} %shard_map.105.source_ref), custom_call_target="tpu_custom_call" | custom-call | bytes 672004 | tf_op jit(solution)/shard_map/pallas_call | solution.py:477
  33.2 0.2 collective-permute-done.9.source_ref
  33.4 0.9 %shard_map.107 = (f32[27,64,64]{2,1,0:T(8,128)}, f32[1,64]{1,0:T(1,128)}) custom-call(s32[1]{0:T(128)} %bitcast.6.own_ref, f32[448,128]{1,0:T(8,128)S(1)} %collective-permute-done.9.source_ref, f32[27,64,64]{2,1,0:T(8,128)} %get-tuple-element.70.begun_ref, f32[1,64]{1,0:T(1,128)S(1)} %get-tuple-element.71.own_bias_ref), custom_call_target="tpu_custom_call", output_to_operand_aliasing={{0}: (2, {})} | custom-call | bytes 1114628 | tf_op jit(solution)/shard_map/pallas_call | solution.py:477
  (12 shorter events, 0.5 us)
Async XLA Ops:
  1.9 4.8 %collective-permute-start.1 = (bf16[64,256]{1,0:T(8,128)(2,1)S(1)}, bf16[64,256]{1,0:T(8,128)(2,1)S(1)}, u32[]{:S(2)}, u32[]{:S(2)}) collective-permute-start(bf16[64,256]{1,0:T(8,128)(2,1)S(1)} %get-tuple-element.52), channel_id=1, source_target_pairs={{0,4},{1,0},{2,6},{3,2},{4,8},{5,1},{6,10},{7,3},{8,12},{9,5},{10,... | collective-permute-start | bytes 98312 | tf_op jit(solution)/shard_map/ppermute | solution.py:524
  5.1 4.0 %collective-permute-start = (bf16[64,256]{1,0:T(8,128)(2,1)S(1)}, bf16[64,256]{1,0:T(8,128)(2,1)S(1)}, u32[]{:S(2)}, u32[]{:S(2)}) collective-permute-start(bf16[64,256]{1,0:T(8,128)(2,1)S(1)} %get-tuple-element.42), channel_id=1, source_target_pairs={{4,0},{0,1},{6,2},{2,3},{8,4},{1,5},{10,6},{3,7},{12,8},{5,9},{14,... | collective-permute-start | bytes 98312 | tf_op jit(solution)/shard_map/ppermute | solution.py:530
  10.0 1.4 %collective-permute-start.2 = (bf16[576,128]{1,0:T(8,128)(2,1)S(1)}, bf16[576,128]{1,0:T(8,128)(2,1)S(1)}, u32[]{:S(2)}, u32[]{:S(2)}) collective-permute-start(bf16[576,128]{1,0:T(8,128)(2,1)S(1)} %get-tuple-element.62), channel_id=1, source_target_pairs={{0,1},{1,0},{2,3},{3,2},{4,5},{5,4},{6,7},{7,6},{8,9},{9,8},{10,11... | collective-permute-start | bytes 442376 | tf_op jit(solution)/shard_map/ppermute | solution.py:579
  11.4 4.3 %collective-permute-start.5 = (bf16[448,128]{1,0:T(8,128)(2,1)S(1)}, bf16[448,128]{1,0:T(8,128)(2,1)S(1)}, u32[]{:S(2)}, u32[]{:S(2)}) collective-permute-start(bf16[448,128]{1,0:T(8,128)(2,1)S(1)} %get-tuple-element.63.after_ref.mine_ref), channel_id=1, source_target_pairs={{0,3},{1,16},{2,19},{3,0},{4,21},{5,6},{6,5},{7,22},{8,25},{9,10},... | collective-permute-start | bytes 344072 | tf_op jit(solution)/shard_map/ppermute | solution.py:599
  15.7 6.3 %collective-permute-start.6 = (bf16[448,128]{1,0:T(8,128)(2,1)S(1)}, bf16[448,128]{1,0:T(8,128)(2,1)S(1)}, u32[]{:S(2)}, u32[]{:S(2)}) collective-permute-start(bf16[448,128]{1,0:T(8,128)(2,1)S(1)} %shard_map.101.mine_ref), channel_id=1, source_target_pairs={{0,17},{1,4},{2,7},{3,18},{4,1},{5,20},{6,23},{7,2},{8,13},{9,24},... | collective-permute-start | bytes 344072 | tf_op jit(solution)/shard_map/ppermute | solution.py:599
  19.5 5.2 %collective-permute-start.3 = (bf16[128,256]{1,0:T(8,128)(2,1)S(1)}, bf16[128,256]{1,0:T(8,128)(2,1)S(1)}, u32[]{:S(2)}, u32[]{:S(2)}) collective-permute-start(bf16[128,256]{1,0:T(8,128)(2,1)S(1)} %get-tuple-element.65), channel_id=1, source_target_pairs={{0,4},{1,0},{2,6},{3,2},{4,8},{5,1},{6,10},{7,3},{8,12},{9,5},{10,... | collective-permute-start | bytes 196616 | tf_op jit(solution)/shard_map/ppermute | solution.py:602
  22.0 5.2 %collective-permute-start.7 = (bf16[448,128]{1,0:T(8,128)(2,1)S(1)}, bf16[448,128]{1,0:T(8,128)(2,1)S(1)}, u32[]{:S(2)}, u32[]{:S(2)}) collective-permute-start(bf16[448,128]{1,0:T(8,128)(2,1)S(1)} %shard_map.102.mine_ref), channel_id=1, source_target_pairs={{0,5},{1,8},{2,11},{3,6},{4,13},{5,0},{6,3},{7,14},{8,1},{9,12},{1... | collective-permute-start | bytes 344072 | tf_op jit(solution)/shard_map/ppermute | solution.py:599
  24.8 1.3 %collective-permute-start.4 = (bf16[64,256]{1,0:T(8,128)(2,1)S(1)}, bf16[64,256]{1,0:T(8,128)(2,1)S(1)}, u32[]{:S(2)}, u32[]{:S(2)}) collective-permute-start(bf16[64,256]{1,0:T(8,128)(2,1)S(1)} %get-tuple-element.74), channel_id=1, source_target_pairs={{0,1},{1,0},{2,3},{3,2},{4,5},{5,4},{6,7},{7,6},{8,9},{9,8},{10,11... | collective-permute-start | bytes 98312 | tf_op jit(solution)/shard_map/ppermute | solution.py:619
  27.3 4.3 %collective-permute-start.8 = (bf16[448,128]{1,0:T(8,128)(2,1)S(1)}, bf16[448,128]{1,0:T(8,128)(2,1)S(1)}, u32[]{:S(2)}, u32[]{:S(2)}) collective-permute-start(bf16[448,128]{1,0:T(8,128)(2,1)S(1)} %shard_map.103.after_ref.mine_ref), channel_id=1, source_target_pairs={{0,9},{1,2},{2,1},{3,10},{4,7},{5,12},{6,15},{7,4},{8,11},{9,0},{1... | collective-permute-start | bytes 344072 | tf_op jit(solution)/shard_map/ppermute | solution.py:599
  31.6 1.8 %collective-permute-start.9 = (f32[448,128]{1,0:T(8,128)S(1)}, f32[448,128]{1,0:T(8,128)S(1)}, u32[]{:S(2)}, u32[]{:S(2)}) collective-permute-start(f32[448,128]{1,0:T(8,128)S(1)} %shard_map.105.source_ref), channel_id=1, source_target_pairs={{0,1},{1,0},{2,3},{3,2},{4,5},{5,4},{6,7},{7,6},{8,9},{9,8},{10,11... | collective-permute-start | bytes 688136 | tf_op jit(solution)/shard_map/ppermute | solution.py:638

commit v9 on v8

--- a/solution.py
+++ b/solution.py
@@ -593,7 +593,8 @@
         [(SMEM, cores), (VMEM, mine), (VMEM, other), (VMEM, padded)],
     )
     bits = [1 << i for i in range(1, (devices).bit_length() - 1)]
-    rounds = list(zip(bits[:1] + bits[-1:] + bits[1:-1], bits[-1:] + bits[1:-1] + bits[:1]))
+    order = bits[1:2] + bits[-1:] + bits[:1] + bits[2:-1]
+    rounds = list(zip(order, order[1:] + order[:1]))
     for i, steps in enumerate(rounds):
         joined = [(j, j ^ 1 ^ steps[j.bit_count() % 2]) for j in range(devices)]
         other = lax.ppermute(mine, axes, joined)

time: 34.5 us -> 34.1 us (0.988)
  waiting for transfers between devices: 7.35 us -> 5.84 us
  starting transfers between devices: 13.7 us -> 14.9 us
    ppermute x4, waiting for transfers between devices: 4.93 us -> 3.42 us  [on_device(): other = lax.ppermute(mine, axes, joined)]
    ppermute x1, starting transfers between devices: 1.14 us -> 2.16 us  [on_device(): faces = lax.ppermute(faces, axes, pairs)]
    ppermute x4, starting transfers between devices: 8.73 us -> 9.15 us  [on_device(): other = lax.ppermute(mine, axes, joined)]
where the time goes in v9:
time: 34.1 us; the launch traced here: 34 us
  starting transfers between devices  14.9 us (44%)
  Pallas kernels  12.5 us (37%)
  waiting for transfers between devices  5.84 us (17%)
  between operations  0.75 us (2%)
    pallas_call x15, Pallas kernels, call(): pl.pallas_call(body, out_shape=shapes, in_specs=[spec for spec, _ in ins]...  12.5 us
    ppermute x4, starting transfers between devices, on_device(): other = lax.ppermute(mine, axes, joined)  9.15 us
    ppermute x4, waiting for transfers between devices, on_device(): other = lax.ppermute(mine, axes, joined)  3.42 us
    ppermute x1, starting transfers between devices, on_device(): first = lax.ppermute(first, axes, pairs)  3 us
    ppermute x1, starting transfers between devices, on_device(): faces = lax.ppermute(faces, axes, pairs)  2.16 us
    ppermute x1, waiting for transfers between devices, on_device(): lax.ppermute(faces[channels:], axes, partner)  1.19 us
  transfers between devices with their start and end apart: 10, of which 8 were waited for; matrix products, arithmetic and copies ran while one was open for 0% of the time, Pallas kernels for 27%

profile of v9, /device:TPU:0, one launch (start us, length us, event | category | flops | bytes accessed | tf_op | source)
XLA Modules:
  0.0 34.0 jit_solution(11401087817953134754)
XLA Ops:
  0.6 1.2 %shard_map.93 = (bf16[64,256]{1,0:T(8,128)(2,1)S(1)}, s32[32,256]{1,0:T(8,128)S(1)}, bf16[4,64,512]{2,1,0:T(8,128)(2,1)S(1)}, s32[4,512]{1,0:T(4,128)S(1)}, bf16...) custom-call(s32[1]{0:T(128)} %bitcast.core_ref, bf16[4,64,512]{2,1,0:T(8,128)(2,1)} %bitcast.10, ...), custom_call_target="tpu_custom_call" | custom-call | bytes 1573796 | tf_op jit(solution)/shard_map/pallas_call | solution.py:477
  1.9 3.0 %collective-permute-start.1 = (bf16[64,256]{1,0:T(8,128)(2,1)S(1)}, bf16[64,256]{1,0:T(8,128)(2,1)S(1)}, u32[]{:S(2)}, u32[]{:S(2)}) collective-permute-start(bf16[64,256]{1,0:T(8,128)(2,1)S(1)} %get-tuple-element.52), channel_id=1, source_target_pairs={{0,4},{1,0},{2,6},{3,2},{4,8},{5,1},{6,10},{7,3},{8,12},{9,5},{10,... | collective-permute-start | bytes 98312 | tf_op jit(solution)/shard_map/ppermute | solution.py:524
  4.9 0.2 shard_map.94
  5.1 1.5 %shard_map.95 = (bf16[8,576,256]{2,1,0:T(8,128)(2,1)S(1)}, f32[8,64,256]{2,1,0:T(8,128)S(1)}, bf16[8,64,256]{2,1,0:T(8,128)(2,1)S(1)}, bf16[192,576]{1,0:T(8,128)(2,1)S(1)}) custom-call(s32[1]{0:T(128)} %bitcast.core_ref, s32[32,256]{1,0:T(8,128)S(1)} %get-tuple-element.39.rows_ref, bf16[8,64,256]{2,1,0:T(8,128)(2,1)S(1)} %get-tuple-element.43.planes_ref, ...), custom_call_target="tpu_custom_call" | custom-call | flops 452984832 | bytes 4153604 | tf_op jit(solution)/shard_map/pallas_call | solution.py:477
  6.7 1.7 %shard_map.96 = (bf16[8,64,256]{2,1,0:T(8,128)(2,1)S(1)}, bf16[768,256]{1,0:T(8,128)(2,1)S(1)}, bf16[576,256]{1,0:T(8,128)(2,1)S(1)}, f32[96,576]{1,0:T(8,128)S(1)}, f32[64,256]{1,0:T(8,128)S(1)}) custom-call(s32[1]{0:T(128)} %bitcast.core_ref, s32[1]{0:T(128)} %bitcast.6.own_ref, s32[32,256]{1,0:T(8,128)S(1)} %get-tuple-element.39.rows_ref, ...), custom_call_target="tpu_custom_call" | custom-call | flops 117440512 | bytes 4734984 | tf_op jit(solution)/shard_map/pallas_call | solution.py:477
  8.4 0.7 %collective-permute-done.face_ref = bf16[64,256]{1,0:T(8,128)(2,1)S(1)} collective-permute-done((bf16[64,256]{1,0:T(8,128)(2,1)S(1)}, bf16[64,256]{1,0:T(8,128)(2,1)S(1)}, u32[]{:S(2)}, u32[]{:S(2)}) %collective-permute-start) | collective-permute-done | bytes 32800 | tf_op jit(solution)/shard_map/ppermute | solution.py:530
  9.0 1.0 %shard_map.97 = (bf16[64,256]{1,0:T(8,128)(2,1)S(1)}, bf16[768,256]{1,0:T(8,128)(2,1)S(1)}, bf16[576,256]{1,0:T(8,128)(2,1)S(1)}, bf16[576,128]{1,0:T(8,128)(2,1)S(1)}, f32[32,64]{1,0:T(8,128)S(1)}) custom-call(s32[1]{0:T(128)} %bitcast.core_ref, s32[1]{0:T(128)} %bitcast.6.own_ref, s32[32,256]{1,0:T(8,128)S(1)} %get-tuple-element.39.rows_ref, ...), custom_call_target="tpu_custom_call" | custom-call | flops 117440512 | bytes 5054472 | tf_op jit(solution)/shard_map/pallas_call | solution.py:477
  10.0 1.0 %shard_map.98.mine_ref = f32[448,128]{1,0:T(8,128)S(1)} custom-call(s32[1]{0:T(128)} %bitcast.core_ref, s32[1]{0:T(128)} %bitcast.6.own_ref, bf16[768,256]{1,0:T(8,128)(2,1)S(1)} %get-tuple-element.56.padded_ref, bf16[8,576,256]{2,1,0:T(8,128)(2,1)S(1)} %get-tuple-element.47.moved_ref, bf16[576,256]{1,0:T(8,128)(2,1)S(1)} %get-tuple-element.59.first_ref, ...), custom_call_target="tpu_custom_call" | custom-call | flops 226492416 | bytes 3579912 | tf_op jit(solution)/shard_map/pallas_call | solution.py:477
  11.1 0.3 collective-permute-done.2.other_ref
  11.4 2.3 %collective-permute-start.5 = (bf16[448,128]{1,0:T(8,128)(2,1)S(1)}, bf16[448,128]{1,0:T(8,128)(2,1)S(1)}, u32[]{:S(2)}, u32[]{:S(2)}) collective-permute-start(bf16[448,128]{1,0:T(8,128)(2,1)S(1)} %get-tuple-element.63.after_ref.mine_ref), channel_id=1, source_target_pairs={{0,5},{1,16},{2,19},{3,6},{4,21},{5,0},{6,3},{7,22},{8,25},{9,12},... | collective-permute-start | bytes 344072 | tf_op jit(solution)/shard_map/ppermute | solution.py:600
  13.7 2.4 %shard_map.100 = (bf16[4,64,512]{2,1,0:T(8,128)(2,1)}, f32[640,256]{1,0:T(8,128)S(1)}, bf16[192,576]{1,0:T(8,128)(2,1)S(1)}) custom-call(s32[1]{0:T(128)} %bitcast.core_ref, s32[32,256]{1,0:T(8,128)S(1)} %get-tuple-element.39.rows_ref, bf16[768,256]{1,0:T(8,128)(2,1)S(1)} %get-tuple-element.56.padded_ref, ...), custom_call_target="tpu_custom_call" | custom-call | flops 452984832 | bytes 2195460 | tf_op jit(solution)/shard_map/pallas_call | solution.py:477
  16.2 3.3 %collective-permute-start.6 = (bf16[448,128]{1,0:T(8,128)(2,1)S(1)}, bf16[448,128]{1,0:T(8,128)(2,1)S(1)}, u32[]{:S(2)}, u32[]{:S(2)}) collective-permute-start(bf16[448,128]{1,0:T(8,128)(2,1)S(1)} %shard_map.101.mine_ref), channel_id=1, source_target_pairs={{0,17},{1,2},{2,1},{3,18},{4,7},{5,20},{6,23},{7,4},{8,11},{9,24},... | collective-permute-start | bytes 344072 | tf_op jit(solution)/shard_map/ppermute | solution.py:600
  19.5 2.2 %collective-permute-start.3 = (bf16[128,256]{1,0:T(8,128)(2,1)S(1)}, bf16[128,256]{1,0:T(8,128)(2,1)S(1)}, u32[]{:S(2)}, u32[]{:S(2)}) collective-permute-start(bf16[128,256]{1,0:T(8,128)(2,1)S(1)} %get-tuple-element.65), channel_id=1, source_target_pairs={{0,4},{1,0},{2,6},{3,2},{4,8},{5,1},{6,10},{7,3},{8,12},{9,5},{10,... | collective-permute-start | bytes 196616 | tf_op jit(solution)/shard_map/ppermute | solution.py:603
  21.7 0.3 collective-permute-done.6.other_ref
  22.0 2.7 %collective-permute-start.7 = (bf16[448,128]{1,0:T(8,128)(2,1)S(1)}, bf16[448,128]{1,0:T(8,128)(2,1)S(1)}, u32[]{:S(2)}, u32[]{:S(2)}) collective-permute-start(bf16[448,128]{1,0:T(8,128)(2,1)S(1)} %shard_map.102.mine_ref), channel_id=1, source_target_pairs={{0,3},{1,8},{2,11},{3,0},{4,13},{5,6},{6,5},{7,14},{8,1},{9,10},{1... | collective-permute-start | bytes 344072 | tf_op jit(solution)/shard_map/ppermute | solution.py:600
  24.8 1.2 %collective-permute-done.4.refs_0_.second_ref = bf16[64,256]{1,0:T(8,128)(2,1)S(1)} collective-permute-done((bf16[64,256]{1,0:T(8,128)(2,1)S(1)}, bf16[64,256]{1,0:T(8,128)(2,1)S(1)}, u32[]{:S(2)}, u32[]{:S(2)}) %collective-permute-start.4) | collective-permute-done | bytes 32800 | tf_op jit(solution)/shard_map/ppermute | solution.py:620
  26.0 1.2 %collective-permute-done.7.other_ref = bf16[448,128]{1,0:T(8,128)(2,1)S(1)} collective-permute-done((bf16[448,128]{1,0:T(8,128)(2,1)S(1)}, bf16[448,128]{1,0:T(8,128)(2,1)S(1)}, u32[]{:S(2)}, u32[]{:S(2)}) %collective-permute-start.7) | collective-permute-done | bytes 114720 | tf_op jit(solution)/shard_map/ppermute | solution.py:600
  27.2 0.9 %collective-permute-start.8 = (bf16[448,128]{1,0:T(8,128)(2,1)S(1)}, bf16[448,128]{1,0:T(8,128)(2,1)S(1)}, u32[]{:S(2)}, u32[]{:S(2)}) collective-permute-start(bf16[448,128]{1,0:T(8,128)(2,1)S(1)} %shard_map.103.after_ref.mine_ref), channel_id=1, source_target_pairs={{0,9},{1,4},{2,7},{3,10},{4,1},{5,12},{6,15},{7,2},{8,13},{9,0},{1... | collective-permute-start | bytes 344072 | tf_op jit(solution)/shard_map/ppermute | solution.py:600
  28.1 1.6 %shard_map.104 = (bf16[4,64,512]{2,1,0:T(8,128)(2,1)}, f32[8,128]{1,0:T(8,128)S(1)}) custom-call(s32[1]{0:T(128)} %bitcast.core_ref, s32[32,256]{1,0:T(8,128)S(1)} %get-tuple-element.39.rows_ref, bf16[64,256]{1,0:T(8,128)(2,1)S(1)} %get-tuple-element.75.first_ref, bf16[64,256]{1,0:T(8,128)(2,1)S(1)} %collective-permute-done.4.refs_0_.second_ref, ...), custom_call_target="tpu_custom_call" | custom-call | flops 100663296 | bytes 1626116 | tf_op jit(solution)/shard_map/pallas_call | solution.py:477
  29.7 1.8 %collective-permute-done.8.other_ref = bf16[448,128]{1,0:T(8,128)(2,1)S(1)} collective-permute-done((bf16[448,128]{1,0:T(8,128)(2,1)S(1)}, bf16[448,128]{1,0:T(8,128)(2,1)S(1)}, u32[]{:S(2)}, u32[]{:S(2)}) %collective-permute-start.8) | collective-permute-done | bytes 114720 | tf_op jit(solution)/shard_map/ppermute | solution.py:600
  31.5 0.4 %collective-permute-start.9 = (f32[448,128]{1,0:T(8,128)S(1)}, f32[448,128]{1,0:T(8,128)S(1)}, u32[]{:S(2)}, u32[]{:S(2)}) collective-permute-start(f32[448,128]{1,0:T(8,128)S(1)} %shard_map.105.source_ref), channel_id=1, source_target_pairs={{0,1},{1,0},{2,3},{3,2},{4,5},{5,4},{6,7},{7,6},{8,9},{9,8},{10,11... | collective-permute-start | bytes 688136 | tf_op jit(solution)/shard_map/ppermute | solution.py:639
  32.0 0.9 %shard_map.106 = (f32[27,64,64]{2,1,0:T(8,128)}, f32[1,64]{1,0:T(1,128)S(1)}) custom-call(s32[1]{0:T(128)} %bitcast.6.own_ref, f32[448,128]{1,0:T(8,128)S(1)} %shard_map.105.source_ref), custom_call_target="tpu_custom_call" | custom-call | bytes 672004 | tf_op jit(solution)/shard_map/pallas_call | solution.py:477
  32.9 0.2 collective-permute-done.9.source_ref
  33.1 0.9 %shard_map.107 = (f32[27,64,64]{2,1,0:T(8,128)}, f32[1,64]{1,0:T(1,128)}) custom-call(s32[1]{0:T(128)} %bitcast.6.own_ref, f32[448,128]{1,0:T(8,128)S(1)} %collective-permute-done.9.source_ref, f32[27,64,64]{2,1,0:T(8,128)} %get-tuple-element.70.begun_ref, f32[1,64]{1,0:T(1,128)S(1)} %get-tuple-element.71.own_bias_ref), custom_call_target="tpu_custom_call", output_to_operand_aliasing={{0}: (2, {})} | custom-call | bytes 1114628 | tf_op jit(solution)/shard_map/pallas_call | solution.py:477
  (12 shorter events, 0.4 us)
Async XLA Ops:
  1.9 4.8 %collective-permute-start.1 = (bf16[64,256]{1,0:T(8,128)(2,1)S(1)}, bf16[64,256]{1,0:T(8,128)(2,1)S(1)}, u32[]{:S(2)}, u32[]{:S(2)}) collective-permute-start(bf16[64,256]{1,0:T(8,128)(2,1)S(1)} %get-tuple-element.52), channel_id=1, source_target_pairs={{0,4},{1,0},{2,6},{3,2},{4,8},{5,1},{6,10},{7,3},{8,12},{9,5},{10,... | collective-permute-start | bytes 98312 | tf_op jit(solution)/shard_map/ppermute | solution.py:524
  5.1 4.0 %collective-permute-start = (bf16[64,256]{1,0:T(8,128)(2,1)S(1)}, bf16[64,256]{1,0:T(8,128)(2,1)S(1)}, u32[]{:S(2)}, u32[]{:S(2)}) collective-permute-start(bf16[64,256]{1,0:T(8,128)(2,1)S(1)} %get-tuple-element.42), channel_id=1, source_target_pairs={{4,0},{0,1},{6,2},{2,3},{8,4},{1,5},{10,6},{3,7},{12,8},{5,9},{14,... | collective-permute-start | bytes 98312 | tf_op jit(solution)/shard_map/ppermute | solution.py:530
  10.0 1.4 %collective-permute-start.2 = (bf16[576,128]{1,0:T(8,128)(2,1)S(1)}, bf16[576,128]{1,0:T(8,128)(2,1)S(1)}, u32[]{:S(2)}, u32[]{:S(2)}) collective-permute-start(bf16[576,128]{1,0:T(8,128)(2,1)S(1)} %get-tuple-element.62), channel_id=1, source_target_pairs={{0,1},{1,0},{2,3},{3,2},{4,5},{5,4},{6,7},{7,6},{8,9},{9,8},{10,11... | collective-permute-start | bytes 442376 | tf_op jit(solution)/shard_map/ppermute | solution.py:579
  11.4 4.8 %collective-permute-start.5 = (bf16[448,128]{1,0:T(8,128)(2,1)S(1)}, bf16[448,128]{1,0:T(8,128)(2,1)S(1)}, u32[]{:S(2)}, u32[]{:S(2)}) collective-permute-start(bf16[448,128]{1,0:T(8,128)(2,1)S(1)} %get-tuple-element.63.after_ref.mine_ref), channel_id=1, source_target_pairs={{0,5},{1,16},{2,19},{3,6},{4,21},{5,0},{6,3},{7,22},{8,25},{9,12},... | collective-permute-start | bytes 344072 | tf_op jit(solution)/shard_map/ppermute | solution.py:600
  16.2 5.8 %collective-permute-start.6 = (bf16[448,128]{1,0:T(8,128)(2,1)S(1)}, bf16[448,128]{1,0:T(8,128)(2,1)S(1)}, u32[]{:S(2)}, u32[]{:S(2)}) collective-permute-start(bf16[448,128]{1,0:T(8,128)(2,1)S(1)} %shard_map.101.mine_ref), channel_id=1, source_target_pairs={{0,17},{1,2},{2,1},{3,18},{4,7},{5,20},{6,23},{7,4},{8,11},{9,24},... | collective-permute-start | bytes 344072 | tf_op jit(solution)/shard_map/ppermute | solution.py:600
  19.5 5.2 %collective-permute-start.3 = (bf16[128,256]{1,0:T(8,128)(2,1)S(1)}, bf16[128,256]{1,0:T(8,128)(2,1)S(1)}, u32[]{:S(2)}, u32[]{:S(2)}) collective-permute-start(bf16[128,256]{1,0:T(8,128)(2,1)S(1)} %get-tuple-element.65), channel_id=1, source_target_pairs={{0,4},{1,0},{2,6},{3,2},{4,8},{5,1},{6,10},{7,3},{8,12},{9,5},{10,... | collective-permute-start | bytes 196616 | tf_op jit(solution)/shard_map/ppermute | solution.py:603
  22.0 5.2 %collective-permute-start.7 = (bf16[448,128]{1,0:T(8,128)(2,1)S(1)}, bf16[448,128]{1,0:T(8,128)(2,1)S(1)}, u32[]{:S(2)}, u32[]{:S(2)}) collective-permute-start(bf16[448,128]{1,0:T(8,128)(2,1)S(1)} %shard_map.102.mine_ref), channel_id=1, source_target_pairs={{0,3},{1,8},{2,11},{3,0},{4,13},{5,6},{6,5},{7,14},{8,1},{9,10},{1... | collective-permute-start | bytes 344072 | tf_op jit(solution)/shard_map/ppermute | solution.py:600
  24.7 1.3 %collective-permute-start.4 = (bf16[64,256]{1,0:T(8,128)(2,1)S(1)}, bf16[64,256]{1,0:T(8,128)(2,1)S(1)}, u32[]{:S(2)}, u32[]{:S(2)}) collective-permute-start(bf16[64,256]{1,0:T(8,128)(2,1)S(1)} %get-tuple-element.74), channel_id=1, source_target_pairs={{0,1},{1,0},{2,3},{3,2},{4,5},{5,4},{6,7},{7,6},{8,9},{9,8},{10,11... | collective-permute-start | bytes 98312 | tf_op jit(solution)/shard_map/ppermute | solution.py:620
  27.2 4.3 %collective-permute-start.8 = (bf16[448,128]{1,0:T(8,128)(2,1)S(1)}, bf16[448,128]{1,0:T(8,128)(2,1)S(1)}, u32[]{:S(2)}, u32[]{:S(2)}) collective-permute-start(bf16[448,128]{1,0:T(8,128)(2,1)S(1)} %shard_map.103.after_ref.mine_ref), channel_id=1, source_target_pairs={{0,9},{1,4},{2,7},{3,10},{4,1},{5,12},{6,15},{7,2},{8,13},{9,0},{1... | collective-permute-start | bytes 344072 | tf_op jit(solution)/shard_map/ppermute | solution.py:600
  31.5 1.6 %collective-permute-start.9 = (f32[448,128]{1,0:T(8,128)S(1)}, f32[448,128]{1,0:T(8,128)S(1)}, u32[]{:S(2)}, u32[]{:S(2)}) collective-permute-start(f32[448,128]{1,0:T(8,128)S(1)} %shard_map.105.source_ref), channel_id=1, source_target_pairs={{0,1},{1,0},{2,3},{3,2},{4,5},{5,4},{6,7},{7,6},{8,9},{9,8},{10,11... | collective-permute-start | bytes 688136 | tf_op jit(solution)/shard_map/ppermute | solution.py:639

commit v10 on v9

--- a/solution.py
+++ b/solution.py
@@ -99,9 +99,9 @@
 
 
 def load_faces(core_ref, first_ref, second_ref):
-    even = core_ref[0] == 0
+    upward = core_ref[0] == 0
     first, second = first_ref[...].astype(F32), second_ref[...].astype(F32)
-    return jnp.where(even, first, second).astype(BF), jnp.where(even, second, first).astype(BF)
+    return jnp.where(upward, first, second).astype(BF), jnp.where(upward, second, first).astype(BF)
 
 
 def stage_kernel(
@@ -258,9 +258,9 @@
 ):
     count, channels, lanes = pre_ref.shape
     bricks = lanes // PLANE
-    even = core_ref[0] == 0
-    face_moved_ref[...] = shifted_face(face_ref[...], side_rows(rows_ref, even), bricks)
-    at = pl.multiple_of(jnp.where(even, 2 * channels, 0), channels)
+    upward = core_ref[0] == 0
+    face_moved_ref[...] = shifted_face(face_ref[...], side_rows(rows_ref, upward), bricks)
+    at = pl.multiple_of(jnp.where(upward, 2 * channels, 0), channels)
     add = dot(weight_ref[pl.ds(at, channels), :], face_moved_ref[...])
     padded_ref[0 : 2 * channels, :] = jnp.zeros((2 * channels, lanes), BF)
     padded_ref[channels * (count + 2) :, :] = jnp.zeros((2 * channels, lanes), BF)
@@ -273,7 +273,7 @@
         masked = moved_ref[x, 4 * channels : 5 * channels, :].astype(F32)
         result, grad = activate(pre, masked, cot2_ref[x].astype(F32), keep)
         if x in (0, count - 1):
-            there = even if x == 0 else jnp.logical_not(even)
+            there = upward if x == 0 else jnp.logical_not(upward)
             grad = jnp.where(there, grad.astype(F32), 0.0).astype(BF)
         result_ref[x] = result
         padded_ref[channels * (x + 2) : channels * (x + 3), :] = grad
@@ -281,7 +281,7 @@
     bias_ref[...] = bias
     half = partial_ref.shape[0]
     start = (1 - own_ref[0]) * half
-    terms = terms_of(padded_ref, jnp.where(even, -1, count), start, half, face_moved_ref[...])
+    terms = terms_of(padded_ref, jnp.where(upward, -1, count), start, half, face_moved_ref[...])
     for x in range(count):
         terms = terms + terms_of(padded_ref, x, start, half, moved_ref[x])
     partial_ref[...] = terms
@@ -295,13 +295,13 @@
 ):
     count, channels, lanes = pre_ref.shape
     bricks = lanes // PLANE
-    even = core_ref[0] == 0
-    plane = jnp.where(even, count - 1, 0)
-    inward = jnp.where(even, -1, 1)
+    upward = core_ref[0] == 0
+    plane = jnp.where(upward, count - 1, 0)
+    inward = jnp.where(upward, -1, 1)
     face_moved_ref[...] = shifted_face(
-        face_ref[...], side_rows(rows_ref, jnp.logical_not(even)), bricks
-    )
-    at = pl.multiple_of(jnp.where(even, 0, 2 * channels), channels)
+        face_ref[...], side_rows(rows_ref, jnp.logical_not(upward)), bricks
+    )
+    at = pl.multiple_of(jnp.where(upward, 0, 2 * channels), channels)
     add = dot(weight_ref[pl.ds(at, channels), :], face_moved_ref[...])
     keep = jnp.broadcast_to(occ2_ref[plane][0:1], (channels, lanes))
     masked = moved_ref[plane, 4 * channels : 5 * channels, :].astype(F32)
@@ -325,7 +325,7 @@
     store_terms(terms, copies_ref, start, theirs_ref)
     low = padded_ref[2 * channels : 3 * channels, :].astype(F32)
     high = padded_ref[channels * (count + 1) : channels * (count + 2), :].astype(F32)
-    face = jnp.where(even, low, high).astype(BF)
+    face = jnp.where(upward, low, high).astype(BF)
     size = theirs_ref.shape[0] - channels * (lanes // 128)
     for t in range(lanes // 128):
         theirs_ref[size + channels * t : size + channels * (t + 1), :] = face[:, 128 * t : 128 * t + 128]
@@ -337,11 +337,11 @@
     count = moved_ref.shape[0]
     half = 3 * copies_ref.shape[1] // 2
     start = own_ref[0] * half
-    even = core_ref[0] == 0
-    terms = terms_of(padded_ref, jnp.where(even, -1, count), start, half, first_ref[...])
+    upward = core_ref[0] == 0
+    terms = terms_of(padded_ref, jnp.where(upward, -1, count), start, half, first_ref[...])
     for x in range(count):
         terms = terms + terms_of(padded_ref, x, start, half, moved_ref[x])
-    terms = terms + terms_of(padded_ref, jnp.where(even, count, -1), start, half, second_ref[...])
+    terms = terms + terms_of(padded_ref, jnp.where(upward, count, -1), start, half, second_ref[...])
     store_terms(terms, copies_ref, start, mine_ref)
 
 
@@ -354,10 +354,10 @@
     out_ref[...] = (mine_ref[...] + other_ref[0:size, :].astype(F32)).astype(BF)
     channels, lanes = faces_ref.shape[0] // 2, faces_ref.shape[1]
     end = padded_ref.shape[0] - 2 * channels
-    even = core_ref[0] == 0
+    upward = core_ref[0] == 0
     low = padded_ref[2 * channels : 3 * channels, :].astype(F32)
     high = padded_ref[end - channels : end, :].astype(F32)
-    faces_ref[0:channels, :] = jnp.where(even, high, low).astype(BF)
+    faces_ref[0:channels, :] = jnp.where(upward, high, low).astype(BF)
     for t in range(lanes // 128):
         rows = slice(size + channels * t, size + channels * (t + 1))
         faces_ref[channels:, 128 * t : 128 * t + 128] = other_ref[rows, :]
@@ -379,14 +379,14 @@
     shifted(flat, moved_ref, rows_ref, bricks, channels)
     total_ref[...] = jnp.zeros(total_ref.shape, F32)
     add_products(core_ref, back_ref, moved_ref, total_ref)
-    even = core_ref[0] == 0
+    upward = core_ref[0] == 0
     late = late_ref[...].astype(F32)
     for t in range(count // 2):
         first, second = result2_ref[2 * t].astype(F32), result2_ref[2 * t + 1].astype(F32)
         if t == 0:
-            first = jnp.where(even, first, late)
+            first = jnp.where(upward, first, late)
         if t == count // 2 - 1:
-            second = jnp.where(even, late, second)
+            second = jnp.where(upward, late, second)
         out = from_planes(first, second)
         for m in range(bricks):
             result_ref[m, :, 128 * t : 128 * t + 128] = out[m].astype(BF)
@@ -491,7 +491,7 @@
     pairs = []
     for space in range(spaces):
         for rep in range(reps):
-            step = 1 if rep % 2 == 0 else -1
+            step = 1 if rep % 2 == 1 else -1
             there, to = space + step, rep
             if not 0 <= there < spaces:
                 there, to = space, rep ^ 1
@@ -505,7 +505,7 @@
     count, lanes = voxels // PLANE, bricks * PLANE
     width = 9 * channels
     plane = ((channels, lanes), BF)
-    core = (lax.axis_index("rep") % 2).astype(jnp.int32)
+    core = 1 - (lax.axis_index("rep") % 2).astype(jnp.int32)
     cores = core[None]
     first, rows, x, occ, cot, weight, bias = call(
         stage_kernel,

time: 34.1 us -> 33.9 us (level)
  starting transfers between devices: 14.9 us -> 13 us
  waiting for transfers between devices: 5.84 us -> 7.55 us
    ppermute x1, starting transfers between devices: 0.06 us -> 2.56 us  [on_device(): second = lax.ppermute(second, axes, [(j, i) for i, j in pairs])]
    ppermute x1, starting transfers between devices: 3 us -> 0.51 us  [on_device(): first = lax.ppermute(first, axes, pairs)]
    ppermute x4, waiting for transfers between devices: 3.42 us -> 5.62 us  [on_device(): other = lax.ppermute(mine, axes, joined)]
    ppermute x1, starting transfers between devices: 2.16 us -> 0.01 us  [on_device(): faces = lax.ppermute(faces, axes, pairs)]
    ppermute x1, waiting for transfers between devices: 0.66 us -> 0.01 us  [on_device(): second = lax.ppermute(second, axes, [(j, i) for i, j in pairs])]
where the time goes in v10:
time: 33.9 us; the launch traced here: 33.8 us
  starting transfers between devices  13 us (38%)
  Pallas kernels  12.5 us (37%)
  waiting for transfers between devices  7.55 us (22%)
  between operations  0.73 us (2%)
    pallas_call x15, Pallas kernels, call(): pl.pallas_call(body, out_shape=shapes, in_specs=[spec for spec, _ in ins]...  12.5 us
    ppermute x4, starting transfers between devices, on_device(): other = lax.ppermute(mine, axes, joined)  9.46 us
    ppermute x4, waiting for transfers between devices, on_device(): other = lax.ppermute(mine, axes, joined)  5.62 us
    ppermute x1, starting transfers between devices, on_device(): second = lax.ppermute(second, axes, [(j, i) for i, j in pairs])  2.56 us
    ppermute x1, waiting for transfers between devices, on_device(): lax.ppermute(faces[channels:], axes, partner)  1.19 us
  transfers between devices with their start and end apart: 10, of which 8 were waited for; matrix products, arithmetic and copies ran while one was open for 0% of the time, Pallas kernels for 27%

profile of v10, /device:TPU:0, one launch (start us, length us, event | category | flops | bytes accessed | tf_op | source)
XLA Modules:
  0.0 33.8 jit_solution(5024114049256195618)
XLA Ops:
  0.6 1.2 %shard_map.93 = (bf16[64,256]{1,0:T(8,128)(2,1)S(1)}, s32[32,256]{1,0:T(8,128)S(1)}, bf16[4,64,512]{2,1,0:T(8,128)(2,1)S(1)}, s32[4,512]{1,0:T(4,128)S(1)}, bf16...) custom-call(s32[1]{0:T(128)} %bitcast.core_ref, bf16[4,64,512]{2,1,0:T(8,128)(2,1)} %bitcast.10, ...), custom_call_target="tpu_custom_call" | custom-call | bytes 1573796 | tf_op jit(solution)/shard_map/pallas_call | solution.py:477
  1.9 0.5 %collective-permute-start.1 = (bf16[64,256]{1,0:T(8,128)(2,1)S(1)}, bf16[64,256]{1,0:T(8,128)(2,1)S(1)}, u32[]{:S(2)}, u32[]{:S(2)}) collective-permute-start(bf16[64,256]{1,0:T(8,128)(2,1)S(1)} %get-tuple-element.52), channel_id=1, source_target_pairs={{0,1},{1,5},{2,3},{3,7},{4,0},{5,9},{6,2},{7,11},{8,4},{9,13},{10,... | collective-permute-start | bytes 98312 | tf_op jit(solution)/shard_map/ppermute | solution.py:524
  2.4 0.2 shard_map.94
  2.6 2.6 %collective-permute-start = (bf16[64,256]{1,0:T(8,128)(2,1)S(1)}, bf16[64,256]{1,0:T(8,128)(2,1)S(1)}, u32[]{:S(2)}, u32[]{:S(2)}) collective-permute-start(bf16[64,256]{1,0:T(8,128)(2,1)S(1)} %get-tuple-element.42), channel_id=1, source_target_pairs={{1,0},{5,1},{3,2},{7,3},{0,4},{9,5},{2,6},{11,7},{4,8},{13,9},{6,1... | collective-permute-start | bytes 98312 | tf_op jit(solution)/shard_map/ppermute | solution.py:530
  5.1 1.5 %shard_map.95 = (bf16[8,576,256]{2,1,0:T(8,128)(2,1)S(1)}, f32[8,64,256]{2,1,0:T(8,128)S(1)}, bf16[8,64,256]{2,1,0:T(8,128)(2,1)S(1)}, bf16[192,576]{1,0:T(8,128)(2,1)S(1)}) custom-call(s32[1]{0:T(128)} %bitcast.core_ref, s32[32,256]{1,0:T(8,128)S(1)} %get-tuple-element.39.rows_ref, bf16[8,64,256]{2,1,0:T(8,128)(2,1)S(1)} %get-tuple-element.43.planes_ref, ...), custom_call_target="tpu_custom_call" | custom-call | flops 452984832 | bytes 4153604 | tf_op jit(solution)/shard_map/pallas_call | solution.py:477
  6.7 0.1 collective-permute-done.1.face_ref
  6.8 1.7 %shard_map.96 = (bf16[8,64,256]{2,1,0:T(8,128)(2,1)S(1)}, bf16[768,256]{1,0:T(8,128)(2,1)S(1)}, bf16[576,256]{1,0:T(8,128)(2,1)S(1)}, f32[96,576]{1,0:T(8,128)S(1)}, f32[64,256]{1,0:T(8,128)S(1)}) custom-call(s32[1]{0:T(128)} %bitcast.core_ref, s32[1]{0:T(128)} %bitcast.6.own_ref, s32[32,256]{1,0:T(8,128)S(1)} %get-tuple-element.39.rows_ref, ...), custom_call_target="tpu_custom_call" | custom-call | flops 117440512 | bytes 4734984 | tf_op jit(solution)/shard_map/pallas_call | solution.py:477
  8.5 1.0 %shard_map.97 = (bf16[64,256]{1,0:T(8,128)(2,1)S(1)}, bf16[768,256]{1,0:T(8,128)(2,1)S(1)}, bf16[576,256]{1,0:T(8,128)(2,1)S(1)}, bf16[576,128]{1,0:T(8,128)(2,1)S(1)}, f32[32,64]{1,0:T(8,128)S(1)}) custom-call(s32[1]{0:T(128)} %bitcast.core_ref, s32[1]{0:T(128)} %bitcast.6.own_ref, s32[32,256]{1,0:T(8,128)S(1)} %get-tuple-element.39.rows_ref, ...), custom_call_target="tpu_custom_call" | custom-call | flops 117440512 | bytes 5054472 | tf_op jit(solution)/shard_map/pallas_call | solution.py:477
  9.5 1.0 %shard_map.98.mine_ref = f32[448,128]{1,0:T(8,128)S(1)} custom-call(s32[1]{0:T(128)} %bitcast.core_ref, s32[1]{0:T(128)} %bitcast.6.own_ref, bf16[768,256]{1,0:T(8,128)(2,1)S(1)} %get-tuple-element.56.padded_ref, bf16[8,576,256]{2,1,0:T(8,128)(2,1)S(1)} %get-tuple-element.47.moved_ref, bf16[576,256]{1,0:T(8,128)(2,1)S(1)} %get-tuple-element.59.first_ref, ...), custom_call_target="tpu_custom_call" | custom-call | flops 226492416 | bytes 3579912 | tf_op jit(solution)/shard_map/pallas_call | solution.py:477
  10.5 0.3 collective-permute-done.2.other_ref
  10.9 2.8 %collective-permute-start.5 = (bf16[448,128]{1,0:T(8,128)(2,1)S(1)}, bf16[448,128]{1,0:T(8,128)(2,1)S(1)}, u32[]{:S(2)}, u32[]{:S(2)}) collective-permute-start(bf16[448,128]{1,0:T(8,128)(2,1)S(1)} %get-tuple-element.63.after_ref.mine_ref), channel_id=1, source_target_pairs={{0,5},{1,16},{2,19},{3,6},{4,21},{5,0},{6,3},{7,22},{8,25},{9,12},... | collective-permute-start | bytes 344072 | tf_op jit(solution)/shard_map/ppermute | solution.py:600
  13.6 2.4 %shard_map.100 = (bf16[4,64,512]{2,1,0:T(8,128)(2,1)}, f32[640,256]{1,0:T(8,128)S(1)}, bf16[192,576]{1,0:T(8,128)(2,1)S(1)}) custom-call(s32[1]{0:T(128)} %bitcast.core_ref, s32[32,256]{1,0:T(8,128)S(1)} %get-tuple-element.39.rows_ref, bf16[768,256]{1,0:T(8,128)(2,1)S(1)} %get-tuple-element.56.padded_ref, ...), custom_call_target="tpu_custom_call" | custom-call | flops 452984832 | bytes 2195460 | tf_op jit(solution)/shard_map/pallas_call | solution.py:477
  16.1 3.1 %collective-permute-start.6 = (bf16[448,128]{1,0:T(8,128)(2,1)S(1)}, bf16[448,128]{1,0:T(8,128)(2,1)S(1)}, u32[]{:S(2)}, u32[]{:S(2)}) collective-permute-start(bf16[448,128]{1,0:T(8,128)(2,1)S(1)} %shard_map.101.mine_ref), channel_id=1, source_target_pairs={{0,17},{1,2},{2,1},{3,18},{4,7},{5,20},{6,23},{7,4},{8,11},{9,24},... | collective-permute-start | bytes 344072 | tf_op jit(solution)/shard_map/ppermute | solution.py:600
  19.3 2.5 %collective-permute-done.6.other_ref = bf16[448,128]{1,0:T(8,128)(2,1)S(1)} collective-permute-done((bf16[448,128]{1,0:T(8,128)(2,1)S(1)}, bf16[448,128]{1,0:T(8,128)(2,1)S(1)}, u32[]{:S(2)}, u32[]{:S(2)}) %collective-permute-start.6) | collective-permute-done | bytes 114720 | tf_op jit(solution)/shard_map/ppermute | solution.py:600
  21.8 2.7 %collective-permute-start.7 = (bf16[448,128]{1,0:T(8,128)(2,1)S(1)}, bf16[448,128]{1,0:T(8,128)(2,1)S(1)}, u32[]{:S(2)}, u32[]{:S(2)}) collective-permute-start(bf16[448,128]{1,0:T(8,128)(2,1)S(1)} %shard_map.102.mine_ref), channel_id=1, source_target_pairs={{0,3},{1,8},{2,11},{3,0},{4,13},{5,6},{6,5},{7,14},{8,1},{9,10},{1... | collective-permute-start | bytes 344072 | tf_op jit(solution)/shard_map/ppermute | solution.py:600
  24.6 1.2 %collective-permute-done.4.refs_0_.second_ref = bf16[64,256]{1,0:T(8,128)(2,1)S(1)} collective-permute-done((bf16[64,256]{1,0:T(8,128)(2,1)S(1)}, bf16[64,256]{1,0:T(8,128)(2,1)S(1)}, u32[]{:S(2)}, u32[]{:S(2)}) %collective-permute-start.4) | collective-permute-done | bytes 32800 | tf_op jit(solution)/shard_map/ppermute | solution.py:620
  25.8 1.2 %collective-permute-done.7.other_ref = bf16[448,128]{1,0:T(8,128)(2,1)S(1)} collective-permute-done((bf16[448,128]{1,0:T(8,128)(2,1)S(1)}, bf16[448,128]{1,0:T(8,128)(2,1)S(1)}, u32[]{:S(2)}, u32[]{:S(2)}) %collective-permute-start.7) | collective-permute-done | bytes 114720 | tf_op jit(solution)/shard_map/ppermute | solution.py:600
  27.0 0.8 %collective-permute-start.8 = (bf16[448,128]{1,0:T(8,128)(2,1)S(1)}, bf16[448,128]{1,0:T(8,128)(2,1)S(1)}, u32[]{:S(2)}, u32[]{:S(2)}) collective-permute-start(bf16[448,128]{1,0:T(8,128)(2,1)S(1)} %shard_map.103.after_ref.mine_ref), channel_id=1, source_target_pairs={{0,9},{1,4},{2,7},{3,10},{4,1},{5,12},{6,15},{7,2},{8,13},{9,0},{1... | collective-permute-start | bytes 344072 | tf_op jit(solution)/shard_map/ppermute | solution.py:600
  27.8 1.6 %shard_map.104 = (bf16[4,64,512]{2,1,0:T(8,128)(2,1)}, f32[8,128]{1,0:T(8,128)S(1)}) custom-call(s32[1]{0:T(128)} %bitcast.core_ref, s32[32,256]{1,0:T(8,128)S(1)} %get-tuple-element.39.rows_ref, bf16[64,256]{1,0:T(8,128)(2,1)S(1)} %get-tuple-element.75.first_ref, bf16[64,256]{1,0:T(8,128)(2,1)S(1)} %collective-permute-done.4.refs_0_.second_ref, ...), custom_call_target="tpu_custom_call" | custom-call | flops 100663296 | bytes 1626116 | tf_op jit(solution)/shard_map/pallas_call | solution.py:477
  29.4 1.9 %collective-permute-done.8.other_ref = bf16[448,128]{1,0:T(8,128)(2,1)S(1)} collective-permute-done((bf16[448,128]{1,0:T(8,128)(2,1)S(1)}, bf16[448,128]{1,0:T(8,128)(2,1)S(1)}, u32[]{:S(2)}, u32[]{:S(2)}) %collective-permute-start.8) | collective-permute-done | bytes 114720 | tf_op jit(solution)/shard_map/ppermute | solution.py:600
  31.3 0.4 %collective-permute-start.9 = (f32[448,128]{1,0:T(8,128)S(1)}, f32[448,128]{1,0:T(8,128)S(1)}, u32[]{:S(2)}, u32[]{:S(2)}) collective-permute-start(f32[448,128]{1,0:T(8,128)S(1)} %shard_map.105.source_ref), channel_id=1, source_target_pairs={{0,1},{1,0},{2,3},{3,2},{4,5},{5,4},{6,7},{7,6},{8,9},{9,8},{10,11... | collective-permute-start | bytes 688136 | tf_op jit(solution)/shard_map/ppermute | solution.py:639
  31.7 0.9 %shard_map.106 = (f32[27,64,64]{2,1,0:T(8,128)}, f32[1,64]{1,0:T(1,128)S(1)}) custom-call(s32[1]{0:T(128)} %bitcast.6.own_ref, f32[448,128]{1,0:T(8,128)S(1)} %shard_map.105.source_ref), custom_call_target="tpu_custom_call" | custom-call | bytes 672004 | tf_op jit(solution)/shard_map/pallas_call | solution.py:477
  32.6 0.3 collective-permute-done.9.source_ref
  32.9 0.9 %shard_map.107 = (f32[27,64,64]{2,1,0:T(8,128)}, f32[1,64]{1,0:T(1,128)}) custom-call(s32[1]{0:T(128)} %bitcast.6.own_ref, f32[448,128]{1,0:T(8,128)S(1)} %collective-permute-done.9.source_ref, f32[27,64,64]{2,1,0:T(8,128)} %get-tuple-element.70.begun_ref, f32[1,64]{1,0:T(1,128)S(1)} %get-tuple-element.71.own_bias_ref), custom_call_target="tpu_custom_call", output_to_operand_aliasing={{0}: (2, {})} | custom-call | bytes 1114628 | tf_op jit(solution)/shard_map/pallas_call | solution.py:477
  (12 shorter events, 0.3 us)
Async XLA Ops:
  1.9 4.9 %collective-permute-start.1 = (bf16[64,256]{1,0:T(8,128)(2,1)S(1)}, bf16[64,256]{1,0:T(8,128)(2,1)S(1)}, u32[]{:S(2)}, u32[]{:S(2)}) collective-permute-start(bf16[64,256]{1,0:T(8,128)(2,1)S(1)} %get-tuple-element.52), channel_id=1, source_target_pairs={{0,1},{1,5},{2,3},{3,7},{4,0},{5,9},{6,2},{7,11},{8,4},{9,13},{10,... | collective-permute-start | bytes 98312 | tf_op jit(solution)/shard_map/ppermute | solution.py:524
  2.6 5.9 %collective-permute-start = (bf16[64,256]{1,0:T(8,128)(2,1)S(1)}, bf16[64,256]{1,0:T(8,128)(2,1)S(1)}, u32[]{:S(2)}, u32[]{:S(2)}) collective-permute-start(bf16[64,256]{1,0:T(8,128)(2,1)S(1)} %get-tuple-element.42), channel_id=1, source_target_pairs={{1,0},{5,1},{3,2},{7,3},{0,4},{9,5},{2,6},{11,7},{4,8},{13,9},{6,1... | collective-permute-start | bytes 98312 | tf_op jit(solution)/shard_map/ppermute | solution.py:530
  9.4 1.4 %collective-permute-start.2 = (bf16[576,128]{1,0:T(8,128)(2,1)S(1)}, bf16[576,128]{1,0:T(8,128)(2,1)S(1)}, u32[]{:S(2)}, u32[]{:S(2)}) collective-permute-start(bf16[576,128]{1,0:T(8,128)(2,1)S(1)} %get-tuple-element.62), channel_id=1, source_target_pairs={{0,1},{1,0},{2,3},{3,2},{4,5},{5,4},{6,7},{7,6},{8,9},{9,8},{10,11... | collective-permute-start | bytes 442376 | tf_op jit(solution)/shard_map/ppermute | solution.py:579
  10.9 5.2 %collective-permute-start.5 = (bf16[448,128]{1,0:T(8,128)(2,1)S(1)}, bf16[448,128]{1,0:T(8,128)(2,1)S(1)}, u32[]{:S(2)}, u32[]{:S(2)}) collective-permute-start(bf16[448,128]{1,0:T(8,128)(2,1)S(1)} %get-tuple-element.63.after_ref.mine_ref), channel_id=1, source_target_pairs={{0,5},{1,16},{2,19},{3,6},{4,21},{5,0},{6,3},{7,22},{8,25},{9,12},... | collective-permute-start | bytes 344072 | tf_op jit(solution)/shard_map/ppermute | solution.py:600
  16.1 5.6 %collective-permute-start.6 = (bf16[448,128]{1,0:T(8,128)(2,1)S(1)}, bf16[448,128]{1,0:T(8,128)(2,1)S(1)}, u32[]{:S(2)}, u32[]{:S(2)}) collective-permute-start(bf16[448,128]{1,0:T(8,128)(2,1)S(1)} %shard_map.101.mine_ref), channel_id=1, source_target_pairs={{0,17},{1,2},{2,1},{3,18},{4,7},{5,20},{6,23},{7,4},{8,11},{9,24},... | collective-permute-start | bytes 344072 | tf_op jit(solution)/shard_map/ppermute | solution.py:600
  19.3 5.2 %collective-permute-start.3 = (bf16[128,256]{1,0:T(8,128)(2,1)S(1)}, bf16[128,256]{1,0:T(8,128)(2,1)S(1)}, u32[]{:S(2)}, u32[]{:S(2)}) collective-permute-start(bf16[128,256]{1,0:T(8,128)(2,1)S(1)} %get-tuple-element.65), channel_id=1, source_target_pairs={{0,1},{1,5},{2,3},{3,7},{4,0},{5,9},{6,2},{7,11},{8,4},{9,13},{10,... | collective-permute-start | bytes 196616 | tf_op jit(solution)/shard_map/ppermute | solution.py:603
  21.8 5.2 %collective-permute-start.7 = (bf16[448,128]{1,0:T(8,128)(2,1)S(1)}, bf16[448,128]{1,0:T(8,128)(2,1)S(1)}, u32[]{:S(2)}, u32[]{:S(2)}) collective-permute-start(bf16[448,128]{1,0:T(8,128)(2,1)S(1)} %shard_map.102.mine_ref), channel_id=1, source_target_pairs={{0,3},{1,8},{2,11},{3,0},{4,13},{5,6},{6,5},{7,14},{8,1},{9,10},{1... | collective-permute-start | bytes 344072 | tf_op jit(solution)/shard_map/ppermute | solution.py:600
  24.5 1.3 %collective-permute-start.4 = (bf16[64,256]{1,0:T(8,128)(2,1)S(1)}, bf16[64,256]{1,0:T(8,128)(2,1)S(1)}, u32[]{:S(2)}, u32[]{:S(2)}) collective-permute-start(bf16[64,256]{1,0:T(8,128)(2,1)S(1)} %get-tuple-element.74), channel_id=1, source_target_pairs={{0,1},{1,0},{2,3},{3,2},{4,5},{5,4},{6,7},{7,6},{8,9},{9,8},{10,11... | collective-permute-start | bytes 98312 | tf_op jit(solution)/shard_map/ppermute | solution.py:620
  27.0 4.3 %collective-permute-start.8 = (bf16[448,128]{1,0:T(8,128)(2,1)S(1)}, bf16[448,128]{1,0:T(8,128)(2,1)S(1)}, u32[]{:S(2)}, u32[]{:S(2)}) collective-permute-start(bf16[448,128]{1,0:T(8,128)(2,1)S(1)} %shard_map.103.after_ref.mine_ref), channel_id=1, source_target_pairs={{0,9},{1,4},{2,7},{3,10},{4,1},{5,12},{6,15},{7,2},{8,13},{9,0},{1... | collective-permute-start | bytes 344072 | tf_op jit(solution)/shard_map/ppermute | solution.py:600
  31.3 1.6 %collective-permute-start.9 = (f32[448,128]{1,0:T(8,128)S(1)}, f32[448,128]{1,0:T(8,128)S(1)}, u32[]{:S(2)}, u32[]{:S(2)}) collective-permute-start(f32[448,128]{1,0:T(8,128)S(1)} %shard_map.105.source_ref), channel_id=1, source_target_pairs={{0,1},{1,0},{2,3},{3,2},{4,5},{5,4},{6,7},{7,6},{8,9},{9,8},{10,11... | collective-permute-start | bytes 688136 | tf_op jit(solution)/shard_map/ppermute | solution.py:639

commit v11 on v10

--- a/solution.py
+++ b/solution.py
@@ -594,7 +594,8 @@
     )
     bits = [1 << i for i in range(1, (devices).bit_length() - 1)]
     order = bits[1:2] + bits[-1:] + bits[:1] + bits[2:-1]
-    rounds = list(zip(order, order[1:] + order[:1]))
+    order = bits[:1] + bits[-1:] + bits[1:-1]
+    rounds = list(zip(order, order[1:2] + order[:1] + order[:1:-1]))
     for i, steps in enumerate(rounds):
         joined = [(j, j ^ 1 ^ steps[j.bit_count() % 2]) for j in range(devices)]
         other = lax.ppermute(mine, axes, joined)

time: 33.9 us -> 34.1 us (level)
  waiting for transfers between devices: 7.55 us -> 7.9 us
where the time goes in v11:
time: 34.1 us; the launch traced here: 33.9 us
  starting transfers between devices  12.8 us (38%)
  Pallas kernels  12.5 us (37%)
  waiting for transfers between devices  7.9 us (23%)
  between operations  0.73 us (2%)
    pallas_call x15, Pallas kernels, call(): pl.pallas_call(body, out_shape=shapes, in_specs=[spec for spec, _ in ins]...  12.5 us
    ppermute x4, starting transfers between devices, on_device(): other = lax.ppermute(mine, axes, joined)  9.46 us
    ppermute x4, waiting for transfers between devices, on_device(): other = lax.ppermute(mine, axes, joined)  5.8 us
    ppermute x1, starting transfers between devices, on_device(): second = lax.ppermute(second, axes, [(j, i) for i, j in pairs])  2.56 us
    ppermute x1, waiting for transfers between devices, on_device(): lax.ppermute(faces[channels:], axes, partner)  1.19 us
  transfers between devices with their start and end apart: 10, of which 8 were waited for; matrix products, arithmetic and copies ran while one was open for 0% of the time, Pallas kernels for 27%

profile of v11, /device:TPU:0, one launch (start us, length us, event | category | flops | bytes accessed | tf_op | source)
XLA Modules:
  0.0 33.9 jit_solution(15825831519769144475)
XLA Ops:
  0.6 1.2 %shard_map.93 = (bf16[64,256]{1,0:T(8,128)(2,1)S(1)}, s32[32,256]{1,0:T(8,128)S(1)}, bf16[4,64,512]{2,1,0:T(8,128)(2,1)S(1)}, s32[4,512]{1,0:T(4,128)S(1)}, bf16...) custom-call(s32[1]{0:T(128)} %bitcast.core_ref, bf16[4,64,512]{2,1,0:T(8,128)(2,1)} %bitcast.10, ...), custom_call_target="tpu_custom_call" | custom-call | bytes 1573796 | tf_op jit(solution)/shard_map/pallas_call | solution.py:477
  1.9 0.5 %collective-permute-start.1 = (bf16[64,256]{1,0:T(8,128)(2,1)S(1)}, bf16[64,256]{1,0:T(8,128)(2,1)S(1)}, u32[]{:S(2)}, u32[]{:S(2)}) collective-permute-start(bf16[64,256]{1,0:T(8,128)(2,1)S(1)} %get-tuple-element.52), channel_id=1, source_target_pairs={{0,1},{1,5},{2,3},{3,7},{4,0},{5,9},{6,2},{7,11},{8,4},{9,13},{10,... | collective-permute-start | bytes 98312 | tf_op jit(solution)/shard_map/ppermute | solution.py:524
  2.4 0.2 shard_map.94
  2.6 2.6 %collective-permute-start = (bf16[64,256]{1,0:T(8,128)(2,1)S(1)}, bf16[64,256]{1,0:T(8,128)(2,1)S(1)}, u32[]{:S(2)}, u32[]{:S(2)}) collective-permute-start(bf16[64,256]{1,0:T(8,128)(2,1)S(1)} %get-tuple-element.42), channel_id=1, source_target_pairs={{1,0},{5,1},{3,2},{7,3},{0,4},{9,5},{2,6},{11,7},{4,8},{13,9},{6,1... | collective-permute-start | bytes 98312 | tf_op jit(solution)/shard_map/ppermute | solution.py:530
  5.1 1.5 %shard_map.95 = (bf16[8,576,256]{2,1,0:T(8,128)(2,1)S(1)}, f32[8,64,256]{2,1,0:T(8,128)S(1)}, bf16[8,64,256]{2,1,0:T(8,128)(2,1)S(1)}, bf16[192,576]{1,0:T(8,128)(2,1)S(1)}) custom-call(s32[1]{0:T(128)} %bitcast.core_ref, s32[32,256]{1,0:T(8,128)S(1)} %get-tuple-element.39.rows_ref, bf16[8,64,256]{2,1,0:T(8,128)(2,1)S(1)} %get-tuple-element.43.planes_ref, ...), custom_call_target="tpu_custom_call" | custom-call | flops 452984832 | bytes 4153604 | tf_op jit(solution)/shard_map/pallas_call | solution.py:477
  6.7 0.1 collective-permute-done.1.face_ref
  6.8 1.7 %shard_map.96 = (bf16[8,64,256]{2,1,0:T(8,128)(2,1)S(1)}, bf16[768,256]{1,0:T(8,128)(2,1)S(1)}, bf16[576,256]{1,0:T(8,128)(2,1)S(1)}, f32[96,576]{1,0:T(8,128)S(1)}, f32[64,256]{1,0:T(8,128)S(1)}) custom-call(s32[1]{0:T(128)} %bitcast.core_ref, s32[1]{0:T(128)} %bitcast.6.own_ref, s32[32,256]{1,0:T(8,128)S(1)} %get-tuple-element.39.rows_ref, ...), custom_call_target="tpu_custom_call" | custom-call | flops 117440512 | bytes 4734984 | tf_op jit(solution)/shard_map/pallas_call | solution.py:477
  8.5 1.0 %shard_map.97 = (bf16[64,256]{1,0:T(8,128)(2,1)S(1)}, bf16[768,256]{1,0:T(8,128)(2,1)S(1)}, bf16[576,256]{1,0:T(8,128)(2,1)S(1)}, bf16[576,128]{1,0:T(8,128)(2,1)S(1)}, f32[32,64]{1,0:T(8,128)S(1)}) custom-call(s32[1]{0:T(128)} %bitcast.core_ref, s32[1]{0:T(128)} %bitcast.6.own_ref, s32[32,256]{1,0:T(8,128)S(1)} %get-tuple-element.39.rows_ref, ...), custom_call_target="tpu_custom_call" | custom-call | flops 117440512 | bytes 5054472 | tf_op jit(solution)/shard_map/pallas_call | solution.py:477
  9.5 1.0 %shard_map.98.mine_ref = f32[448,128]{1,0:T(8,128)S(1)} custom-call(s32[1]{0:T(128)} %bitcast.core_ref, s32[1]{0:T(128)} %bitcast.6.own_ref, bf16[768,256]{1,0:T(8,128)(2,1)S(1)} %get-tuple-element.56.padded_ref, bf16[8,576,256]{2,1,0:T(8,128)(2,1)S(1)} %get-tuple-element.47.moved_ref, bf16[576,256]{1,0:T(8,128)(2,1)S(1)} %get-tuple-element.59.first_ref, ...), custom_call_target="tpu_custom_call" | custom-call | flops 226492416 | bytes 3579912 | tf_op jit(solution)/shard_map/pallas_call | solution.py:477
  10.5 0.3 collective-permute-done.2.other_ref
  10.9 2.0 %collective-permute-start.5 = (bf16[448,128]{1,0:T(8,128)(2,1)S(1)}, bf16[448,128]{1,0:T(8,128)(2,1)S(1)}, u32[]{:S(2)}, u32[]{:S(2)}) collective-permute-start(bf16[448,128]{1,0:T(8,128)(2,1)S(1)} %get-tuple-element.63.after_ref.mine_ref), channel_id=1, source_target_pairs={{0,3},{1,16},{2,19},{3,0},{4,21},{5,6},{6,5},{7,22},{8,25},{9,10},... | collective-permute-start | bytes 344072 | tf_op jit(solution)/shard_map/ppermute | solution.py:601
  12.8 2.4 %shard_map.100 = (bf16[4,64,512]{2,1,0:T(8,128)(2,1)}, f32[640,256]{1,0:T(8,128)S(1)}, bf16[192,576]{1,0:T(8,128)(2,1)S(1)}) custom-call(s32[1]{0:T(128)} %bitcast.core_ref, s32[32,256]{1,0:T(8,128)S(1)} %get-tuple-element.39.rows_ref, bf16[768,256]{1,0:T(8,128)(2,1)S(1)} %get-tuple-element.56.padded_ref, ...), custom_call_target="tpu_custom_call" | custom-call | flops 452984832 | bytes 2195460 | tf_op jit(solution)/shard_map/pallas_call | solution.py:477
  15.3 3.9 %collective-permute-start.6 = (bf16[448,128]{1,0:T(8,128)(2,1)S(1)}, bf16[448,128]{1,0:T(8,128)(2,1)S(1)}, u32[]{:S(2)}, u32[]{:S(2)}) collective-permute-start(bf16[448,128]{1,0:T(8,128)(2,1)S(1)} %shard_map.101.mine_ref), channel_id=1, source_target_pairs={{0,17},{1,2},{2,1},{3,18},{4,7},{5,20},{6,23},{7,4},{8,11},{9,24},... | collective-permute-start | bytes 344072 | tf_op jit(solution)/shard_map/ppermute | solution.py:601
  19.3 2.5 %collective-permute-done.6.other_ref = bf16[448,128]{1,0:T(8,128)(2,1)S(1)} collective-permute-done((bf16[448,128]{1,0:T(8,128)(2,1)S(1)}, bf16[448,128]{1,0:T(8,128)(2,1)S(1)}, u32[]{:S(2)}, u32[]{:S(2)}) %collective-permute-start.6) | collective-permute-done | bytes 114720 | tf_op jit(solution)/shard_map/ppermute | solution.py:601
  21.8 2.9 %collective-permute-start.7 = (bf16[448,128]{1,0:T(8,128)(2,1)S(1)}, bf16[448,128]{1,0:T(8,128)(2,1)S(1)}, u32[]{:S(2)}, u32[]{:S(2)}) collective-permute-start(bf16[448,128]{1,0:T(8,128)(2,1)S(1)} %shard_map.102.mine_ref), channel_id=1, source_target_pairs={{0,5},{1,8},{2,11},{3,6},{4,13},{5,0},{6,3},{7,14},{8,1},{9,12},{1... | collective-permute-start | bytes 344072 | tf_op jit(solution)/shard_map/ppermute | solution.py:601
  24.8 1.2 %collective-permute-done.4.refs_0_.second_ref = bf16[64,256]{1,0:T(8,128)(2,1)S(1)} collective-permute-done((bf16[64,256]{1,0:T(8,128)(2,1)S(1)}, bf16[64,256]{1,0:T(8,128)(2,1)S(1)}, u32[]{:S(2)}, u32[]{:S(2)}) %collective-permute-start.4) | collective-permute-done | bytes 32800 | tf_op jit(solution)/shard_map/ppermute | solution.py:621
  26.0 1.2 %collective-permute-done.7.other_ref = bf16[448,128]{1,0:T(8,128)(2,1)S(1)} collective-permute-done((bf16[448,128]{1,0:T(8,128)(2,1)S(1)}, bf16[448,128]{1,0:T(8,128)(2,1)S(1)}, u32[]{:S(2)}, u32[]{:S(2)}) %collective-permute-start.7) | collective-permute-done | bytes 114720 | tf_op jit(solution)/shard_map/ppermute | solution.py:601
  27.2 0.6 %collective-permute-start.8 = (bf16[448,128]{1,0:T(8,128)(2,1)S(1)}, bf16[448,128]{1,0:T(8,128)(2,1)S(1)}, u32[]{:S(2)}, u32[]{:S(2)}) collective-permute-start(bf16[448,128]{1,0:T(8,128)(2,1)S(1)} %shard_map.103.after_ref.mine_ref), channel_id=1, source_target_pairs={{0,9},{1,4},{2,7},{3,10},{4,1},{5,12},{6,15},{7,2},{8,13},{9,0},{1... | collective-permute-start | bytes 344072 | tf_op jit(solution)/shard_map/ppermute | solution.py:601
  27.8 1.6 %shard_map.104 = (bf16[4,64,512]{2,1,0:T(8,128)(2,1)}, f32[8,128]{1,0:T(8,128)S(1)}) custom-call(s32[1]{0:T(128)} %bitcast.core_ref, s32[32,256]{1,0:T(8,128)S(1)} %get-tuple-element.39.rows_ref, bf16[64,256]{1,0:T(8,128)(2,1)S(1)} %get-tuple-element.75.first_ref, bf16[64,256]{1,0:T(8,128)(2,1)S(1)} %collective-permute-done.4.refs_0_.second_ref, ...), custom_call_target="tpu_custom_call" | custom-call | flops 100663296 | bytes 1626116 | tf_op jit(solution)/shard_map/pallas_call | solution.py:477
  29.4 2.1 %collective-permute-done.8.other_ref = bf16[448,128]{1,0:T(8,128)(2,1)S(1)} collective-permute-done((bf16[448,128]{1,0:T(8,128)(2,1)S(1)}, bf16[448,128]{1,0:T(8,128)(2,1)S(1)}, u32[]{:S(2)}, u32[]{:S(2)}) %collective-permute-start.8) | collective-permute-done | bytes 114720 | tf_op jit(solution)/shard_map/ppermute | solution.py:601
  31.5 0.2 collective-permute-start.9
  31.7 0.9 %shard_map.106 = (f32[27,64,64]{2,1,0:T(8,128)}, f32[1,64]{1,0:T(1,128)S(1)}) custom-call(s32[1]{0:T(128)} %bitcast.6.own_ref, f32[448,128]{1,0:T(8,128)S(1)} %shard_map.105.source_ref), custom_call_target="tpu_custom_call" | custom-call | bytes 672004 | tf_op jit(solution)/shard_map/pallas_call | solution.py:477
  32.6 0.5 %collective-permute-done.9.source_ref = f32[448,128]{1,0:T(8,128)S(1)} collective-permute-done((f32[448,128]{1,0:T(8,128)S(1)}, f32[448,128]{1,0:T(8,128)S(1)}, u32[]{:S(2)}, u32[]{:S(2)}) %collective-permute-start.9) | collective-permute-done | bytes 229408 | tf_op jit(solution)/shard_map/ppermute | solution.py:640
  33.1 0.9 %shard_map.107 = (f32[27,64,64]{2,1,0:T(8,128)}, f32[1,64]{1,0:T(1,128)}) custom-call(s32[1]{0:T(128)} %bitcast.6.own_ref, f32[448,128]{1,0:T(8,128)S(1)} %collective-permute-done.9.source_ref, f32[27,64,64]{2,1,0:T(8,128)} %get-tuple-element.70.begun_ref, f32[1,64]{1,0:T(1,128)S(1)} %get-tuple-element.71.own_bias_ref), custom_call_target="tpu_custom_call", output_to_operand_aliasing={{0}: (2, {})} | custom-call | bytes 1114628 | tf_op jit(solution)/shard_map/pallas_call | solution.py:477
  (12 shorter events, 0.3 us)
Async XLA Ops:
  1.9 4.9 %collective-permute-start.1 = (bf16[64,256]{1,0:T(8,128)(2,1)S(1)}, bf16[64,256]{1,0:T(8,128)(2,1)S(1)}, u32[]{:S(2)}, u32[]{:S(2)}) collective-permute-start(bf16[64,256]{1,0:T(8,128)(2,1)S(1)} %get-tuple-element.52), channel_id=1, source_target_pairs={{0,1},{1,5},{2,3},{3,7},{4,0},{5,9},{6,2},{7,11},{8,4},{9,13},{10,... | collective-permute-start | bytes 98312 | tf_op jit(solution)/shard_map/ppermute | solution.py:524
  2.6 5.9 %collective-permute-start = (bf16[64,256]{1,0:T(8,128)(2,1)S(1)}, bf16[64,256]{1,0:T(8,128)(2,1)S(1)}, u32[]{:S(2)}, u32[]{:S(2)}) collective-permute-start(bf16[64,256]{1,0:T(8,128)(2,1)S(1)} %get-tuple-element.42), channel_id=1, source_target_pairs={{1,0},{5,1},{3,2},{7,3},{0,4},{9,5},{2,6},{11,7},{4,8},{13,9},{6,1... | collective-permute-start | bytes 98312 | tf_op jit(solution)/shard_map/ppermute | solution.py:530
  9.4 1.4 %collective-permute-start.2 = (bf16[576,128]{1,0:T(8,128)(2,1)S(1)}, bf16[576,128]{1,0:T(8,128)(2,1)S(1)}, u32[]{:S(2)}, u32[]{:S(2)}) collective-permute-start(bf16[576,128]{1,0:T(8,128)(2,1)S(1)} %get-tuple-element.62), channel_id=1, source_target_pairs={{0,1},{1,0},{2,3},{3,2},{4,5},{5,4},{6,7},{7,6},{8,9},{9,8},{10,11... | collective-permute-start | bytes 442376 | tf_op jit(solution)/shard_map/ppermute | solution.py:579
  10.9 4.4 %collective-permute-start.5 = (bf16[448,128]{1,0:T(8,128)(2,1)S(1)}, bf16[448,128]{1,0:T(8,128)(2,1)S(1)}, u32[]{:S(2)}, u32[]{:S(2)}) collective-permute-start(bf16[448,128]{1,0:T(8,128)(2,1)S(1)} %get-tuple-element.63.after_ref.mine_ref), channel_id=1, source_target_pairs={{0,3},{1,16},{2,19},{3,0},{4,21},{5,6},{6,5},{7,22},{8,25},{9,10},... | collective-permute-start | bytes 344072 | tf_op jit(solution)/shard_map/ppermute | solution.py:601
  15.3 6.4 %collective-permute-start.6 = (bf16[448,128]{1,0:T(8,128)(2,1)S(1)}, bf16[448,128]{1,0:T(8,128)(2,1)S(1)}, u32[]{:S(2)}, u32[]{:S(2)}) collective-permute-start(bf16[448,128]{1,0:T(8,128)(2,1)S(1)} %shard_map.101.mine_ref), channel_id=1, source_target_pairs={{0,17},{1,2},{2,1},{3,18},{4,7},{5,20},{6,23},{7,4},{8,11},{9,24},... | collective-permute-start | bytes 344072 | tf_op jit(solution)/shard_map/ppermute | solution.py:601
  19.3 5.4 %collective-permute-start.3 = (bf16[128,256]{1,0:T(8,128)(2,1)S(1)}, bf16[128,256]{1,0:T(8,128)(2,1)S(1)}, u32[]{:S(2)}, u32[]{:S(2)}) collective-permute-start(bf16[128,256]{1,0:T(8,128)(2,1)S(1)} %get-tuple-element.65), channel_id=1, source_target_pairs={{0,1},{1,5},{2,3},{3,7},{4,0},{5,9},{6,2},{7,11},{8,4},{9,13},{10,... | collective-permute-start | bytes 196616 | tf_op jit(solution)/shard_map/ppermute | solution.py:604
  21.8 5.4 %collective-permute-start.7 = (bf16[448,128]{1,0:T(8,128)(2,1)S(1)}, bf16[448,128]{1,0:T(8,128)(2,1)S(1)}, u32[]{:S(2)}, u32[]{:S(2)}) collective-permute-start(bf16[448,128]{1,0:T(8,128)(2,1)S(1)} %shard_map.102.mine_ref), channel_id=1, source_target_pairs={{0,5},{1,8},{2,11},{3,6},{4,13},{5,0},{6,3},{7,14},{8,1},{9,12},{1... | collective-permute-start | bytes 344072 | tf_op jit(solution)/shard_map/ppermute | solution.py:601
  24.7 1.3 %collective-permute-start.4 = (bf16[64,256]{1,0:T(8,128)(2,1)S(1)}, bf16[64,256]{1,0:T(8,128)(2,1)S(1)}, u32[]{:S(2)}, u32[]{:S(2)}) collective-permute-start(bf16[64,256]{1,0:T(8,128)(2,1)S(1)} %get-tuple-element.74), channel_id=1, source_target_pairs={{0,1},{1,0},{2,3},{3,2},{4,5},{5,4},{6,7},{7,6},{8,9},{9,8},{10,11... | collective-permute-start | bytes 98312 | tf_op jit(solution)/shard_map/ppermute | solution.py:621
  27.2 4.3 %collective-permute-start.8 = (bf16[448,128]{1,0:T(8,128)(2,1)S(1)}, bf16[448,128]{1,0:T(8,128)(2,1)S(1)}, u32[]{:S(2)}, u32[]{:S(2)}) collective-permute-start(bf16[448,128]{1,0:T(8,128)(2,1)S(1)} %shard_map.103.after_ref.mine_ref), channel_id=1, source_target_pairs={{0,9},{1,4},{2,7},{3,10},{4,1},{5,12},{6,15},{7,2},{8,13},{9,0},{1... | collective-permute-start | bytes 344072 | tf_op jit(solution)/shard_map/ppermute | solution.py:601
  31.5 1.6 %collective-permute-start.9 = (f32[448,128]{1,0:T(8,128)S(1)}, f32[448,128]{1,0:T(8,128)S(1)}, u32[]{:S(2)}, u32[]{:S(2)}) collective-permute-start(f32[448,128]{1,0:T(8,128)S(1)} %shard_map.105.source_ref), channel_id=1, source_target_pairs={{0,1},{1,0},{2,3},{3,2},{4,5},{5,4},{6,7},{7,6},{8,9},{9,8},{10,11... | collective-permute-start | bytes 688136 | tf_op jit(solution)/shard_map/ppermute | solution.py:640
